TPU v7x, 32 devices: a whole 2x2x4 slice. The times are simulated.
32 devices in a mesh: grp: 4 (over y, x), mem: 8 (over z, core).
Axes of the slice: x: 2, y: 2, z: 4, core: 2. Of those that a mesh axis runs over, the one named last changes fastest.
Arguments:
- features: bfloat16 [131072, 1024], P(('grp', 'mem')), may hold values from -24 to 24
- lengths: int32 [32, 2], P(('grp', 'mem')), may hold values from 512 to 2048, as said below
Outputs:
- sample_count: float32 [1], replicated
- feature_mean: float32 [1024], replicated
- covariance: float32 [1024, 1024], P(('grp', 'mem'))
Inputs may be any that keep to these rules, and one draw needn't show every extreme that they name: Every block of a device has 2048 slots; lengths count the valid leading slots.
All inputs are finite; a program needn't handle non-finite values.
Results may differ from a plain program's by a relative error of at most 0.0003.
Values sent between devices are 32-bit elements; how exact they have to be, the bound alone decides.
No kernel may reach another device: no remote copies, remote signals or barrier semaphores. Data moves between devices by JAX's collectives and lax.ppermute only.
A program may use at most 64 MiB of HBM per device.

v0:
```python
import jax
import jax.numpy as jnp
from jax import lax
from jax.sharding import PartitionSpec as P


def body(features, lengths):
    half_rows = features.shape[0] // 2
    position = lax.broadcasted_iota(jnp.int32, (2, half_rows), 1)
    keep = (position < lengths[0][:, None]).reshape(1, 2 * half_rows).astype(jnp.bfloat16)
    masked = features * keep.reshape(2 * half_rows, 1)
    own_count = jnp.sum(lengths).astype(jnp.float32).reshape(1)
    own_sum = jnp.dot(keep, features, preferred_element_type=jnp.float32)
    total_count, total_sum = lax.psum((own_count, own_sum), ("grp", "mem"))
    global_mean = total_sum / total_count[0]
    own_mean = own_sum / own_count[0]
    offset_vec = own_mean - global_mean
    mean_part = own_mean[0]
    offset_part = offset_vec[0]
    fix = mean_part[:, None] * own_mean - offset_part[:, None] * offset_vec
    grouped = lax.psum_scatter(
        lax.dot_general(
            masked, masked, (((0,), (0,)), ((), ())), preferred_element_type=jnp.float32
        )
        - own_count[0] * fix,
        "grp",
        scatter_dimension=0,
        tiled=True,
    )
    second = lax.psum_scatter(grouped, "mem", scatter_dimension=0, tiled=True)
    covariance = second / (total_count[0] - 1.0)
    return (total_count, global_mean[0], covariance)


def solution(mesh):
    return jax.shard_map(
        body,
        mesh=mesh,
        in_specs=(P(("grp", "mem"), None), P(("grp", "mem"), None)),
        out_specs=(P(), P(), P(("grp", "mem"), None)),
        check_vma=False,
    )
```

profile of v0, /device:TPU:0, one launch (start us, length us, event | category | flops | bytes accessed | tf_op | source)
XLA Modules:
  0.0 171.9 jit_solution(11424493982436879420)
XLA Ops:
  7.2 0.0 reduce-scatter.3.cloned.1.call-start
  7.2 1.3 reduce_sum.9
  9.2 0.7 iota_compare_fusion
  9.9 4.6 %fusion.7 = f32[1,1024]{1,0:T(1,128)S(1)} fusion(pred[4096,1]{0,1:T(4,128)(4,1)S(1)} %bitcast.14, bf16[4096,1024]{1,0:T(8,128)(2,1)} %param.2), kind=kOutput, calls=%fused_computation.10 | convolution fusion | flops 8388608 | bytes 8396800 | tf_op jit(solution)/shard_map/dot_general | solution.py:13
  14.5 42.8 %all-reduce = (f32[1]{0:T(128)}, f32[1,1024]{1,0:T(1,128)S(1)}) all-reduce(f32[1]{0:T(128)} %bitcast, f32[1,1024]{1,0:T(1,128)S(1)} %fusion.7), channel_id=1, replica_groups=mesh['grp'=4,'mem'=8] {'grp','mem'}, use_global_device_ids=true, to_apply=%region_1.0 | all-reduce | flops 1025 | bytes 8200 | tf_op jit(solution)/shard_map/psum | solution.py:14
  57.3 1.2 fusion.6
  58.6 17.2 %multiply_subtract_fusion = f32[1024,1024]{1,0:T(8,128)} fusion(bf16[4096,1024]{1,0:T(8,128)(2,1)} %param.2, bf16[4096]{0:T(1024)(128)(2,1)S(1)} %convert_element_type.13, f32[1024]{0:T(1024)S(1)} %bitcast.18, f32[1024]{0:T(1024)S(1)} %broadcast_divide_fusion.1, f32[]{:T(128)} %convert_element_type.12), kind=kOutput, calls=%fused_computation.2 | convolution fusion | flops 8599371776 | bytes 12599300 | tf_op jit(solution)/shard_map/dot_general | solution.py:22
  75.7 0.0 reduce-scatter.3.cloned.1.call-update
  75.8 0.0 reduce-scatter.5.cloned.1.call-start
  75.8 52.8 %reduce-scatter.3.cloned.1.call-done = f32[256,1024]{1,0:T(8,128)} async-done(((f32[1024,1024]{1,0:T(8,128)}), f32[256,1024]{1,0:T(8,128)}) %reduce-scatter.3.cloned.1.call-update) | async-done | bytes 1048592 | tf_op jit(solution)/shard_map/reduce_scatter | solution.py:21
  128.6 0.0 reduce-scatter.5.cloned.1.call-update
  129.3 34.2 %reduce-scatter.5.cloned.1.call-done = f32[32,1024]{1,0:T(8,128)} async-done(((f32[256,1024]{1,0:T(8,128)}), f32[32,1024]{1,0:T(8,128)}) %reduce-scatter.5.cloned.1.call-update) | async-done | bytes 131088 | tf_op jit(solution)/shard_map/reduce_scatter | solution.py:30
  163.5 1.6 broadcast_divide_fusion
  (4 shorter events, 0.1 us)
Async XLA Ops:
  7.2 121.5 %reduce-scatter.3.cloned.1.call-start = ((), (), s32[]{:S(2)}) async-start(), calls=%async_computation.2 | async-start | bytes 5242880 | tf_op jit(solution)/shard_map/reduce_scatter | solution.py:21
  75.8 87.7 %reduce-scatter.5.cloned.1.call-start = ((), (), s32[]{:S(2)}) async-start(), calls=%async_computation.3 | async-start | bytes 1179648 | tf_op jit(solution)/shard_map/reduce_scatter | solution.py:30
Sparse Core Ops, SparseCore 0:
  75.9 52.6 reduce-scatter.2
  131.0 32.4 reduce-scatter.4
where the time goes:
time: 172 us
  waiting for transfers between devices  87 us (51%)
  blocking collectives  42.8 us (25%)
  matrix products  21.7 us (13%)
  between operations  15.4 us (9%)
  other arithmetic  4.86 us (3%)
    reduce_scatter x1, waiting for transfers between devices, body(): lax.psum_scatter(lax.dot_general(masked, masked, (((0,), (0,)), ((), ()))...  52.8 us
    psum x1, blocking collectives, body(): total_count, total_sum = lax.psum((own_count, own_sum), ('grp', 'mem'))  42.8 us
    reduce_scatter x1, waiting for transfers between devices, body(): second = lax.psum_scatter(grouped, 'mem', scatter_dimension=0, tiled=True)  34.2 us
    dot_general x1, matrix products, body(): lax.dot_general(masked, masked, (((0,), (0,)), ((), ())), preferred_eleme...  17.2 us
    dot_general x1, matrix products, body(): own_sum = jnp.dot(keep, features, preferred_element_type=jnp.float32)  4.57 us
  transfers between devices with their start and end apart: 2, of which 2 were waited for; matrix products, arithmetic and copies ran while one was open for 0% of the time, Pallas kernels for 0%

commit v1 on v0

v1 whole, which is shorter than its diff:
```python
import functools

import jax
import jax.numpy as jnp
from jax import lax
from jax.experimental import pallas as pl
from jax.experimental.pallas import tpu as pltpu
from jax.sharding import PartitionSpec as P

LANES = 128
SUBLANES = 8


def exchange_masks(groups, members):
    core, others = 1, []
    for bit in range(groups.bit_length() - 1):
        others.append(members << bit)
    for bit in range(1, members.bit_length() - 1):
        others.append(1 << bit if bit % 2 else 3 << (bit - 1))
    return core, others


def exchange_orders(others, width):
    portions = 1
    while 2 * portions <= len(others) and width % (2 * portions * LANES) == 0:
        portions *= 2
    step = max(1, len(others) // portions)
    return [others[i * step:] + others[:i * step] for i in range(portions)]


def relative(order, place):
    device = 0
    for i, mask in enumerate(order):
        if not place >> (len(order) - 1 - i) & 1:
            device ^= mask
    return device


def gram_kernel(me_ref, len_ref, x_hbm, mine_ref, theirs_ref, extra_ref,
                x_ref, acc_ref, sem, *, tile, core, orders, rows):
    depth, width = x_hbm.shape
    half_tiles = depth // 2 // tile

    def fetch(i):
        part = pl.ds(i * tile, tile)
        return pltpu.make_async_copy(x_hbm.at[part], x_ref.at[part], sem.at[i])

    for i in range(2 * half_tiles):
        fetch(i).start()
    total = jnp.zeros((1, width), jnp.float32)
    for i in range(2 * half_tiles):
        fetch(i).wait()
        valid = len_ref[i // half_tiles] - (i % half_tiles) * tile
        x = x_ref[pl.ds(i * tile, tile), :]
        position = lax.broadcasted_iota(jnp.int32, x.shape, 0)
        masked = jnp.where(position < valid, x, jnp.zeros_like(x))
        total += jnp.sum(masked.astype(jnp.float32), axis=0, keepdims=True)
        product = lax.dot_general(
            masked, x, (((0,), (0,)), ((), ())), preferred_element_type=jnp.float32
        )
        if i:
            acc_ref[...] += product
        else:
            acc_ref[...] = product
    me = me_ref[0]
    columns = width // len(orders)
    for p, order in enumerate(orders):
        places = 1 << len(order)
        for place in range(places):
            device = relative(order, place)
            out = pl.ds((p * places + place) * rows, rows)
            for ref, mask in ((mine_ref, device), (theirs_ref, device ^ core)):
                source = pl.ds(pl.multiple_of((me ^ mask) * rows, rows), rows)
                ref[out, :] = acc_ref[source, pl.ds(p * columns, columns)]
    count = (len_ref[0] + len_ref[1]).astype(jnp.float32)
    for i in range(width // LANES):
        extra_ref[pl.ds(i, 1), :] = total[:, i * LANES:(i + 1) * LANES]
    extra_ref[pl.ds(width // LANES, SUBLANES), :] = jnp.full((SUBLANES, LANES), count)


def gram(me, lengths, x, core, orders, rows, tile=1024):
    depth, width = x.shape
    columns = width // len(orders)
    half = jax.ShapeDtypeStruct((width // 2 * len(orders), columns), jnp.float32)
    extra = jax.ShapeDtypeStruct((width // LANES + SUBLANES, LANES), jnp.float32)
    smem = pl.BlockSpec(memory_space=pltpu.SMEM)
    vmem = pl.BlockSpec(memory_space=pltpu.VMEM)
    return pl.pallas_call(
        functools.partial(gram_kernel, tile=tile, core=core, orders=orders, rows=rows),
        out_shape=[half, half, extra],
        in_specs=[smem, smem, pl.BlockSpec(memory_space=pl.ANY)],
        out_specs=[vmem, vmem, vmem],
        scratch_shapes=[
            pltpu.VMEM((depth, width), x.dtype),
            pltpu.VMEM((width, width), jnp.float32),
            pltpu.SemaphoreType.DMA((depth // tile,)),
        ],
        compiler_params=pltpu.CompilerParams(vmem_limit_bytes=40 << 20),
        cost_estimate=pl.CostEstimate(
            flops=2 * depth * width * width, bytes_accessed=depth * width * 2, transcendentals=0
        ),
    )(me, lengths, x)


def finish_kernel(me_ref, extra_ref, *refs, rows, terms):
    portions = len(refs) // terms
    pieces, (cov_ref, mean_ref, count_ref) = refs[:-3], refs[-3:]
    width = cov_ref.shape[1]
    tiles = width // LANES
    count = extra_ref[tiles:tiles + 1, 0:1]
    total = jnp.concatenate([extra_ref[i:i + 1, :] for i in range(tiles)], axis=1)
    lane = lax.broadcasted_iota(jnp.int32, (rows, width), 1)
    row = lax.broadcasted_iota(jnp.int32, (rows, width), 0)
    own = jnp.sum(
        jnp.where(lane == row + me_ref[0] * rows, total, 0.0), axis=1, keepdims=True
    )
    mean = total / count
    mean_ref[...] = mean
    count_ref[...] = count
    columns = width // portions
    for p in range(portions):
        part = pieces[p * terms][...]
        for ref in pieces[p * terms + 1:(p + 1) * terms]:
            part += ref[...]
        at = slice(p * columns, (p + 1) * columns)
        cov_ref[:, at] = (part - own * mean[:, at]) / (count - 1.0)


def finish(me, extra, pieces, rows, width):
    terms = len(pieces[0])
    return pl.pallas_call(
        functools.partial(finish_kernel, rows=rows, terms=terms),
        out_shape=[
            jax.ShapeDtypeStruct((rows, width), jnp.float32),
            jax.ShapeDtypeStruct((1, width), jnp.float32),
            jax.ShapeDtypeStruct((1, 1), jnp.float32),
        ],
        in_specs=[pl.BlockSpec(memory_space=pltpu.SMEM)]
        + [pl.BlockSpec(memory_space=pltpu.VMEM)] * (1 + terms * len(pieces)),
        out_specs=[pl.BlockSpec(memory_space=pltpu.VMEM)] * 3,
    )(me, extra, *[term for piece in pieces for term in piece])


def solution(mesh):
    axes = ("grp", "mem")
    groups, members = mesh.shape["grp"], mesh.shape["mem"]
    devices = groups * members
    core, others = exchange_masks(groups, members)

    def swap(value, mask):
        return lax.ppermute(value, axes, [(i, i ^ mask) for i in range(devices)])

    def body(features, lengths):
        width = features.shape[1]
        rows = width // devices
        orders = exchange_orders(others, width)
        places = 1 << len(others)
        me = (lax.axis_index("grp") * members + lax.axis_index("mem")).reshape(1)
        mine, theirs, extra = gram(me, lengths[0], features, core, orders, rows)
        other = swap(theirs, core)
        for mask in [core] + others:
            extra = extra + swap(extra, mask)
        parts = []
        for p in range(len(orders)):
            at = slice(p * places * rows, (p + 1) * places * rows)
            parts.append([mine[at], other[at]])
        for step in range(len(others)):
            send = places >> (step + 1)
            for p, order in enumerate(orders):
                message = sum(part[:send * rows] for part in parts[p])
                arrived = swap(message, order[step])
                parts[p] = [part[send * rows:] for part in parts[p]] + [arrived]
        covariance, mean, count = finish(me, extra, parts, rows, width)
        return count.reshape(1), mean.reshape(width), covariance

    return jax.shard_map(
        body,
        mesh=mesh,
        in_specs=(P(axes, None), P(axes, None)),
        out_specs=(P(), P(), P(axes, None)),
        check_vma=False,
    )
```

time: 172 us -> 82.7 us (0.48)
  waiting for transfers between devices: 87 us -> 28.2 us
  blocking collectives: 42.8 us -> 0 us
  starting transfers between devices: 0.08 us -> 28 us
  matrix products: 21.7 us -> 0 us
  between operations: 15.4 us -> 0.75 us
  Pallas kernels: 0 us -> 12.9 us
  local copies, waits for them, and re-layouts: 0.04 us -> 10.2 us
  other arithmetic: 4.86 us -> 2.41 us
    reduce_scatter x2 -> x0, waiting for transfers between devices: 87 us -> none  [the longest x1 52.8 us: body(): lax.psum_scatter(lax.dot_general(masked, masked, (((0,), (0,)), ((), ()))...]
    psum x1 -> x0, blocking collectives: 42.8 us -> none  [body(): total_count, total_sum = lax.psum((own_count, own_sum), ('grp', 'mem'))]
    ppermute x0 -> x22, waiting for transfers between devices: none -> 28.2 us  [swap(): return lax.ppermute(value, axes, [(i, i ^ mask) for i in range(devices)])]
    ppermute x0 -> x22, starting transfers between devices: none -> 28 us  [swap(): return lax.ppermute(value, axes, [(i, i ^ mask) for i in range(devices)])]
    dot_general x2 -> x0, matrix products: 21.7 us -> none  [the longest x1 17.2 us: body(): lax.dot_general(masked, masked, (((0,), (0,)), ((), ())), preferred_eleme...]
    pallas_call x0 -> x2, Pallas kernels: none -> 12.9 us  [the longest x1 11 us: gram(): pl.pallas_call(functools.partial(gram_kernel, tile=tile, core=core, order...]
    slice x0 -> x9, local copies, waits for them, and re-layouts: none -> 5.52 us  [body(): parts[p] = [part[send * rows:] for part in parts[p]] + [arrived]]
    unnamed x1 -> x12, local copies, waits for them, and re-layouts: 0.02 us -> 4.63 us
  transfers between devices with their start and end apart: 2 -> 22, of which waited for: 2 -> 13; matrix products, arithmetic and copies ran while one was open for 0% -> 9% of each run, Pallas kernels for 0% -> 0%
where the time goes in v1:
time: 82.7 us; the launch traced here: 82.5 us
  waiting for transfers between devices  28.2 us (34%)
  starting transfers between devices  28 us (34%)
  Pallas kernels  12.9 us (16%)
  local copies, waits for them, and re-layouts  10.2 us (12%)
  other arithmetic  2.41 us (3%)
    ppermute x22, waiting for transfers between devices, swap(): return lax.ppermute(value, axes, [(i, i ^ mask) for i in range(devices)])  28.2 us
    ppermute x22, starting transfers between devices, swap(): return lax.ppermute(value, axes, [(i, i ^ mask) for i in range(devices)])  28 us
    pallas_call x1, Pallas kernels, gram(): pl.pallas_call(functools.partial(gram_kernel, tile=tile, core=core, order...  11 us
    slice x9, local copies, waits for them, and re-layouts, body(): parts[p] = [part[send * rows:] for part in parts[p]] + [arrived]  5.52 us
    unnamed x12, local copies, waits for them, and re-layouts  4.63 us
    pallas_call x1, Pallas kernels, finish(): pl.pallas_call(functools.partial(finish_kernel, rows=rows, terms=terms),...  1.86 us
  transfers between devices with their start and end apart: 22, of which 13 were waited for; matrix products, arithmetic and copies ran while one was open for 9% of the time, Pallas kernels for 0%

profile of v1, /device:TPU:0, one launch (start us, length us, event | category | flops | bytes accessed | tf_op | source)
XLA Modules:
  0.0 82.5 jit_solution(14204982177792651828)
XLA Ops:
  0.6 3.4 %copy-done = bf16[4096,1024]{1,0:T(8,128)(2,1)S(1)} copy-done((bf16[4096,1024]{1,0:T(8,128)(2,1)S(1)}, bf16[4096,1024]{1,0:T(8,128)(2,1)}, u32[]{:S(2)}) %copy-start) | copy-done | bytes 8388632
  4.0 0.7 copy-done.1
  4.7 11.0 %shard_map.49 = (f32[2048,256]{1,0:T(8,128)S(1)}, f32[2048,256]{1,0:T(8,128)S(1)}, f32[16,128]{1,0:T(8,128)S(1)}) custom-call(s32[1]{0:T(128)} %bitcast.me_ref, s32[2]{0:T(128)S(1)} %bitcast.4, bf16[4096,1024]{1,0:T(8,128)(2,1)S(1)} %copy-done), custom_call_target="tpu_custom_call" | custom-call | flops 8589934592 | bytes 8388608 | tf_op jit(solution)/shard_map/pallas_call | solution.py:88
  15.7 0.5 collective-permute-start.5
  16.2 3.8 %collective-permute-done.5 = f32[2048,256]{1,0:T(8,128)S(1)} collective-permute-done((f32[2048,256]{1,0:T(8,128)S(1)}, f32[2048,256]{1,0:T(8,128)S(1)}, u32[]{:S(2)}, u32[]{:S(2)}) %collective-permute-start.5) | collective-permute-done | bytes 2097184 | tf_op jit(solution)/shard_map/ppermute | solution.py:151
  20.0 0.2 slice_add_fusion
  20.2 2.9 %collective-permute-start.10 = (f32[256,256]{1,0:T(8,128)S(1)}, f32[256,256]{1,0:T(8,128)S(1)}, u32[]{:S(2)}, u32[]{:S(2)}) collective-permute-start(f32[256,256]{1,0:T(8,128)S(1)} %get-tuple-element.28), channel_id=1, source_target_pairs={{0,16},{1,17},{2,18},{3,19},{4,20},{5,21},{6,22},{7,23},{8,24},{9,... | collective-permute-start | bytes 786440 | tf_op jit(solution)/shard_map/ppermute | solution.py:151
  23.2 1.6 %collective-permute-start.14 = (f32[256,256]{1,0:T(8,128)S(1)}, f32[256,256]{1,0:T(8,128)S(1)}, u32[]{:S(2)}, u32[]{:S(2)}) collective-permute-start(f32[256,256]{1,0:T(8,128)S(1)} %get-tuple-element.27), channel_id=1, source_target_pairs={{0,2},{1,3},{2,0},{3,1},{4,6},{5,7},{6,4},{7,5},{8,10},{9,11},{10,... | collective-permute-start | bytes 786440 | tf_op jit(solution)/shard_map/ppermute | solution.py:151
  24.7 2.5 %collective-permute-start.18 = (f32[256,256]{1,0:T(8,128)S(1)}, f32[256,256]{1,0:T(8,128)S(1)}, u32[]{:S(2)}, u32[]{:S(2)}) collective-permute-start(f32[256,256]{1,0:T(8,128)S(1)} %get-tuple-element.26), channel_id=1, source_target_pairs={{0,6},{1,7},{2,4},{3,5},{4,2},{5,3},{6,0},{7,1},{8,14},{9,15},{10,... | collective-permute-start | bytes 786440 | tf_op jit(solution)/shard_map/ppermute | solution.py:151
  27.2 1.5 %collective-permute-start.6 = (f32[256,256]{1,0:T(8,128)S(1)}, f32[256,256]{1,0:T(8,128)S(1)}, u32[]{:S(2)}, u32[]{:S(2)}) collective-permute-start(f32[256,256]{1,0:T(8,128)S(1)} %get-tuple-element.29), channel_id=1, source_target_pairs={{0,8},{1,9},{2,10},{3,11},{4,12},{5,13},{6,14},{7,15},{8,0},{9,1},... | collective-permute-start | bytes 786440 | tf_op jit(solution)/shard_map/ppermute | solution.py:151
  28.7 1.1 %collective-permute-done.10 = f32[256,256]{1,0:T(8,128)S(1)} collective-permute-done((f32[256,256]{1,0:T(8,128)S(1)}, f32[256,256]{1,0:T(8,128)S(1)}, u32[]{:S(2)}, u32[]{:S(2)}) %collective-permute-start.10) | collective-permute-done | bytes 262176 | tf_op jit(solution)/shard_map/ppermute | solution.py:151
  29.8 1.7 %collective-permute-done.14 = f32[256,256]{1,0:T(8,128)S(1)} collective-permute-done((f32[256,256]{1,0:T(8,128)S(1)}, f32[256,256]{1,0:T(8,128)S(1)}, u32[]{:S(2)}, u32[]{:S(2)}) %collective-permute-start.14) | collective-permute-done | bytes 262176 | tf_op jit(solution)/shard_map/ppermute | solution.py:151
  31.4 7.5 %collective-permute-done.18 = f32[256,256]{1,0:T(8,128)S(1)} collective-permute-done((f32[256,256]{1,0:T(8,128)S(1)}, f32[256,256]{1,0:T(8,128)S(1)}, u32[]{:S(2)}, u32[]{:S(2)}) %collective-permute-start.18) | collective-permute-done | bytes 262176 | tf_op jit(solution)/shard_map/ppermute | solution.py:151
  39.0 0.1 slice_add_fusion.4
  39.1 0.6 collective-permute-start.11
  39.7 2.6 %collective-permute-start.15 = (f32[128,256]{1,0:T(8,128)S(1)}, f32[128,256]{1,0:T(8,128)S(1)}, u32[]{:S(2)}, u32[]{:S(2)}) collective-permute-start(f32[128,256]{1,0:T(8,128)S(1)} %get-tuple-element.23), channel_id=1, source_target_pairs={{0,6},{1,7},{2,4},{3,5},{4,2},{5,3},{6,0},{7,1},{8,14},{9,15},{10,... | collective-permute-start | bytes 393224 | tf_op jit(solution)/shard_map/ppermute | solution.py:151
  42.4 1.5 %collective-permute-start.19 = (f32[128,256]{1,0:T(8,128)S(1)}, f32[128,256]{1,0:T(8,128)S(1)}, u32[]{:S(2)}, u32[]{:S(2)}) collective-permute-start(f32[128,256]{1,0:T(8,128)S(1)} %get-tuple-element.22), channel_id=1, source_target_pairs={{0,8},{1,9},{2,10},{3,11},{4,12},{5,13},{6,14},{7,15},{8,0},{9,1},... | collective-permute-start | bytes 393224 | tf_op jit(solution)/shard_map/ppermute | solution.py:151
  43.9 0.5 collective-permute-start.7
  44.4 1.1 %collective-permute-done.11 = f32[128,256]{1,0:T(8,128)S(1)} collective-permute-done((f32[128,256]{1,0:T(8,128)S(1)}, f32[128,256]{1,0:T(8,128)S(1)}, u32[]{:S(2)}, u32[]{:S(2)}) %collective-permute-start.11) | collective-permute-done | bytes 131104 | tf_op jit(solution)/shard_map/ppermute | solution.py:151
  45.5 1.4 %collective-permute-done.15 = f32[128,256]{1,0:T(8,128)S(1)} collective-permute-done((f32[128,256]{1,0:T(8,128)S(1)}, f32[128,256]{1,0:T(8,128)S(1)}, u32[]{:S(2)}, u32[]{:S(2)}) %collective-permute-start.15) | collective-permute-done | bytes 131104 | tf_op jit(solution)/shard_map/ppermute | solution.py:151
  46.9 0.4 collective-permute-done.19
  47.3 1.5 %collective-permute-done.7 = f32[128,256]{1,0:T(8,128)S(1)} collective-permute-done((f32[128,256]{1,0:T(8,128)S(1)}, f32[128,256]{1,0:T(8,128)S(1)}, u32[]{:S(2)}, u32[]{:S(2)}) %collective-permute-start.7) | collective-permute-done | bytes 131104 | tf_op jit(solution)/shard_map/ppermute | solution.py:151
  48.8 0.1 slice_add_fusion.12
  48.9 0.1 collective-permute-start.8
  49.0 0.1 collective-permute-start
  49.1 1.2 %collective-permute-done = f32[16,128]{1,0:T(8,128)S(1)} collective-permute-done((f32[16,128]{1,0:T(8,128)S(1)}, f32[16,128]{1,0:T(8,128)S(1)}, u32[]{:S(2)}, u32[]{:S(2)}) %collective-permute-start) | collective-permute-done | bytes 8224 | tf_op jit(solution)/shard_map/ppermute | solution.py:151
  50.2 0.6 collective-permute-start.1
  50.9 1.6 %collective-permute-start.12 = (f32[64,256]{1,0:T(8,128)S(1)}, f32[64,256]{1,0:T(8,128)S(1)}, u32[]{:S(2)}, u32[]{:S(2)}) collective-permute-start(f32[64,256]{1,0:T(8,128)S(1)} %get-tuple-element.20), channel_id=1, source_target_pairs={{0,6},{1,7},{2,4},{3,5},{4,2},{5,3},{6,0},{7,1},{8,14},{9,15},{10,... | collective-permute-start | bytes 196616 | tf_op jit(solution)/shard_map/ppermute | solution.py:151
  52.4 1.5 %collective-permute-start.16 = (f32[64,256]{1,0:T(8,128)S(1)}, f32[64,256]{1,0:T(8,128)S(1)}, u32[]{:S(2)}, u32[]{:S(2)}) collective-permute-start(f32[64,256]{1,0:T(8,128)S(1)} %get-tuple-element.19), channel_id=1, source_target_pairs={{0,8},{1,9},{2,10},{3,11},{4,12},{5,13},{6,14},{7,15},{8,0},{9,1},... | collective-permute-start | bytes 196616 | tf_op jit(solution)/shard_map/ppermute | solution.py:151
  53.9 0.5 collective-permute-start.20
  54.4 0.7 fusion
  55.1 2.2 %collective-permute-start.9 = (f32[32,256]{1,0:T(8,128)S(1)}, f32[32,256]{1,0:T(8,128)S(1)}, u32[]{:S(2)}, u32[]{:S(2)}) collective-permute-start(f32[32,256]{1,0:T(8,128)S(1)} %get-tuple-element.37), channel_id=1, source_target_pairs={{0,6},{1,7},{2,4},{3,5},{4,2},{5,3},{6,0},{7,1},{8,14},{9,15},{10,... | collective-permute-start | bytes 98312 | tf_op jit(solution)/shard_map/ppermute | solution.py:151
  57.3 0.0 collective-permute-done.12
  57.3 0.0 collective-permute-done.16
  57.3 0.9 %collective-permute-done.20 = f32[64,256]{1,0:T(8,128)S(1)} collective-permute-done((f32[64,256]{1,0:T(8,128)S(1)}, f32[64,256]{1,0:T(8,128)S(1)}, u32[]{:S(2)}, u32[]{:S(2)}) %collective-permute-start.20) | collective-permute-done | bytes 65568 | tf_op jit(solution)/shard_map/ppermute | solution.py:151
  58.2 0.7 slice_add_fusion.24
  58.9 0.5 collective-permute-start.13
  59.4 0.7 collective-permute-start.17
  60.2 0.9 %collective-permute-start.21 = (f32[32,256]{1,0:T(8,128)S(1)}, f32[32,256]{1,0:T(8,128)S(1)}, u32[]{:S(2)}, u32[]{:S(2)}) collective-permute-start(f32[32,256]{1,0:T(8,128)S(1)} %get-tuple-element.15), channel_id=1, source_target_pairs={{0,2},{1,3},{2,0},{3,1},{4,6},{5,7},{6,4},{7,5},{8,10},{9,11},{10,... | collective-permute-start | bytes 98312 | tf_op jit(solution)/shard_map/ppermute | solution.py:151
  61.1 0.0 collective-permute-done.1
  61.1 1.9 %collective-permute-start.2 = (f32[16,128]{1,0:T(8,128)S(1)}, f32[16,128]{1,0:T(8,128)S(1)}, u32[]{:S(2)}, u32[]{:S(2)}) collective-permute-start(f32[16,128]{1,0:T(8,128)S(1)} %add.140), channel_id=1, source_target_pairs={{0,16},{1,17},{2,18},{3,19},{4,20},{5,21},{6,22},{7,23},{8,24},{9,... | collective-permute-start | bytes 24584 | tf_op jit(solution)/shard_map/ppermute | solution.py:151
  63.0 1.8 %collective-permute-done.2 = f32[16,128]{1,0:T(8,128)S(1)} collective-permute-done((f32[16,128]{1,0:T(8,128)S(1)}, f32[16,128]{1,0:T(8,128)S(1)}, u32[]{:S(2)}, u32[]{:S(2)}) %collective-permute-start.2) | collective-permute-done | bytes 8224 | tf_op jit(solution)/shard_map/ppermute | solution.py:151
  64.7 1.1 %collective-permute-start.3 = (f32[16,128]{1,0:T(8,128)S(1)}, f32[16,128]{1,0:T(8,128)S(1)}, u32[]{:S(2)}, u32[]{:S(2)}) collective-permute-start(f32[16,128]{1,0:T(8,128)S(1)} %add.141), channel_id=1, source_target_pairs={{0,2},{1,3},{2,0},{3,1},{4,6},{5,7},{6,4},{7,5},{8,10},{9,11},{10,... | collective-permute-start | bytes 24584 | tf_op jit(solution)/shard_map/ppermute | solution.py:151
  65.9 2.5 %collective-permute-done.3 = f32[16,128]{1,0:T(8,128)S(1)} collective-permute-done((f32[16,128]{1,0:T(8,128)S(1)}, f32[16,128]{1,0:T(8,128)S(1)}, u32[]{:S(2)}, u32[]{:S(2)}) %collective-permute-start.3) | collective-permute-done | bytes 8224 | tf_op jit(solution)/shard_map/ppermute | solution.py:151
  68.4 2.1 %collective-permute-start.4 = (f32[16,128]{1,0:T(8,128)S(1)}, f32[16,128]{1,0:T(8,128)S(1)}, u32[]{:S(2)}, u32[]{:S(2)}) collective-permute-start(f32[16,128]{1,0:T(8,128)S(1)} %add.142), channel_id=1, source_target_pairs={{0,6},{1,7},{2,4},{3,5},{4,2},{5,3},{6,0},{7,1},{8,14},{9,15},{10,... | collective-permute-start | bytes 24584 | tf_op jit(solution)/shard_map/ppermute | solution.py:151
  70.5 3.4 %collective-permute-done.4 = f32[16,128]{1,0:T(8,128)S(1)} collective-permute-done((f32[16,128]{1,0:T(8,128)S(1)}, f32[16,128]{1,0:T(8,128)S(1)}, u32[]{:S(2)}, u32[]{:S(2)}) %collective-permute-start.4) | collective-permute-done | bytes 8224 | tf_op jit(solution)/shard_map/ppermute | solution.py:151
  73.8 0.6 add.143.extra_ref
  74.4 0.6 slice.452.refs_8_
  75.1 0.6 slice.466.refs_14_
  75.7 0.6 slice.480.refs_20_
  76.3 0.6 slice.455.refs_9_
  76.9 0.6 slice.469.refs_15_
  77.5 0.6 slice.483.refs_21_
  78.1 0.6 slice.459.refs_10_
  78.7 0.6 slice.473.refs_16_
  79.4 0.6 slice.487.refs_22_
  80.0 0.0 collective-permute-done.9.refs_5_
  80.0 0.0 collective-permute-done.17.refs_17_
  80.0 0.0 collective-permute-done.21.refs_23_
  80.0 0.6 copy-done.2
  80.6 0.0 copy-done.3
  80.6 0.0 copy-done.4
  80.6 0.0 copy-done.5
  80.6 1.9 %shard_map.50 = (f32[32,1024]{1,0:T(8,128)}, f32[1,1024]{1,0:T(1,128)}, f32[1,1]{1,0:T(1,128)}) custom-call(s32[1]{0:T(128)} %bitcast.me_ref, f32[16,128]{1,0:T(8,128)} %add.143.extra_ref, f32[32,256]{1,0:T(8,128)} %get-tuple-element.33.refs_0_, f32[32,256]{1,0:T(8,128)} %get-tuple-element.38.refs_1_, f32[32,256]{1,0:T(8,128)} %get-tuple-element.39.refs_2_, ...), custom_call_target="tpu_custom_call" | custom-call | tf_op jit(solution)/shard_map/pallas_call | solution.py:131
  (13 shorter events, 0.0 us)
Async XLA Ops:
  0.6 3.4 %copy-start = (bf16[4096,1024]{1,0:T(8,128)(2,1)S(1)}, bf16[4096,1024]{1,0:T(8,128)(2,1)}, u32[]{:S(2)}) copy-start(bf16[4096,1024]{1,0:T(8,128)(2,1)} %x_hbm.1) | copy-start | bytes 25165828
  4.0 0.7 copy-start.1
  15.7 4.3 %collective-permute-start.5 = (f32[2048,256]{1,0:T(8,128)S(1)}, f32[2048,256]{1,0:T(8,128)S(1)}, u32[]{:S(2)}, u32[]{:S(2)}) collective-permute-start(f32[2048,256]{1,0:T(8,128)S(1)} %get-tuple-element.11), channel_id=1, source_target_pairs={{0,1},{1,0},{2,3},{3,2},{4,5},{5,4},{6,7},{7,6},{8,9},{9,8},{10,11... | collective-permute-start | bytes 6291464 | tf_op jit(solution)/shard_map/ppermute | solution.py:151
  20.2 9.6 %collective-permute-start.10 = (f32[256,256]{1,0:T(8,128)S(1)}, f32[256,256]{1,0:T(8,128)S(1)}, u32[]{:S(2)}, u32[]{:S(2)}) collective-permute-start(f32[256,256]{1,0:T(8,128)S(1)} %get-tuple-element.28), channel_id=1, source_target_pairs={{0,16},{1,17},{2,18},{3,19},{4,20},{5,21},{6,22},{7,23},{8,24},{9,... | collective-permute-start | bytes 786440 | tf_op jit(solution)/shard_map/ppermute | solution.py:151
  23.2 8.3 %collective-permute-start.14 = (f32[256,256]{1,0:T(8,128)S(1)}, f32[256,256]{1,0:T(8,128)S(1)}, u32[]{:S(2)}, u32[]{:S(2)}) collective-permute-start(f32[256,256]{1,0:T(8,128)S(1)} %get-tuple-element.27), channel_id=1, source_target_pairs={{0,2},{1,3},{2,0},{3,1},{4,6},{5,7},{6,4},{7,5},{8,10},{9,11},{10,... | collective-permute-start | bytes 786440 | tf_op jit(solution)/shard_map/ppermute | solution.py:151
  24.7 14.2 %collective-permute-start.18 = (f32[256,256]{1,0:T(8,128)S(1)}, f32[256,256]{1,0:T(8,128)S(1)}, u32[]{:S(2)}, u32[]{:S(2)}) collective-permute-start(f32[256,256]{1,0:T(8,128)S(1)} %get-tuple-element.26), channel_id=1, source_target_pairs={{0,6},{1,7},{2,4},{3,5},{4,2},{5,3},{6,0},{7,1},{8,14},{9,15},{10,... | collective-permute-start | bytes 786440 | tf_op jit(solution)/shard_map/ppermute | solution.py:151
  27.2 11.8 %collective-permute-start.6 = (f32[256,256]{1,0:T(8,128)S(1)}, f32[256,256]{1,0:T(8,128)S(1)}, u32[]{:S(2)}, u32[]{:S(2)}) collective-permute-start(f32[256,256]{1,0:T(8,128)S(1)} %get-tuple-element.29), channel_id=1, source_target_pairs={{0,8},{1,9},{2,10},{3,11},{4,12},{5,13},{6,14},{7,15},{8,0},{9,1},... | collective-permute-start | bytes 786440 | tf_op jit(solution)/shard_map/ppermute | solution.py:151
  39.1 6.4 %collective-permute-start.11 = (f32[128,256]{1,0:T(8,128)S(1)}, f32[128,256]{1,0:T(8,128)S(1)}, u32[]{:S(2)}, u32[]{:S(2)}) collective-permute-start(f32[128,256]{1,0:T(8,128)S(1)} %get-tuple-element.24), channel_id=1, source_target_pairs={{0,2},{1,3},{2,0},{3,1},{4,6},{5,7},{6,4},{7,5},{8,10},{9,11},{10,... | collective-permute-start | bytes 393224 | tf_op jit(solution)/shard_map/ppermute | solution.py:151
  39.7 7.2 %collective-permute-start.15 = (f32[128,256]{1,0:T(8,128)S(1)}, f32[128,256]{1,0:T(8,128)S(1)}, u32[]{:S(2)}, u32[]{:S(2)}) collective-permute-start(f32[128,256]{1,0:T(8,128)S(1)} %get-tuple-element.23), channel_id=1, source_target_pairs={{0,6},{1,7},{2,4},{3,5},{4,2},{5,3},{6,0},{7,1},{8,14},{9,15},{10,... | collective-permute-start | bytes 393224 | tf_op jit(solution)/shard_map/ppermute | solution.py:151
  42.4 5.0 %collective-permute-start.19 = (f32[128,256]{1,0:T(8,128)S(1)}, f32[128,256]{1,0:T(8,128)S(1)}, u32[]{:S(2)}, u32[]{:S(2)}) collective-permute-start(f32[128,256]{1,0:T(8,128)S(1)} %get-tuple-element.22), channel_id=1, source_target_pairs={{0,8},{1,9},{2,10},{3,11},{4,12},{5,13},{6,14},{7,15},{8,0},{9,1},... | collective-permute-start | bytes 393224 | tf_op jit(solution)/shard_map/ppermute | solution.py:151
  43.9 5.0 %collective-permute-start.7 = (f32[128,256]{1,0:T(8,128)S(1)}, f32[128,256]{1,0:T(8,128)S(1)}, u32[]{:S(2)}, u32[]{:S(2)}) collective-permute-start(f32[128,256]{1,0:T(8,128)S(1)} %get-tuple-element.25), channel_id=1, source_target_pairs={{0,16},{1,17},{2,18},{3,19},{4,20},{5,21},{6,22},{7,23},{8,24},{9,... | collective-permute-start | bytes 393224 | tf_op jit(solution)/shard_map/ppermute | solution.py:151
  48.9 5.5 %collective-permute-start.8 = (f32[64,256]{1,0:T(8,128)S(1)}, f32[64,256]{1,0:T(8,128)S(1)}, u32[]{:S(2)}, u32[]{:S(2)}) collective-permute-start(f32[64,256]{1,0:T(8,128)S(1)} %get-tuple-element.21), channel_id=1, source_target_pairs={{0,2},{1,3},{2,0},{3,1},{4,6},{5,7},{6,4},{7,5},{8,10},{9,11},{10,... | collective-permute-start | bytes 196616 | tf_op jit(solution)/shard_map/ppermute | solution.py:151
  49.0 1.2 %collective-permute-start = (f32[16,128]{1,0:T(8,128)S(1)}, f32[16,128]{1,0:T(8,128)S(1)}, u32[]{:S(2)}, u32[]{:S(2)}) collective-permute-start(f32[16,128]{1,0:T(8,128)S(1)} %get-tuple-element.9), channel_id=1, source_target_pairs={{0,1},{1,0},{2,3},{3,2},{4,5},{5,4},{6,7},{7,6},{8,9},{9,8},{10,11... | collective-permute-start | bytes 24584 | tf_op jit(solution)/shard_map/ppermute | solution.py:151
  50.2 10.8 %collective-permute-start.1 = (f32[16,128]{1,0:T(8,128)S(1)}, f32[16,128]{1,0:T(8,128)S(1)}, u32[]{:S(2)}, u32[]{:S(2)}) collective-permute-start(f32[16,128]{1,0:T(8,128)S(1)} %add.139), channel_id=1, source_target_pairs={{0,8},{1,9},{2,10},{3,11},{4,12},{5,13},{6,14},{7,15},{8,0},{9,1},... | collective-permute-start | bytes 24584 | tf_op jit(solution)/shard_map/ppermute | solution.py:151
  50.9 6.4 %collective-permute-start.12 = (f32[64,256]{1,0:T(8,128)S(1)}, f32[64,256]{1,0:T(8,128)S(1)}, u32[]{:S(2)}, u32[]{:S(2)}) collective-permute-start(f32[64,256]{1,0:T(8,128)S(1)} %get-tuple-element.20), channel_id=1, source_target_pairs={{0,6},{1,7},{2,4},{3,5},{4,2},{5,3},{6,0},{7,1},{8,14},{9,15},{10,... | collective-permute-start | bytes 196616 | tf_op jit(solution)/shard_map/ppermute | solution.py:151
  52.4 4.9 %collective-permute-start.16 = (f32[64,256]{1,0:T(8,128)S(1)}, f32[64,256]{1,0:T(8,128)S(1)}, u32[]{:S(2)}, u32[]{:S(2)}) collective-permute-start(f32[64,256]{1,0:T(8,128)S(1)} %get-tuple-element.19), channel_id=1, source_target_pairs={{0,8},{1,9},{2,10},{3,11},{4,12},{5,13},{6,14},{7,15},{8,0},{9,1},... | collective-permute-start | bytes 196616 | tf_op jit(solution)/shard_map/ppermute | solution.py:151
  53.9 4.3 %collective-permute-start.20 = (f32[64,256]{1,0:T(8,128)S(1)}, f32[64,256]{1,0:T(8,128)S(1)}, u32[]{:S(2)}, u32[]{:S(2)}) collective-permute-start(f32[64,256]{1,0:T(8,128)S(1)} %get-tuple-element.18), channel_id=1, source_target_pairs={{0,16},{1,17},{2,18},{3,19},{4,20},{5,21},{6,22},{7,23},{8,24},{9,... | collective-permute-start | bytes 196616 | tf_op jit(solution)/shard_map/ppermute | solution.py:151
  55.1 24.8 %collective-permute-start.9 = (f32[32,256]{1,0:T(8,128)S(1)}, f32[32,256]{1,0:T(8,128)S(1)}, u32[]{:S(2)}, u32[]{:S(2)}) collective-permute-start(f32[32,256]{1,0:T(8,128)S(1)} %get-tuple-element.37), channel_id=1, source_target_pairs={{0,6},{1,7},{2,4},{3,5},{4,2},{5,3},{6,0},{7,1},{8,14},{9,15},{10,... | collective-permute-start | bytes 98312 | tf_op jit(solution)/shard_map/ppermute | solution.py:151
  58.9 21.1 %collective-permute-start.13 = (f32[32,256]{1,0:T(8,128)S(1)}, f32[32,256]{1,0:T(8,128)S(1)}, u32[]{:S(2)}, u32[]{:S(2)}) collective-permute-start(f32[32,256]{1,0:T(8,128)S(1)} %get-tuple-element.17), channel_id=1, source_target_pairs={{0,8},{1,9},{2,10},{3,11},{4,12},{5,13},{6,14},{7,15},{8,0},{9,1},... | collective-permute-start | bytes 98312 | tf_op jit(solution)/shard_map/ppermute | solution.py:151
  59.4 20.6 %collective-permute-start.17 = (f32[32,256]{1,0:T(8,128)S(1)}, f32[32,256]{1,0:T(8,128)S(1)}, u32[]{:S(2)}, u32[]{:S(2)}) collective-permute-start(f32[32,256]{1,0:T(8,128)S(1)} %get-tuple-element.16), channel_id=1, source_target_pairs={{0,16},{1,17},{2,18},{3,19},{4,20},{5,21},{6,22},{7,23},{8,24},{9,... | collective-permute-start | bytes 98312 | tf_op jit(solution)/shard_map/ppermute | solution.py:151
  60.2 19.8 %collective-permute-start.21 = (f32[32,256]{1,0:T(8,128)S(1)}, f32[32,256]{1,0:T(8,128)S(1)}, u32[]{:S(2)}, u32[]{:S(2)}) collective-permute-start(f32[32,256]{1,0:T(8,128)S(1)} %get-tuple-element.15), channel_id=1, source_target_pairs={{0,2},{1,3},{2,0},{3,1},{4,6},{5,7},{6,4},{7,5},{8,10},{9,11},{10,... | collective-permute-start | bytes 98312 | tf_op jit(solution)/shard_map/ppermute | solution.py:151
  61.1 3.7 %collective-permute-start.2 = (f32[16,128]{1,0:T(8,128)S(1)}, f32[16,128]{1,0:T(8,128)S(1)}, u32[]{:S(2)}, u32[]{:S(2)}) collective-permute-start(f32[16,128]{1,0:T(8,128)S(1)} %add.140), channel_id=1, source_target_pairs={{0,16},{1,17},{2,18},{3,19},{4,20},{5,21},{6,22},{7,23},{8,24},{9,... | collective-permute-start | bytes 24584 | tf_op jit(solution)/shard_map/ppermute | solution.py:151
  64.7 3.7 %collective-permute-start.3 = (f32[16,128]{1,0:T(8,128)S(1)}, f32[16,128]{1,0:T(8,128)S(1)}, u32[]{:S(2)}, u32[]{:S(2)}) collective-permute-start(f32[16,128]{1,0:T(8,128)S(1)} %add.141), channel_id=1, source_target_pairs={{0,2},{1,3},{2,0},{3,1},{4,6},{5,7},{6,4},{7,5},{8,10},{9,11},{10,... | collective-permute-start | bytes 24584 | tf_op jit(solution)/shard_map/ppermute | solution.py:151
  68.4 5.4 %collective-permute-start.4 = (f32[16,128]{1,0:T(8,128)S(1)}, f32[16,128]{1,0:T(8,128)S(1)}, u32[]{:S(2)}, u32[]{:S(2)}) collective-permute-start(f32[16,128]{1,0:T(8,128)S(1)} %add.142), channel_id=1, source_target_pairs={{0,6},{1,7},{2,4},{3,5},{4,2},{5,3},{6,0},{7,1},{8,14},{9,15},{10,... | collective-permute-start | bytes 24584 | tf_op jit(solution)/shard_map/ppermute | solution.py:151
  80.0 0.6 copy-start.2
  80.0 0.6 copy-start.3
  80.0 0.6 copy-start.4
  80.0 0.6 copy-start.5

commit v2 on v0

v2 whole, which is shorter than its diff:
```python
import functools

import jax
import jax.numpy as jnp
from jax import lax
from jax.experimental import pallas as pl
from jax.experimental.pallas import tpu as pltpu
from jax.sharding import PartitionSpec as P

LANES = 128
EXTRA = 8
CORE = 1
SMEM = pl.BlockSpec(memory_space=pltpu.SMEM)
VMEM = pl.BlockSpec(memory_space=pltpu.VMEM)
ANY = pl.BlockSpec(memory_space=pl.ANY)


def exchange_masks(groups, members):
    masks = [members << bit for bit in range(groups.bit_length() - 1)]
    return masks + [1 << bit for bit in range(1, members.bit_length() - 1)]


def column_portions(masks, width):
    heads, tail = masks[:3], masks[3:]
    tiles = width // LANES
    portions, start = [], 0
    for i in range(len(heads)):
        size = (tiles + len(heads) - 1 - i) // len(heads) * LANES
        portions.append((start, size, heads[i:] + heads[:i] + tail))
        start += size
    return portions


def mirror(acc_ref, done, count, block):
    for n in range(count):
        for other in range(n):
            at = slice(n * block, (n + 1) * block)
            left = slice((done + other) * block, (done + other + 1) * block)
            above = slice(other * block, (other + 1) * block)
            right = slice((done + n) * block, (done + n + 1) * block)
            acc_ref[at, left] = acc_ref[above, right].T


def gram_rows(order, done, count, acc_ref, me, outs, groups, members, rows):
    group, member = me // members, me % members
    block = members * rows
    place = 0
    for n in range(count):
        for j in range(0, members, 2):
            for out, mask in zip(outs, (j, j ^ CORE)):
                source = pl.ds(pl.multiple_of(n * block + (member ^ mask) * rows, rows), rows)
                for other, key in enumerate(order):
                    columns = pl.ds(pl.multiple_of((group ^ key) * block, block), block)
                    out[pl.ds(place * rows, rows), columns] = (
                        acc_ref[source, other * block:(other + 1) * block]
                    )
            place += 1


def transposed_dot(a, b):
    return lax.dot_general(a, b, (((0,), (0,)), ((), ())), preferred_element_type=jnp.float32)


def first_kernel(me_ref, len_ref, x_hbm, mine_ref, theirs_ref, x_ref, acc_ref, sums_ref, sem,
                 *, tile, order, count, groups, members, rows, pack):
    depth, width = x_hbm.shape
    block = width // groups
    half_tiles = depth // 2 // tile
    me = me_ref[0]
    group = me // members

    for i in range(2 * half_tiles):
        part = pl.ds(i * tile, tile)
        for n, key in enumerate(order):
            columns = pl.ds(pl.multiple_of((group ^ key) * block, block), block)
            pltpu.make_async_copy(
                x_hbm.at[part, columns], x_ref.at[part, pl.ds(n * block, block)], sem.at[i]
            ).start()
    total = jnp.zeros((1, width), jnp.float32)
    for i in range(2 * half_tiles):
        part = pl.ds(i * tile, tile)
        pltpu.make_async_copy(x_hbm.at[part], x_ref.at[part], sem.at[i]).wait()
        valid = len_ref[i // half_tiles] - (i % half_tiles) * tile

        @pl.when(valid < tile)
        def _():
            x = x_ref[part, :]
            position = lax.broadcasted_iota(jnp.int32, x.shape, 0)
            x_ref[part, :] = jnp.where(position < valid, x, jnp.zeros_like(x))

        total += jnp.sum(x_ref[part, :].astype(jnp.float32), axis=0, keepdims=True)
        for n in range(count):
            product = transposed_dot(x_ref[part, n * block:(n + 1) * block], x_ref[part, n * block:])
            at = pl.ds(n * block, block), pl.ds(n * block, width - n * block)
            if i:
                acc_ref[at] += product
            else:
                acc_ref[at] = product
    mirror(acc_ref, 0, count, block)
    gram_rows(order, 0, count, acc_ref, me, (mine_ref, theirs_ref), groups, members, rows)
    images = (len_ref[0] + len_ref[1]).astype(jnp.float32)
    for n, key in enumerate(order):
        columns = pl.ds(pl.multiple_of((group ^ key) * block, block), block)
        sums_ref[0:1, columns] = total[:, n * block:(n + 1) * block]
    at = count * members // 2 * rows
    for ref in (mine_ref, theirs_ref):
        ref[pl.ds(at, EXTRA), :] = jnp.full((EXTRA, width), images)
        for line, start in enumerate(range(0, width, pack)):
            size = min(pack, width - start)
            ref[pl.ds(at + line, 1), pl.ds(0, size)] = sums_ref[0:1, start:start + size]


def second_kernel(me_ref, x_ref, done_ref, mine_ref, theirs_ref, acc_ref,
                  *, order, count, groups, members, rows):
    width = x_ref.shape[1]
    block = width // groups
    done = done_ref.shape[0] // block
    for n in range(done, done + count):
        at = slice((n - done) * block, (n - done + 1) * block)
        for other in range(done):
            acc_ref[at, other * block:(other + 1) * block] = (
                done_ref[other * block:(other + 1) * block, n * block:(n + 1) * block].T
            )
        acc_ref[at, n * block:] = transposed_dot(
            x_ref[:, n * block:(n + 1) * block], x_ref[:, n * block:]
        )
    mirror(acc_ref, done, count, block)
    gram_rows(order, done, count, acc_ref, me_ref[0], (mine_ref, theirs_ref), groups, members, rows)


def grams(me, lengths, x, groups, members, pack, tile=1024):
    depth, width = x.shape
    block, rows = width // groups, width // groups // members
    first = [key for key in reversed(range(groups)) if key & 1]
    second = [key for key in reversed(range(groups)) if not key & 1]

    def half(keys, extra):
        return jax.ShapeDtypeStruct((len(keys) * block // 2 + extra, width), jnp.float32)

    def cost(blocks):
        return pl.CostEstimate(
            flops=2 * depth * block * block * blocks,
            bytes_accessed=depth * width * 2,
            transcendentals=0,
        )

    sizes = dict(order=first + second, groups=groups, members=members, rows=rows)
    mine, theirs, kept, done = pl.pallas_call(
        functools.partial(first_kernel, tile=tile, count=len(first), pack=pack, **sizes),
        out_shape=[half(first, EXTRA)] * 2
        + [
            jax.ShapeDtypeStruct(x.shape, x.dtype),
            jax.ShapeDtypeStruct((len(first) * block, width), jnp.float32),
        ],
        in_specs=[SMEM, SMEM, ANY],
        out_specs=[VMEM] * 4,
        scratch_shapes=[
            pltpu.VMEM((EXTRA, width), jnp.float32),
            pltpu.SemaphoreType.DMA((depth // tile,)),
        ],
        compiler_params=pltpu.CompilerParams(vmem_limit_bytes=40 << 20),
        cost_estimate=cost(len(first) * groups),
    )(me, lengths, x)
    later = pl.pallas_call(
        functools.partial(second_kernel, count=len(second), **sizes),
        out_shape=[half(second, 0)] * 2,
        in_specs=[SMEM] + [VMEM] * 2,
        out_specs=[VMEM] * 2,
        scratch_shapes=[pltpu.VMEM((len(second) * block, width), jnp.float32)],
        compiler_params=pltpu.CompilerParams(vmem_limit_bytes=32 << 20),
        cost_estimate=cost(len(second)),
    )(me, kept, done)
    return (mine, theirs), tuple(later), first, second


def total_of(refs, terms, height, size):
    parts = [refs[i][pl.ds(row, height), pl.ds(column, size)] for i, row, column in terms]
    return sum(parts[1:], parts[0])


def combine_kernel(*refs, plan, rows):
    outs = refs[len(refs) - len(plan):]
    for out, (size, atoms, extra) in zip(outs, plan):
        for place, terms in enumerate(atoms):
            out[pl.ds(place * rows, rows), :] = total_of(refs, terms, rows, size)
        if extra:
            out[pl.ds(len(atoms) * rows, EXTRA), :] = total_of(refs, extra, EXTRA, size)


def combine(arrays, plan, rows):
    used = sorted({t[0] for _, atoms, extra in plan for terms in atoms + [extra] for t in terms})
    where = {index: i for i, index in enumerate(used)}

    def local(terms):
        return [(where[i], row, column) for i, row, column in terms]

    plan = [(size, [local(terms) for terms in atoms], local(extra)) for size, atoms, extra in plan]
    return pl.pallas_call(
        functools.partial(combine_kernel, plan=plan, rows=rows),
        out_shape=[
            jax.ShapeDtypeStruct((len(atoms) * rows + EXTRA * bool(extra), size), jnp.float32)
            for size, atoms, extra in plan
        ],
        in_specs=[VMEM] * len(used),
        out_specs=[VMEM] * len(plan),
        compiler_params=pltpu.CompilerParams(vmem_limit_bytes=12 << 20),
    )(*[arrays[i] for i in used])


def finish_kernel(me_ref, *refs, plan, extra, rows, pack):
    cov_ref, mean_ref, count_ref = refs[-3:]
    width = cov_ref.shape[1]
    block = total_of(refs, extra, EXTRA, pack)
    lines = -(-width // pack)
    total = jnp.concatenate([block[i:i + 1] for i in range(lines)], axis=1)[:, :width]
    count = block[lines:lines + 1, 0:1]
    lane = lax.broadcasted_iota(jnp.int32, (rows, width), 1)
    row = lax.broadcasted_iota(jnp.int32, (rows, width), 0)
    own = jnp.sum(
        jnp.where(lane == row + me_ref[0] * rows, total, 0.0), axis=1, keepdims=True
    )
    mean = total / count
    mean_ref[...] = mean
    count_ref[...] = count
    for start, size, terms in plan:
        at = slice(start, start + size)
        second = total_of(refs, terms, rows, size) - own * mean[:, at]
        cov_ref[:, at] = second / (count - 1.0)


def solution(mesh):
    axes = ("grp", "mem")
    groups, members = mesh.shape["grp"], mesh.shape["mem"]
    devices = groups * members
    masks = exchange_masks(groups, members)

    def swap(value, mask):
        return lax.ppermute(value, axes, [(i, i ^ mask) for i in range(devices)])

    def body(features, lengths):
        width = features.shape[1]
        rows = width // devices
        portions = column_portions(masks, width)
        pack = portions[0][1]
        me = (lax.axis_index("grp") * members + lax.axis_index("mem")).reshape(1)
        early, late, first, second = grams(me, lengths[0], features, groups, members, pack)

        arrays = []
        tables = [{} for _ in portions]
        for keys, (mine, theirs) in ((first, early), (second, late)):
            arrays += [mine, swap(theirs, CORE)]
            sources = (len(arrays) - 2, len(arrays) - 1)
            relatives = [key * members + j for key in keys for j in range(0, members, 2)]
            for table, (start, _, _) in zip(tables, portions):
                for place, device in enumerate(relatives):
                    table[device] = [(i, place * rows, start) for i in sources]
        extra = [(i, len(first) * members // 2 * rows, 0) for i in (0, 1)]

        for step in range(len(masks)):
            if step == 0:
                batches = [lambda d: d & masks[0], lambda d: not d & masks[0]]
            else:
                batches = [lambda d: True]
            arrived = []
            for batch in batches:
                plan, sent = [], []
                for p, (_, size, order) in enumerate(portions):
                    mask = order[step]
                    chosen = [d for d in tables[p] if d & mask and batch(d)]
                    if chosen:
                        carried = extra if p == 0 else []
                        plan.append((size, [tables[p][d] for d in chosen], carried))
                        sent.append((p, mask, chosen))
                for (p, mask, chosen), item in zip(sent, plan):
                    message, = combine(arrays, [item], rows)
                    arrived.append((p, mask, chosen, swap(message, mask)))
            for p, mask, chosen, array in arrived:
                for place, device in enumerate(chosen):
                    terms = tables[p].pop(device)
                    tables[p][device ^ mask].append((len(arrays), place * rows, 0))
                if p == 0:
                    extra = extra + [(len(arrays), len(chosen) * rows, 0)]
                arrays.append(array)

        plan = [(start, size, table[0]) for table, (start, size, _) in zip(tables, portions)]
        used = sorted({t[0] for terms in [extra] + [terms for _, _, terms in plan] for t in terms})
        where = {index: i for i, index in enumerate(used)}
        plan = [(s, n, [(where[i], r, c) for i, r, c in terms]) for s, n, terms in plan]
        covariance, mean, count = pl.pallas_call(
            functools.partial(
                finish_kernel,
                plan=plan,
                extra=[(where[i], r, c) for i, r, c in extra],
                rows=rows,
                pack=pack,
            ),
            out_shape=[
                jax.ShapeDtypeStruct((rows, width), jnp.float32),
                jax.ShapeDtypeStruct((1, width), jnp.float32),
                jax.ShapeDtypeStruct((1, 1), jnp.float32),
            ],
            in_specs=[SMEM] + [VMEM] * len(used),
            out_specs=[VMEM] * 3,
            compiler_params=pltpu.CompilerParams(vmem_limit_bytes=12 << 20),
        )(me, *[arrays[i] for i in used])
        return count.reshape(1), mean.reshape(width), covariance

    return jax.shard_map(
        body,
        mesh=mesh,
        in_specs=(P(axes, None), P(axes, None)),
        out_specs=(P(), P(), P(axes, None)),
        check_vma=False,
    )
```

time: 172 us -> 50.6 us (0.29)
  waiting for transfers between devices: 87 us -> 15 us
  blocking collectives: 42.8 us -> 0 us
  starting transfers between devices: 0.08 us -> 22.7 us
  matrix products: 21.7 us -> 0 us
  between operations: 15.4 us -> 0.71 us
  Pallas kernels: 0 us -> 11.3 us
  other arithmetic: 4.86 us -> 0 us
    reduce_scatter x2 -> x0, waiting for transfers between devices: 87 us -> none  [the longest x1 52.8 us: body(): lax.psum_scatter(lax.dot_general(masked, masked, (((0,), (0,)), ((), ()))...]
    psum x1 -> x0, blocking collectives: 42.8 us -> none  [body(): total_count, total_sum = lax.psum((own_count, own_sum), ('grp', 'mem'))]
    ppermute x0 -> x16, starting transfers between devices: none -> 22.7 us  [swap(): return lax.ppermute(value, axes, [(i, i ^ mask) for i in range(devices)])]
    dot_general x2 -> x0, matrix products: 21.7 us -> none  [the longest x1 17.2 us: body(): lax.dot_general(masked, masked, (((0,), (0,)), ((), ())), preferred_eleme...]
    ppermute x0 -> x16, waiting for transfers between devices: none -> 15 us  [swap(): return lax.ppermute(value, axes, [(i, i ^ mask) for i in range(devices)])]
    pallas_call x0 -> x17, Pallas kernels: none -> 11.3 us  [the longest x1 8.1 us: grams(): pl.pallas_call(functools.partial(first_kernel, tile=tile, count=len(first...]
  transfers between devices with their start and end apart: 2 -> 16, of which waited for: 2 -> 7; matrix products, arithmetic and copies ran while one was open for 0% -> 0% of each run, Pallas kernels for 0% -> 5%
where the time goes in v2:
time: 50.6 us; the launch traced here: 50.4 us
  starting transfers between devices  22.7 us (45%)
  waiting for transfers between devices  15 us (30%)
  Pallas kernels  11.3 us (22%)
  between operations  0.71 us (1%)
  local copies, waits for them, and re-layouts  0.65 us (1%)
    ppermute x16, starting transfers between devices, swap(): return lax.ppermute(value, axes, [(i, i ^ mask) for i in range(devices)])  22.7 us
    ppermute x16, waiting for transfers between devices, swap(): return lax.ppermute(value, axes, [(i, i ^ mask) for i in range(devices)])  15 us
    pallas_call x1, Pallas kernels, grams(): pl.pallas_call(functools.partial(first_kernel, tile=tile, count=len(first...  8.1 us
    pallas_call x1, Pallas kernels, grams(): pl.pallas_call(functools.partial(second_kernel, count=len(second), **size...  2.07 us
  transfers between devices with their start and end apart: 16, of which 7 were waited for; matrix products, arithmetic and copies ran while one was open for 0% of the time, Pallas kernels for 5%

profile of v2, /device:TPU:0, one launch (start us, length us, event | category | flops | bytes accessed | tf_op | source)
XLA Modules:
  0.0 50.4 jit_solution(5104995801986300625)
XLA Ops:
  0.6 0.0 copy-start
  0.6 0.6 %copy-done = s32[1,2]{1,0:T(1,128)S(1)} copy-done((s32[1,2]{1,0:T(1,128)S(1)}, s32[1,2]{1,0:T(1,128)}, u32[]{:S(2)}) %copy-start) | copy-done | bytes 32
  1.3 8.1 %shard_map.49 = (f32[264,1024]{1,0:T(8,128)S(1)}, f32[264,1024]{1,0:T(8,128)S(1)}, bf16[4096,1024]{1,0:T(8,128)(2,1)S(1)}, f32[512,1024]{1,0:T(8,128)S(1)}) custom-call(s32[1]{0:T(128)} %bitcast.me_ref, s32[2]{0:T(128)S(1)} %bitcast.4, bf16[4096,1024]{1,0:T(8,128)(2,1)} %x_hbm.1), custom_call_target="tpu_custom_call" | custom-call | flops 4294967296 | bytes 8388608 | tf_op jit(solution)/shard_map/pallas_call | solution.py:148
  9.4 0.5 %collective-permute-start = (f32[264,1024]{1,0:T(8,128)S(1)}, f32[264,1024]{1,0:T(8,128)S(1)}, u32[]{:S(2)}, u32[]{:S(2)}) collective-permute-start(f32[264,1024]{1,0:T(8,128)S(1)} %get-tuple-element.13), channel_id=1, source_target_pairs={{0,1},{1,0},{2,3},{3,2},{4,5},{5,4},{6,7},{7,6},{8,9},{9,8},{10,11... | collective-permute-start | bytes 3244040 | tf_op jit(solution)/shard_map/ppermute | solution.py:238
  9.9 2.1 %shard_map.50 = (f32[256,1024]{1,0:T(8,128)S(1)}, f32[256,1024]{1,0:T(8,128)S(1)}) custom-call(s32[1]{0:T(128)} %bitcast.me_ref, bf16[4096,1024]{1,0:T(8,128)(2,1)S(1)} %get-tuple-element.14.x_ref, f32[512,1024]{1,0:T(8,128)S(1)} %get-tuple-element.15.done_ref), custom_call_target="tpu_custom_call" | custom-call | flops 1073741824 | bytes 8388608 | tf_op jit(solution)/shard_map/pallas_call | solution.py:164
  12.0 0.1 collective-permute-start.1
  12.1 0.1 collective-permute-done.refs_1_
  12.3 2.9 %collective-permute-start.2 = (f32[264,384]{1,0:T(8,128)S(1)}, f32[264,384]{1,0:T(8,128)S(1)}, u32[]{:S(2)}, u32[]{:S(2)}) collective-permute-start(f32[264,384]{1,0:T(8,128)S(1)} %shard_map.51), channel_id=1, source_target_pairs={{0,8},{1,9},{2,10},{3,11},{4,12},{5,13},{6,14},{7,15},{8,0},{9,1},... | collective-permute-start | bytes 1216520 | tf_op jit(solution)/shard_map/ppermute | solution.py:238
  15.2 0.0 collective-permute-done.1.refs_1_.refs_3_
  15.3 2.1 %collective-permute-start.3 = (f32[128,384]{1,0:T(8,128)S(1)}, f32[128,384]{1,0:T(8,128)S(1)}, u32[]{:S(2)}, u32[]{:S(2)}) collective-permute-start(f32[128,384]{1,0:T(8,128)S(1)} %shard_map.52), channel_id=1, source_target_pairs={{0,16},{1,17},{2,18},{3,19},{4,20},{5,21},{6,22},{7,23},{8,24},{9,... | collective-permute-start | bytes 589832 | tf_op jit(solution)/shard_map/ppermute | solution.py:238
  17.3 0.1 collective-permute-start.6
  17.4 7.5 %collective-permute-done.2.refs_4_ = f32[264,384]{1,0:T(8,128)S(1)} collective-permute-done((f32[264,384]{1,0:T(8,128)S(1)}, f32[264,384]{1,0:T(8,128)S(1)}, u32[]{:S(2)}, u32[]{:S(2)}) %collective-permute-start.2) | collective-permute-done | bytes 405536 | tf_op jit(solution)/shard_map/ppermute | solution.py:238
  25.0 1.7 %collective-permute-start.5 = (f32[136,384]{1,0:T(8,128)S(1)}, f32[136,384]{1,0:T(8,128)S(1)}, u32[]{:S(2)}, u32[]{:S(2)}) collective-permute-start(f32[136,384]{1,0:T(8,128)S(1)} %shard_map.54), channel_id=1, source_target_pairs={{0,16},{1,17},{2,18},{3,19},{4,20},{5,21},{6,22},{7,23},{8,24},{9,... | collective-permute-start | bytes 626696 | tf_op jit(solution)/shard_map/ppermute | solution.py:238
  26.6 1.6 %collective-permute-start.8 = (f32[128,256]{1,0:T(8,128)S(1)}, f32[128,256]{1,0:T(8,128)S(1)}, u32[]{:S(2)}, u32[]{:S(2)}) collective-permute-start(f32[128,256]{1,0:T(8,128)S(1)} %shard_map.57), channel_id=1, source_target_pairs={{0,2},{1,3},{2,0},{3,1},{4,6},{5,7},{6,4},{7,5},{8,10},{9,11},{10,... | collective-permute-start | bytes 393224 | tf_op jit(solution)/shard_map/ppermute | solution.py:238
  28.3 0.0 collective-permute-done.3.refs_5_.refs_2_
  28.3 0.0 collective-permute-done.6.refs_4_.refs_2_
  28.3 0.8 %collective-permute-start.7 = (f32[128,384]{1,0:T(8,128)S(1)}, f32[128,384]{1,0:T(8,128)S(1)}, u32[]{:S(2)}, u32[]{:S(2)}) collective-permute-start(f32[128,384]{1,0:T(8,128)S(1)} %shard_map.56), channel_id=1, source_target_pairs={{0,2},{1,3},{2,0},{3,1},{4,6},{5,7},{6,4},{7,5},{8,10},{9,11},{10,... | collective-permute-start | bytes 589832 | tf_op jit(solution)/shard_map/ppermute | solution.py:238
  29.2 1.3 %collective-permute-start.4 = (f32[128,256]{1,0:T(8,128)S(1)}, f32[128,256]{1,0:T(8,128)S(1)}, u32[]{:S(2)}, u32[]{:S(2)}) collective-permute-start(f32[128,256]{1,0:T(8,128)S(1)} %shard_map.53), channel_id=1, source_target_pairs={{0,2},{1,3},{2,0},{3,1},{4,6},{5,7},{6,4},{7,5},{8,10},{9,11},{10,... | collective-permute-start | bytes 393224 | tf_op jit(solution)/shard_map/ppermute | solution.py:238
  30.5 2.5 %collective-permute-done.8.refs_2_ = f32[128,256]{1,0:T(8,128)S(1)} collective-permute-done((f32[128,256]{1,0:T(8,128)S(1)}, f32[128,256]{1,0:T(8,128)S(1)}, u32[]{:S(2)}, u32[]{:S(2)}) %collective-permute-start.8) | collective-permute-done | bytes 131104 | tf_op jit(solution)/shard_map/ppermute | solution.py:238
  33.0 1.5 %collective-permute-start.9 = (f32[128,256]{1,0:T(8,128)S(1)}, f32[128,256]{1,0:T(8,128)S(1)}, u32[]{:S(2)}, u32[]{:S(2)}) collective-permute-start(f32[128,256]{1,0:T(8,128)S(1)} %shard_map.58), channel_id=1, source_target_pairs={{0,8},{1,9},{2,10},{3,11},{4,12},{5,13},{6,14},{7,15},{8,0},{9,1},... | collective-permute-start | bytes 393224 | tf_op jit(solution)/shard_map/ppermute | solution.py:238
  34.6 0.0 collective-permute-done.5.refs_5_.refs_7_
  34.6 1.8 %collective-permute-start.10 = (f32[72,384]{1,0:T(8,128)S(1)}, f32[72,384]{1,0:T(8,128)S(1)}, u32[]{:S(2)}, u32[]{:S(2)}) collective-permute-start(f32[72,384]{1,0:T(8,128)S(1)} %shard_map.59), channel_id=1, source_target_pairs={{0,2},{1,3},{2,0},{3,1},{4,6},{5,7},{6,4},{7,5},{8,10},{9,11},{10,... | collective-permute-start | bytes 331784 | tf_op jit(solution)/shard_map/ppermute | solution.py:238
  36.4 0.8 %collective-permute-done.7.refs_3_.refs_8_ = f32[128,384]{1,0:T(8,128)S(1)} collective-permute-done((f32[128,384]{1,0:T(8,128)S(1)}, f32[128,384]{1,0:T(8,128)S(1)}, u32[]{:S(2)}, u32[]{:S(2)}) %collective-permute-start.7) | collective-permute-done | bytes 196640 | tf_op jit(solution)/shard_map/ppermute | solution.py:238
  37.3 1.5 %collective-permute-start.11 = (f32[64,384]{1,0:T(8,128)S(1)}, f32[64,384]{1,0:T(8,128)S(1)}, u32[]{:S(2)}, u32[]{:S(2)}) collective-permute-start(f32[64,384]{1,0:T(8,128)S(1)} %shard_map.60), channel_id=1, source_target_pairs={{0,8},{1,9},{2,10},{3,11},{4,12},{5,13},{6,14},{7,15},{8,0},{9,1},... | collective-permute-start | bytes 294920 | tf_op jit(solution)/shard_map/ppermute | solution.py:238
  38.8 0.6 %collective-permute-done.4.refs_2_.refs_6_ = f32[128,256]{1,0:T(8,128)S(1)} collective-permute-done((f32[128,256]{1,0:T(8,128)S(1)}, f32[128,256]{1,0:T(8,128)S(1)}, u32[]{:S(2)}, u32[]{:S(2)}) %collective-permute-start.4) | collective-permute-done | bytes 131104 | tf_op jit(solution)/shard_map/ppermute | solution.py:238
  39.4 0.0 collective-permute-done.9.refs_3_.refs_9_
  39.4 1.0 %collective-permute-start.12 = (f32[64,256]{1,0:T(8,128)S(1)}, f32[64,256]{1,0:T(8,128)S(1)}, u32[]{:S(2)}, u32[]{:S(2)}) collective-permute-start(f32[64,256]{1,0:T(8,128)S(1)} %shard_map.61), channel_id=1, source_target_pairs={{0,16},{1,17},{2,18},{3,19},{4,20},{5,21},{6,22},{7,23},{8,24},{9,... | collective-permute-start | bytes 196616 | tf_op jit(solution)/shard_map/ppermute | solution.py:238
  40.4 0.2 collective-permute-done.10.refs_6_.refs_10_
  40.6 2.6 %collective-permute-start.13 = (f32[40,384]{1,0:T(8,128)S(1)}, f32[40,384]{1,0:T(8,128)S(1)}, u32[]{:S(2)}, u32[]{:S(2)}) collective-permute-start(f32[40,384]{1,0:T(8,128)S(1)} %shard_map.62), channel_id=1, source_target_pairs={{0,4},{1,5},{2,6},{3,7},{4,0},{5,1},{6,2},{7,3},{8,12},{9,13},{10,... | collective-permute-start | bytes 184328 | tf_op jit(solution)/shard_map/ppermute | solution.py:238
  43.1 0.0 collective-permute-done.11.refs_4_.refs_11_
  43.2 1.5 %collective-permute-start.14 = (f32[32,384]{1,0:T(8,128)S(1)}, f32[32,384]{1,0:T(8,128)S(1)}, u32[]{:S(2)}, u32[]{:S(2)}) collective-permute-start(f32[32,384]{1,0:T(8,128)S(1)} %shard_map.63), channel_id=1, source_target_pairs={{0,4},{1,5},{2,6},{3,7},{4,0},{5,1},{6,2},{7,3},{8,12},{9,13},{10,... | collective-permute-start | bytes 147464 | tf_op jit(solution)/shard_map/ppermute | solution.py:238
  44.6 0.0 collective-permute-done.12.refs_4_.refs_12_
  44.6 1.7 %collective-permute-start.15 = (f32[32,256]{1,0:T(8,128)S(1)}, f32[32,256]{1,0:T(8,128)S(1)}, u32[]{:S(2)}, u32[]{:S(2)}) collective-permute-start(f32[32,256]{1,0:T(8,128)S(1)} %shard_map.64), channel_id=1, source_target_pairs={{0,4},{1,5},{2,6},{3,7},{4,0},{5,1},{6,2},{7,3},{8,12},{9,13},{10,... | collective-permute-start | bytes 98312 | tf_op jit(solution)/shard_map/ppermute | solution.py:238
  46.3 3.3 %collective-permute-done.15.refs_15_ = f32[32,256]{1,0:T(8,128)S(1)} collective-permute-done((f32[32,256]{1,0:T(8,128)S(1)}, f32[32,256]{1,0:T(8,128)S(1)}, u32[]{:S(2)}, u32[]{:S(2)}) %collective-permute-start.15) | collective-permute-done | bytes 32800 | tf_op jit(solution)/shard_map/ppermute | solution.py:238
  49.6 0.0 collective-permute-done.14.refs_14_
  49.6 0.0 collective-permute-done.13.refs_13_
  49.6 0.8 %shard_map.65 = (f32[32,1024]{1,0:T(8,128)}, f32[1,1024]{1,0:T(1,128)}, f32[1,1]{1,0:T(1,128)}) custom-call(s32[1]{0:T(128)} %bitcast.me_ref, f32[264,1024]{1,0:T(8,128)S(1)} %get-tuple-element.12.refs_0_, f32[264,1024]{1,0:T(8,128)S(1)} %collective-permute-done.refs_1_, f32[256,1024]{1,0:T(8,128)S(1)} %get-tuple-element.16.refs_0_.refs_2_, ...), custom_call_target="tpu_custom_call" | custom-call | tf_op jit(solution)/shard_map/pallas_call | solution.py:289
  (14 shorter events, 0.4 us)
Async XLA Ops:
  0.6 0.7 %copy-start = (s32[1,2]{1,0:T(1,128)S(1)}, s32[1,2]{1,0:T(1,128)}, u32[]{:S(2)}) copy-start(s32[1,2]{1,0:T(1,128)} %param.3) | copy-start | bytes 28
  9.4 2.9 %collective-permute-start = (f32[264,1024]{1,0:T(8,128)S(1)}, f32[264,1024]{1,0:T(8,128)S(1)}, u32[]{:S(2)}, u32[]{:S(2)}) collective-permute-start(f32[264,1024]{1,0:T(8,128)S(1)} %get-tuple-element.13), channel_id=1, source_target_pairs={{0,1},{1,0},{2,3},{3,2},{4,5},{5,4},{6,7},{7,6},{8,9},{9,8},{10,11... | collective-permute-start | bytes 3244040 | tf_op jit(solution)/shard_map/ppermute | solution.py:238
  12.0 3.2 %collective-permute-start.1 = (f32[256,1024]{1,0:T(8,128)S(1)}, f32[256,1024]{1,0:T(8,128)S(1)}, u32[]{:S(2)}, u32[]{:S(2)}) collective-permute-start(f32[256,1024]{1,0:T(8,128)S(1)} %get-tuple-element.17), channel_id=1, source_target_pairs={{0,1},{1,0},{2,3},{3,2},{4,5},{5,4},{6,7},{7,6},{8,9},{9,8},{10,11... | collective-permute-start | bytes 3145736 | tf_op jit(solution)/shard_map/ppermute | solution.py:238
  12.3 12.6 %collective-permute-start.2 = (f32[264,384]{1,0:T(8,128)S(1)}, f32[264,384]{1,0:T(8,128)S(1)}, u32[]{:S(2)}, u32[]{:S(2)}) collective-permute-start(f32[264,384]{1,0:T(8,128)S(1)} %shard_map.51), channel_id=1, source_target_pairs={{0,8},{1,9},{2,10},{3,11},{4,12},{5,13},{6,14},{7,15},{8,0},{9,1},... | collective-permute-start | bytes 1216520 | tf_op jit(solution)/shard_map/ppermute | solution.py:238
  15.3 13.0 %collective-permute-start.3 = (f32[128,384]{1,0:T(8,128)S(1)}, f32[128,384]{1,0:T(8,128)S(1)}, u32[]{:S(2)}, u32[]{:S(2)}) collective-permute-start(f32[128,384]{1,0:T(8,128)S(1)} %shard_map.52), channel_id=1, source_target_pairs={{0,16},{1,17},{2,18},{3,19},{4,20},{5,21},{6,22},{7,23},{8,24},{9,... | collective-permute-start | bytes 589832 | tf_op jit(solution)/shard_map/ppermute | solution.py:238
  17.3 10.9 %collective-permute-start.6 = (f32[128,384]{1,0:T(8,128)S(1)}, f32[128,384]{1,0:T(8,128)S(1)}, u32[]{:S(2)}, u32[]{:S(2)}) collective-permute-start(f32[128,384]{1,0:T(8,128)S(1)} %shard_map.55), channel_id=1, source_target_pairs={{0,16},{1,17},{2,18},{3,19},{4,20},{5,21},{6,22},{7,23},{8,24},{9,... | collective-permute-start | bytes 589832 | tf_op jit(solution)/shard_map/ppermute | solution.py:238
  25.0 9.6 %collective-permute-start.5 = (f32[136,384]{1,0:T(8,128)S(1)}, f32[136,384]{1,0:T(8,128)S(1)}, u32[]{:S(2)}, u32[]{:S(2)}) collective-permute-start(f32[136,384]{1,0:T(8,128)S(1)} %shard_map.54), channel_id=1, source_target_pairs={{0,16},{1,17},{2,18},{3,19},{4,20},{5,21},{6,22},{7,23},{8,24},{9,... | collective-permute-start | bytes 626696 | tf_op jit(solution)/shard_map/ppermute | solution.py:238
  26.6 6.4 %collective-permute-start.8 = (f32[128,256]{1,0:T(8,128)S(1)}, f32[128,256]{1,0:T(8,128)S(1)}, u32[]{:S(2)}, u32[]{:S(2)}) collective-permute-start(f32[128,256]{1,0:T(8,128)S(1)} %shard_map.57), channel_id=1, source_target_pairs={{0,2},{1,3},{2,0},{3,1},{4,6},{5,7},{6,4},{7,5},{8,10},{9,11},{10,... | collective-permute-start | bytes 393224 | tf_op jit(solution)/shard_map/ppermute | solution.py:238
  28.3 8.9 %collective-permute-start.7 = (f32[128,384]{1,0:T(8,128)S(1)}, f32[128,384]{1,0:T(8,128)S(1)}, u32[]{:S(2)}, u32[]{:S(2)}) collective-permute-start(f32[128,384]{1,0:T(8,128)S(1)} %shard_map.56), channel_id=1, source_target_pairs={{0,2},{1,3},{2,0},{3,1},{4,6},{5,7},{6,4},{7,5},{8,10},{9,11},{10,... | collective-permute-start | bytes 589832 | tf_op jit(solution)/shard_map/ppermute | solution.py:238
  29.2 10.2 %collective-permute-start.4 = (f32[128,256]{1,0:T(8,128)S(1)}, f32[128,256]{1,0:T(8,128)S(1)}, u32[]{:S(2)}, u32[]{:S(2)}) collective-permute-start(f32[128,256]{1,0:T(8,128)S(1)} %shard_map.53), channel_id=1, source_target_pairs={{0,2},{1,3},{2,0},{3,1},{4,6},{5,7},{6,4},{7,5},{8,10},{9,11},{10,... | collective-permute-start | bytes 393224 | tf_op jit(solution)/shard_map/ppermute | solution.py:238
  33.0 6.3 %collective-permute-start.9 = (f32[128,256]{1,0:T(8,128)S(1)}, f32[128,256]{1,0:T(8,128)S(1)}, u32[]{:S(2)}, u32[]{:S(2)}) collective-permute-start(f32[128,256]{1,0:T(8,128)S(1)} %shard_map.58), channel_id=1, source_target_pairs={{0,8},{1,9},{2,10},{3,11},{4,12},{5,13},{6,14},{7,15},{8,0},{9,1},... | collective-permute-start | bytes 393224 | tf_op jit(solution)/shard_map/ppermute | solution.py:238
  34.6 5.9 %collective-permute-start.10 = (f32[72,384]{1,0:T(8,128)S(1)}, f32[72,384]{1,0:T(8,128)S(1)}, u32[]{:S(2)}, u32[]{:S(2)}) collective-permute-start(f32[72,384]{1,0:T(8,128)S(1)} %shard_map.59), channel_id=1, source_target_pairs={{0,2},{1,3},{2,0},{3,1},{4,6},{5,7},{6,4},{7,5},{8,10},{9,11},{10,... | collective-permute-start | bytes 331784 | tf_op jit(solution)/shard_map/ppermute | solution.py:238
  37.3 5.9 %collective-permute-start.11 = (f32[64,384]{1,0:T(8,128)S(1)}, f32[64,384]{1,0:T(8,128)S(1)}, u32[]{:S(2)}, u32[]{:S(2)}) collective-permute-start(f32[64,384]{1,0:T(8,128)S(1)} %shard_map.60), channel_id=1, source_target_pairs={{0,8},{1,9},{2,10},{3,11},{4,12},{5,13},{6,14},{7,15},{8,0},{9,1},... | collective-permute-start | bytes 294920 | tf_op jit(solution)/shard_map/ppermute | solution.py:238
  39.4 5.2 %collective-permute-start.12 = (f32[64,256]{1,0:T(8,128)S(1)}, f32[64,256]{1,0:T(8,128)S(1)}, u32[]{:S(2)}, u32[]{:S(2)}) collective-permute-start(f32[64,256]{1,0:T(8,128)S(1)} %shard_map.61), channel_id=1, source_target_pairs={{0,16},{1,17},{2,18},{3,19},{4,20},{5,21},{6,22},{7,23},{8,24},{9,... | collective-permute-start | bytes 196616 | tf_op jit(solution)/shard_map/ppermute | solution.py:238
  40.6 9.0 %collective-permute-start.13 = (f32[40,384]{1,0:T(8,128)S(1)}, f32[40,384]{1,0:T(8,128)S(1)}, u32[]{:S(2)}, u32[]{:S(2)}) collective-permute-start(f32[40,384]{1,0:T(8,128)S(1)} %shard_map.62), channel_id=1, source_target_pairs={{0,4},{1,5},{2,6},{3,7},{4,0},{5,1},{6,2},{7,3},{8,12},{9,13},{10,... | collective-permute-start | bytes 184328 | tf_op jit(solution)/shard_map/ppermute | solution.py:238
  43.2 6.4 %collective-permute-start.14 = (f32[32,384]{1,0:T(8,128)S(1)}, f32[32,384]{1,0:T(8,128)S(1)}, u32[]{:S(2)}, u32[]{:S(2)}) collective-permute-start(f32[32,384]{1,0:T(8,128)S(1)} %shard_map.63), channel_id=1, source_target_pairs={{0,4},{1,5},{2,6},{3,7},{4,0},{5,1},{6,2},{7,3},{8,12},{9,13},{10,... | collective-permute-start | bytes 147464 | tf_op jit(solution)/shard_map/ppermute | solution.py:238
  44.6 5.0 %collective-permute-start.15 = (f32[32,256]{1,0:T(8,128)S(1)}, f32[32,256]{1,0:T(8,128)S(1)}, u32[]{:S(2)}, u32[]{:S(2)}) collective-permute-start(f32[32,256]{1,0:T(8,128)S(1)} %shard_map.64), channel_id=1, source_target_pairs={{0,4},{1,5},{2,6},{3,7},{4,0},{5,1},{6,2},{7,3},{8,12},{9,13},{10,... | collective-permute-start | bytes 98312 | tf_op jit(solution)/shard_map/ppermute | solution.py:238

commit v3 on v0

v3 whole, which is shorter than its diff:
```python
import functools

import jax
import jax.numpy as jnp
from jax import lax
from jax.experimental import pallas as pl
from jax.experimental.pallas import tpu as pltpu
from jax.sharding import PartitionSpec as P

EXTRA = 8
SMEM = pl.BlockSpec(memory_space=pltpu.SMEM)
VMEM = pl.BlockSpec(memory_space=pltpu.VMEM)
HBM = pl.BlockSpec(memory_space=pltpu.HBM)


def member_masks(members):
    near = [1 << bit for bit in range(1, members.bit_length() - 1)]
    far = list(near)
    for i in range(0, len(far) - 1, 2):
        far[i], far[i + 1] = far[i + 1], far[i]
    return near, far


def member_order(masks):
    order = []
    for place in range(1 << len(masks)):
        member = 0
        for i, mask in enumerate(masks):
            if not place >> (len(masks) - 1 - i) & 1:
                member ^= mask
        order.append(member)
    return order


def dot_transposed(a, b):
    return lax.dot_general(a, b, (((0,), (0,)), ((), ())), preferred_element_type=jnp.float32)


def block_columns(group, key, block):
    return pl.ds(pl.multiple_of((group ^ key) * block, block), block)


def write_rows(outs, chunks, me, members, rows, keys):
    group, member = me // members, me % members
    core = me % 2
    block = members * rows
    orders = [member_order(masks) for masks in member_masks(members)]
    for out, other in zip(outs, (0, 1)):
        owner = core ^ other
        for c, chunk in enumerate(chunks):
            for i, (even, odd) in enumerate(zip(*orders)):
                relative = jnp.where(owner == 0, even, odd)
                start = ((member ^ other) ^ relative) * rows
                at = pl.ds((c * len(orders[0]) + i) * rows, rows)
                for n, key in enumerate(keys):
                    ref, row, column = chunk(owner, n)
                    source = pl.ds(pl.multiple_of(row + start, rows), rows)
                    out[at, block_columns(group, key, block)] = ref[source, pl.ds(column, block)]


def first_kernel(me_ref, len_hbm, x_hbm, mine_ref, theirs_ref, x_ref, acc_ref,
                 len_ref, sums_ref, sem, *, tile, keys, members, rows, pack):
    depth, width = x_hbm.shape
    block = members * rows
    tiles = depth // tile
    half_tiles = tiles // 2
    me = me_ref[0]
    group = me // members

    lengths = pltpu.make_async_copy(len_hbm, len_ref, sem.at[tiles])
    lengths.start()
    for i in range(tiles):
        part = pl.ds(i * tile, tile)
        for n, key in enumerate(keys):
            pltpu.make_async_copy(
                x_hbm.at[part, block_columns(group, key, block)],
                x_ref.at[part, pl.ds(n * block, block)],
                sem.at[i],
            ).start()
    lengths.wait()
    total = jnp.zeros((1, width), jnp.float32)
    for i in range(tiles):
        part = pl.ds(i * tile, tile)
        pltpu.make_async_copy(x_hbm.at[part], x_ref.at[part], sem.at[i]).wait()
        valid = len_ref[0, i // half_tiles] - (i % half_tiles) * tile

        @pl.when(valid < tile)
        def _():
            x = x_ref[part, :]
            position = lax.broadcasted_iota(jnp.int32, x.shape, 0)
            x_ref[part, :] = jnp.where(position < valid, x, jnp.zeros_like(x))

        total += jnp.sum(x_ref[part, :].astype(jnp.float32), axis=0, keepdims=True)
        product = dot_transposed(x_ref[part, 0:block], x_ref[part, :])
        if i:
            acc_ref[...] += product
        else:
            acc_ref[...] = product
    write_rows(
        (mine_ref, theirs_ref), [lambda owner, n: (acc_ref, 0, n * block)], me, members, rows, keys
    )
    for n, key in enumerate(keys):
        sums_ref[0:1, block_columns(group, key, block)] = total[:, n * block:(n + 1) * block]
    count = (len_ref[0, 0] + len_ref[0, 1]).astype(jnp.float32)
    for ref in (mine_ref, theirs_ref):
        ref[pl.ds(block // 2, EXTRA), :] = jnp.full((EXTRA, width), count)
        for line, start in enumerate(range(0, width, pack)):
            ref[pl.ds(block // 2 + line, 1), 0:pack] = sums_ref[0:1, start:start + pack]


def second_kernel(x_ref, acc_ref, *, block):
    acc_ref[...] = dot_transposed(x_ref[:, block:2 * block], x_ref[:, block:])


def third_kernel(me_ref, x_ref, first_ref, second_ref, after_ref, mine_ref, theirs_ref,
                 mine_rest_ref, theirs_rest_ref, acc_ref, *, keys, members, rows):
    block = members * rows

    def cut(n):
        return slice(n * block, (n + 1) * block)

    for n in (1, 2, 3):
        acc_ref[cut(n - 1), cut(0)] = first_ref[:, cut(n)].T
    acc_ref[cut(0), block:] = second_ref[...]
    for n in (2, 3):
        acc_ref[cut(n - 1), cut(1)] = second_ref[:, cut(n - 1)].T
    acc_ref[cut(1), 2 * block:] = dot_transposed(x_ref[:, cut(2)], x_ref[:, 2 * block:])
    acc_ref[cut(2), cut(3)] = dot_transposed(x_ref[:, cut(3)], x_ref[:, cut(3)])
    acc_ref[cut(2), cut(2)] = acc_ref[cut(1), cut(3)].T

    def step_one(owner, n):
        return acc_ref, owner * block, n * block

    def step_two(owner, n):
        return acc_ref, (1 - owner) * block, n * block

    def kept(owner, n):
        return acc_ref, 2 * block, n * block

    me = me_ref[0]
    write_rows((mine_ref, theirs_ref), [step_one], me, members, rows, keys)
    write_rows((mine_rest_ref, theirs_rest_ref), [step_two, kept], me, members, rows, keys)


def total_of(refs, terms, height, size):
    parts = [refs[i][pl.ds(row, height), pl.ds(column, size)] for i, row, column in terms]
    return sum(parts[1:], parts[0])


def sum_kernel(*refs, plan, size):
    out = refs[-1]
    at = 0
    for height, terms in plan:
        out[pl.ds(at, height), :] = total_of(refs, terms, height, size)
        at += height


def finish_kernel(me_ref, *refs, chains, extra, rows):
    cov_ref, mean_ref, count_ref = refs[-3:]
    width = cov_ref.shape[1]
    pack = width // len(chains)
    block = total_of(refs, extra, EXTRA, pack)
    total = jnp.concatenate([block[i:i + 1] for i in range(len(chains))], axis=1)
    count = block[len(chains):len(chains) + 1, 0:1]
    lane = lax.broadcasted_iota(jnp.int32, (rows, width), 1)
    row = lax.broadcasted_iota(jnp.int32, (rows, width), 0)
    own = jnp.sum(
        jnp.where(lane == row + me_ref[0] * rows, total, 0.0), axis=1, keepdims=True
    )
    mean = total / count
    mean_ref[...] = mean
    count_ref[...] = count
    for c, terms in enumerate(chains):
        at = slice(c * pack, (c + 1) * pack)
        second = total_of(refs, terms, rows, pack) - own * mean[:, at]
        cov_ref[:, at] = second / (count - 1.0)


def limit(mebibytes):
    return pltpu.CompilerParams(vmem_limit_bytes=mebibytes << 20)


def solution(mesh):
    axes = ("grp", "mem")
    groups, members = mesh.shape["grp"], mesh.shape["mem"]
    devices = groups * members
    keys = (3, 1, 2, 0)
    assert groups == len(keys)
    near, far = member_masks(members)
    steps = [(members, 2 * members), (2 * members, members), *zip(near, far)]

    def swap(value, masks):
        pairs = [(i, i ^ masks[i % 2]) for i in range(devices)]
        return lax.ppermute(value, axes, pairs)

    def body(features, lengths):
        depth, width = features.shape
        rows = width // devices
        block = members * rows
        half = block // 2
        pack = width // 2
        me = (lax.axis_index("grp") * members + lax.axis_index("mem")).reshape(1)

        def f32(height, size=width):
            return jax.ShapeDtypeStruct((height, size), jnp.float32)

        def cost(blocks):
            return pl.CostEstimate(
                flops=2 * depth * block * block * blocks,
                bytes_accessed=depth * width * 2,
                transcendentals=0,
            )

        tile = depth // 4
        sizes = dict(keys=keys, members=members, rows=rows)
        mine, theirs, x, acc = pl.pallas_call(
            functools.partial(first_kernel, tile=tile, pack=pack, **sizes),
            out_shape=[f32(half + EXTRA)] * 2
            + [jax.ShapeDtypeStruct(features.shape, features.dtype), f32(block)],
            in_specs=[SMEM, HBM, HBM],
            out_specs=[VMEM] * 4,
            scratch_shapes=[
                pltpu.SMEM(lengths.shape, jnp.int32),
                pltpu.VMEM((EXTRA, width), jnp.float32),
                pltpu.SemaphoreType.DMA((depth // tile + 1,)),
            ],
            compiler_params=limit(40),
            cost_estimate=cost(4),
        )(me, lengths, features)
        arrays, narrow = [], []
        acc_next = pl.pallas_call(
            functools.partial(second_kernel, block=block),
            out_shape=jax.ShapeDtypeStruct((block, width - block), jnp.float32),
            in_specs=[VMEM],
            out_specs=VMEM,
            compiler_params=limit(32),
            cost_estimate=cost(3),
        )(x)

        def localise(used, terms, start):
            return [(used.index(i), row, 0 if narrow[i] else start) for i, row in terms]

        def total(plan, start, size, after=()):
            used = sorted({i for _, terms in plan for i, _ in terms}.union(after))
            plan = [(height, localise(used, terms, start)) for height, terms in plan]
            return pl.pallas_call(
                functools.partial(sum_kernel, plan=plan, size=size),
                out_shape=f32(sum(height for height, _ in plan), size),
                in_specs=[VMEM] * len(used),
                out_specs=VMEM,
                compiler_params=limit(12),
                cost_estimate=pl.CostEstimate(flops=1, bytes_accessed=1, transcendentals=0),
            )(*[arrays[i] for i in used])

        def put(array, wide=True):
            arrays.append(array)
            narrow.append(not wide)
            return len(arrays) - 1

        one, one_in = put(mine), put(swap(theirs, (1, 1)))
        extra = [(one, half), (one_in, half)]
        message = total([(half, [(one, 0), (one_in, 0)]), (EXTRA, extra)], 0, width)
        one_next = put(swap(message, steps[0]))
        mine, theirs, mine_rest, theirs_rest = pl.pallas_call(
            functools.partial(third_kernel, **sizes),
            out_shape=[f32(half)] * 2 + [f32(2 * half)] * 2,
            in_specs=[SMEM] + [VMEM] * 4,
            out_specs=[VMEM] * 4,
            scratch_shapes=[pltpu.VMEM((3 * block, width), jnp.float32)],
            compiler_params=limit(32),
            cost_estimate=cost(3),
        )(me, x, acc, acc_next, message)
        two, two_in = put(mine), put(swap(theirs, (1, 1)))
        rest, rest_in = put(mine_rest), put(swap(theirs_rest, (1, 1)))
        extra.append((one_next, half))

        starts = range(0, width, pack)
        two_next = [
            put(swap(total([(half, [(two, 0), (two_in, 0)])], start, pack), steps[0]), False)
            for start in starts
        ]
        chains = []
        for start, two_out in zip(starts, two_next):
            carried = [] if start else [(EXTRA, extra)]
            message = total(
                [(half, [(rest, 0), (rest_in, 0), (one_next, 0)])] + carried, start, pack, [two_out]
            )
            added = put(swap(message, steps[1]), False)
            chains.append([(rest, half), (rest_in, half), (two_out, 0), (added, 0)])
            if not start:
                extra = extra + [(added, half)]
        height = half
        for masks in steps[2:]:
            height //= 2
            for c, start in enumerate(starts):
                carried = [] if start else [(EXTRA, extra)]
                message = total([(height, chains[c])] + carried, start, pack)
                added = put(swap(message, masks), False)
                chains[c] = [(i, row + height) for i, row in chains[c]] + [(added, 0)]
                if not start:
                    extra = extra + [(added, height)]

        used = sorted({i for terms in chains + [extra] for i, _ in terms})
        covariance, mean, count = pl.pallas_call(
            functools.partial(
                finish_kernel,
                chains=[localise(used, terms, start) for terms, start in zip(chains, starts)],
                extra=localise(used, extra, 0),
                rows=rows,
            ),
            out_shape=[f32(rows), f32(1), jax.ShapeDtypeStruct((1, 1), jnp.float32)],
            in_specs=[SMEM] + [VMEM] * len(used),
            out_specs=[VMEM] * 3,
            compiler_params=limit(12),
            cost_estimate=pl.CostEstimate(flops=1, bytes_accessed=1, transcendentals=0),
        )(me, *[arrays[i] for i in used])
        return count.reshape(1), mean.reshape(width), covariance

    return jax.shard_map(
        body,
        mesh=mesh,
        in_specs=(P(axes, None), P(axes, None)),
        out_specs=(P(), P(), P(axes, None)),
        check_vma=False,
    )
```

time: 172 us -> 46.8 us (0.27)
  waiting for transfers between devices: 87 us -> 14.2 us
  blocking collectives: 42.8 us -> 0 us
  matrix products: 21.7 us -> 0 us
  starting transfers between devices: 0.08 us -> 20.9 us
  between operations: 15.4 us -> 0.72 us
  Pallas kernels: 0 us -> 10.1 us
  other arithmetic: 4.86 us -> 0 us
    reduce_scatter x2 -> x0, waiting for transfers between devices: 87 us -> none  [the longest x1 52.8 us: body(): lax.psum_scatter(lax.dot_general(masked, masked, (((0,), (0,)), ((), ()))...]
    psum x1 -> x0, blocking collectives: 42.8 us -> none  [body(): total_count, total_sum = lax.psum((own_count, own_sum), ('grp', 'mem'))]
    dot_general x2 -> x0, matrix products: 21.7 us -> none  [the longest x1 17.2 us: body(): lax.dot_general(masked, masked, (((0,), (0,)), ((), ())), preferred_eleme...]
    ppermute x0 -> x12, starting transfers between devices: none -> 20.9 us  [swap(): return lax.ppermute(value, axes, pairs)]
    ppermute x0 -> x12, waiting for transfers between devices: none -> 14.2 us  [swap(): return lax.ppermute(value, axes, pairs)]
    pallas_call x0 -> x13, Pallas kernels: none -> 10.1 us  [the longest x1 5.02 us: body(): pl.pallas_call(functools.partial(first_kernel, tile=tile, pack=pack, **si...]
  transfers between devices with their start and end apart: 2 -> 12, of which waited for: 2 -> 9; matrix products, arithmetic and copies ran while one was open for 0% -> 0% of each run, Pallas kernels for 0% -> 5%
where the time goes in v3:
time: 46.8 us; the launch traced here: 46.6 us
  starting transfers between devices  20.9 us (45%)
  waiting for transfers between devices  14.2 us (30%)
  Pallas kernels  10.1 us (22%)
  between operations  0.72 us (2%)
  local copies, waits for them, and re-layouts  0.65 us (1%)
    ppermute x12, starting transfers between devices, swap(): return lax.ppermute(value, axes, pairs)  20.9 us
    ppermute x12, waiting for transfers between devices, swap(): return lax.ppermute(value, axes, pairs)  14.2 us
    pallas_call x1, Pallas kernels, body(): pl.pallas_call(functools.partial(first_kernel, tile=tile, pack=pack, **si...  5.02 us
    pallas_call x1, Pallas kernels, body(): pl.pallas_call(functools.partial(third_kernel, **sizes), out_shape=[f32(h...  2.17 us
    pallas_call x1, Pallas kernels, body(): pl.pallas_call(functools.partial(second_kernel, block=block), out_shape=j...  1.88 us
  transfers between devices with their start and end apart: 12, of which 9 were waited for; matrix products, arithmetic and copies ran while one was open for 0% of the time, Pallas kernels for 5%

profile of v3, /device:TPU:0, one launch (start us, length us, event | category | flops | bytes accessed | tf_op | source)
XLA Modules:
  0.0 46.6 jit_solution(7865606705600275305)
XLA Ops:
  0.6 0.0 copy-start
  0.6 0.6 %copy-done = s32[1,2]{1,0:T(1,128)S(1)} copy-done((s32[1,2]{1,0:T(1,128)S(1)}, s32[1,2]{1,0:T(1,128)}, u32[]{:S(2)}) %copy-start) | copy-done | bytes 32
  1.3 5.0 %shard_map.49 = (f32[136,1024]{1,0:T(8,128)S(1)}, f32[136,1024]{1,0:T(8,128)S(1)}, bf16[4096,1024]{1,0:T(8,128)(2,1)S(1)}, f32[256,1024]{1,0:T(8,128)S(1)}) custom-call(s32[1]{0:T(128)} %bitcast.me_ref, s32[1,2]{1,0:T(1,128)S(1)} %copy-done, bf16[4096,1024]{1,0:T(8,128)(2,1)} %x_hbm.1), custom_call_target="tpu_custom_call" | custom-call | flops 2147483648 | bytes 8388608 | tf_op jit(solution)/shard_map/pallas_call | solution.py:216
  6.3 0.5 %collective-permute-start = (f32[136,1024]{1,0:T(8,128)S(1)}, f32[136,1024]{1,0:T(8,128)S(1)}, u32[]{:S(2)}, u32[]{:S(2)}) collective-permute-start(f32[136,1024]{1,0:T(8,128)S(1)} %get-tuple-element.15), channel_id=1, source_target_pairs={{0,1},{1,0},{2,3},{3,2},{4,5},{5,4},{6,7},{7,6},{8,9},{9,8},{10,11... | collective-permute-start | bytes 1671176 | tf_op jit(solution)/shard_map/ppermute | solution.py:194
  6.8 1.9 %shard_map.51.second_ref = f32[256,768]{1,0:T(8,128)S(1)} custom-call(bf16[4096,1024]{1,0:T(8,128)(2,1)S(1)} %get-tuple-element.16.x_ref), custom_call_target="tpu_custom_call" | custom-call | flops 1610612736 | bytes 8388608 | tf_op jit(solution)/shard_map/pallas_call | solution.py:231
  8.7 0.0 collective-permute-done.refs_1_
  8.7 0.1 shard_map.50.after_ref
  8.8 2.2 %shard_map.52 = (f32[128,1024]{1,0:T(8,128)S(1)}, f32[128,1024]{1,0:T(8,128)S(1)}, f32[256,1024]{1,0:T(8,128)S(1)}, f32[256,1024]{1,0:T(8,128)S(1)}) custom-call(s32[1]{0:T(128)} %bitcast.me_ref, bf16[4096,1024]{1,0:T(8,128)(2,1)S(1)} %get-tuple-element.16.x_ref, f32[256,1024]{1,0:T(8,128)S(1)} %get-tuple-element.17.first_ref, ...), custom_call_target="tpu_custom_call" | custom-call | flops 1610612736 | bytes 8388608 | tf_op jit(solution)/shard_map/pallas_call | solution.py:264
  11.0 0.1 collective-permute-start.2
  11.1 0.4 collective-permute-start.3
  11.6 2.6 %collective-permute-start.1 = (f32[136,1024]{1,0:T(8,128)S(1)}, f32[136,1024]{1,0:T(8,128)S(1)}, u32[]{:S(2)}, u32[]{:S(2)}) collective-permute-start(f32[136,1024]{1,0:T(8,128)S(1)} %shard_map.50.after_ref), channel_id=1, source_target_pairs={{0,8},{1,17},{2,10},{3,19},{4,12},{5,21},{6,14},{7,23},{8,0},{9,25... | collective-permute-start | bytes 1671176 | tf_op jit(solution)/shard_map/ppermute | solution.py:194
  14.1 0.3 collective-permute-done.3.refs_1_
  14.5 2.7 %collective-permute-start.4 = (f32[128,512]{1,0:T(8,128)S(1)}, f32[128,512]{1,0:T(8,128)S(1)}, u32[]{:S(2)}, u32[]{:S(2)}) collective-permute-start(f32[128,512]{1,0:T(8,128)S(1)} %shard_map.53), channel_id=1, source_target_pairs={{0,8},{1,17},{2,10},{3,19},{4,12},{5,21},{6,14},{7,23},{8,0},{9,25... | collective-permute-start | bytes 786440 | tf_op jit(solution)/shard_map/ppermute | solution.py:194
  17.2 0.1 collective-permute-start.5
  17.3 4.3 %collective-permute-done.1.refs_2_.refs_0_ = f32[136,1024]{1,0:T(8,128)S(1)} collective-permute-done((f32[136,1024]{1,0:T(8,128)S(1)}, f32[136,1024]{1,0:T(8,128)S(1)}, u32[]{:S(2)}, u32[]{:S(2)}) %collective-permute-start.1) | collective-permute-done | bytes 557088 | tf_op jit(solution)/shard_map/ppermute | solution.py:194
  21.6 2.8 %collective-permute-done.4.refs_5_ = f32[128,512]{1,0:T(8,128)S(1)} collective-permute-done((f32[128,512]{1,0:T(8,128)S(1)}, f32[128,512]{1,0:T(8,128)S(1)}, u32[]{:S(2)}, u32[]{:S(2)}) %collective-permute-start.4) | collective-permute-done | bytes 262176 | tf_op jit(solution)/shard_map/ppermute | solution.py:194
  24.4 0.0 collective-permute-done.2.refs_4_.refs_2_.refs_1_
  24.5 1.8 %collective-permute-start.6 = (f32[136,512]{1,0:T(8,128)S(1)}, f32[136,512]{1,0:T(8,128)S(1)}, u32[]{:S(2)}, u32[]{:S(2)}) collective-permute-start(f32[136,512]{1,0:T(8,128)S(1)} %shard_map.55), channel_id=1, source_target_pairs={{0,16},{1,9},{2,18},{3,11},{4,20},{5,13},{6,22},{7,15},{8,24},{9,1... | collective-permute-start | bytes 835592 | tf_op jit(solution)/shard_map/ppermute | solution.py:194
  26.3 1.1 %collective-permute-done.5.refs_3_.refs_2_.refs_6_ = f32[128,512]{1,0:T(8,128)S(1)} collective-permute-done((f32[128,512]{1,0:T(8,128)S(1)}, f32[128,512]{1,0:T(8,128)S(1)}, u32[]{:S(2)}, u32[]{:S(2)}) %collective-permute-start.5) | collective-permute-done | bytes 262176 | tf_op jit(solution)/shard_map/ppermute | solution.py:194
  27.5 2.1 %collective-permute-start.7 = (f32[128,512]{1,0:T(8,128)S(1)}, f32[128,512]{1,0:T(8,128)S(1)}, u32[]{:S(2)}, u32[]{:S(2)}) collective-permute-start(f32[128,512]{1,0:T(8,128)S(1)} %shard_map.56), channel_id=1, source_target_pairs={{0,16},{1,9},{2,18},{3,11},{4,20},{5,13},{6,22},{7,15},{8,24},{9,1... | collective-permute-start | bytes 786440 | tf_op jit(solution)/shard_map/ppermute | solution.py:194
  29.6 1.6 %collective-permute-done.6.refs_6_.refs_7_ = f32[136,512]{1,0:T(8,128)S(1)} collective-permute-done((f32[136,512]{1,0:T(8,128)S(1)}, f32[136,512]{1,0:T(8,128)S(1)}, u32[]{:S(2)}, u32[]{:S(2)}) %collective-permute-start.6) | collective-permute-done | bytes 278560 | tf_op jit(solution)/shard_map/ppermute | solution.py:194
  31.1 2.2 %collective-permute-start.8 = (f32[72,512]{1,0:T(8,128)S(1)}, f32[72,512]{1,0:T(8,128)S(1)}, u32[]{:S(2)}, u32[]{:S(2)}) collective-permute-start(f32[72,512]{1,0:T(8,128)S(1)} %shard_map.57), channel_id=1, source_target_pairs={{0,2},{1,5},{2,0},{3,7},{4,6},{5,1},{6,4},{7,3},{8,10},{9,13},{10,... | collective-permute-start | bytes 442376 | tf_op jit(solution)/shard_map/ppermute | solution.py:194
  33.3 0.6 %collective-permute-done.7.refs_3_.refs_8_ = f32[128,512]{1,0:T(8,128)S(1)} collective-permute-done((f32[128,512]{1,0:T(8,128)S(1)}, f32[128,512]{1,0:T(8,128)S(1)}, u32[]{:S(2)}, u32[]{:S(2)}) %collective-permute-start.7) | collective-permute-done | bytes 262176 | tf_op jit(solution)/shard_map/ppermute | solution.py:194
  34.0 2.4 %collective-permute-start.9 = (f32[64,512]{1,0:T(8,128)S(1)}, f32[64,512]{1,0:T(8,128)S(1)}, u32[]{:S(2)}, u32[]{:S(2)}) collective-permute-start(f32[64,512]{1,0:T(8,128)S(1)} %shard_map.58), channel_id=1, source_target_pairs={{0,2},{1,5},{2,0},{3,7},{4,6},{5,1},{6,4},{7,3},{8,10},{9,13},{10,... | collective-permute-start | bytes 393224 | tf_op jit(solution)/shard_map/ppermute | solution.py:194
  36.4 0.8 %collective-permute-done.8.refs_7_.refs_9_ = f32[72,512]{1,0:T(8,128)S(1)} collective-permute-done((f32[72,512]{1,0:T(8,128)S(1)}, f32[72,512]{1,0:T(8,128)S(1)}, u32[]{:S(2)}, u32[]{:S(2)}) %collective-permute-start.8) | collective-permute-done | bytes 147488 | tf_op jit(solution)/shard_map/ppermute | solution.py:194
  37.2 3.0 %collective-permute-start.10 = (f32[40,512]{1,0:T(8,128)S(1)}, f32[40,512]{1,0:T(8,128)S(1)}, u32[]{:S(2)}, u32[]{:S(2)}) collective-permute-start(f32[40,512]{1,0:T(8,128)S(1)} %shard_map.59), channel_id=1, source_target_pairs={{0,4},{1,3},{2,6},{3,1},{4,0},{5,7},{6,2},{7,5},{8,12},{9,11},{10,... | collective-permute-start | bytes 245768 | tf_op jit(solution)/shard_map/ppermute | solution.py:194
  40.2 0.4 collective-permute-done.9.refs_4_.refs_10_
  40.6 3.0 %collective-permute-start.11 = (f32[32,512]{1,0:T(8,128)S(1)}, f32[32,512]{1,0:T(8,128)S(1)}, u32[]{:S(2)}, u32[]{:S(2)}) collective-permute-start(f32[32,512]{1,0:T(8,128)S(1)} %shard_map.60), channel_id=1, source_target_pairs={{0,4},{1,3},{2,6},{3,1},{4,0},{5,7},{6,2},{7,5},{8,12},{9,11},{10,... | collective-permute-start | bytes 196616 | tf_op jit(solution)/shard_map/ppermute | solution.py:194
  43.6 2.2 %collective-permute-done.11.refs_12_ = f32[32,512]{1,0:T(8,128)S(1)} collective-permute-done((f32[32,512]{1,0:T(8,128)S(1)}, f32[32,512]{1,0:T(8,128)S(1)}, u32[]{:S(2)}, u32[]{:S(2)}) %collective-permute-start.11) | collective-permute-done | bytes 65568 | tf_op jit(solution)/shard_map/ppermute | solution.py:194
  45.9 0.0 collective-permute-done.10.refs_11_
  45.9 0.8 %shard_map.61 = (f32[32,1024]{1,0:T(8,128)}, f32[1,1024]{1,0:T(1,128)}, f32[1,1]{1,0:T(1,128)}) custom-call(s32[1]{0:T(128)} %bitcast.me_ref, f32[136,1024]{1,0:T(8,128)S(1)} %get-tuple-element.14.refs_0_, f32[136,1024]{1,0:T(8,128)S(1)} %collective-permute-done.refs_1_, f32[136,1024]{1,0:T(8,128)S(1)} %collective-permute-done.1.refs_2_.refs_0_, ...), custom_call_target="tpu_custom_call" | custom-call | flops 1 | bytes 1 | tf_op jit(solution)/shard_map/pallas_call | solution.py:304
  (8 shorter events, 0.2 us)
Async XLA Ops:
  0.6 0.7 %copy-start = (s32[1,2]{1,0:T(1,128)S(1)}, s32[1,2]{1,0:T(1,128)}, u32[]{:S(2)}) copy-start(s32[1,2]{1,0:T(1,128)} %len_hbm.1) | copy-start | bytes 28
  6.3 2.4 %collective-permute-start = (f32[136,1024]{1,0:T(8,128)S(1)}, f32[136,1024]{1,0:T(8,128)S(1)}, u32[]{:S(2)}, u32[]{:S(2)}) collective-permute-start(f32[136,1024]{1,0:T(8,128)S(1)} %get-tuple-element.15), channel_id=1, source_target_pairs={{0,1},{1,0},{2,3},{3,2},{4,5},{5,4},{6,7},{7,6},{8,9},{9,8},{10,11... | collective-permute-start | bytes 1671176 | tf_op jit(solution)/shard_map/ppermute | solution.py:194
  11.0 13.5 %collective-permute-start.2 = (f32[256,1024]{1,0:T(8,128)S(1)}, f32[256,1024]{1,0:T(8,128)S(1)}, u32[]{:S(2)}, u32[]{:S(2)}) collective-permute-start(f32[256,1024]{1,0:T(8,128)S(1)} %get-tuple-element.19), channel_id=1, source_target_pairs={{0,1},{1,0},{2,3},{3,2},{4,5},{5,4},{6,7},{7,6},{8,9},{9,8},{10,11... | collective-permute-start | bytes 3145736 | tf_op jit(solution)/shard_map/ppermute | solution.py:194
  11.1 3.3 %collective-permute-start.3 = (f32[128,1024]{1,0:T(8,128)S(1)}, f32[128,1024]{1,0:T(8,128)S(1)}, u32[]{:S(2)}, u32[]{:S(2)}) collective-permute-start(f32[128,1024]{1,0:T(8,128)S(1)} %get-tuple-element.21), channel_id=1, source_target_pairs={{0,1},{1,0},{2,3},{3,2},{4,5},{5,4},{6,7},{7,6},{8,9},{9,8},{10,11... | collective-permute-start | bytes 1572872 | tf_op jit(solution)/shard_map/ppermute | solution.py:194
  11.6 10.1 %collective-permute-start.1 = (f32[136,1024]{1,0:T(8,128)S(1)}, f32[136,1024]{1,0:T(8,128)S(1)}, u32[]{:S(2)}, u32[]{:S(2)}) collective-permute-start(f32[136,1024]{1,0:T(8,128)S(1)} %shard_map.50.after_ref), channel_id=1, source_target_pairs={{0,8},{1,17},{2,10},{3,19},{4,12},{5,21},{6,14},{7,23},{8,0},{9,25... | collective-permute-start | bytes 1671176 | tf_op jit(solution)/shard_map/ppermute | solution.py:194
  14.5 10.0 %collective-permute-start.4 = (f32[128,512]{1,0:T(8,128)S(1)}, f32[128,512]{1,0:T(8,128)S(1)}, u32[]{:S(2)}, u32[]{:S(2)}) collective-permute-start(f32[128,512]{1,0:T(8,128)S(1)} %shard_map.53), channel_id=1, source_target_pairs={{0,8},{1,17},{2,10},{3,19},{4,12},{5,21},{6,14},{7,23},{8,0},{9,25... | collective-permute-start | bytes 786440 | tf_op jit(solution)/shard_map/ppermute | solution.py:194
  17.2 10.2 %collective-permute-start.5 = (f32[128,512]{1,0:T(8,128)S(1)}, f32[128,512]{1,0:T(8,128)S(1)}, u32[]{:S(2)}, u32[]{:S(2)}) collective-permute-start(f32[128,512]{1,0:T(8,128)S(1)} %shard_map.54), channel_id=1, source_target_pairs={{0,8},{1,17},{2,10},{3,19},{4,12},{5,21},{6,14},{7,23},{8,0},{9,25... | collective-permute-start | bytes 786440 | tf_op jit(solution)/shard_map/ppermute | solution.py:194
  24.5 6.6 %collective-permute-start.6 = (f32[136,512]{1,0:T(8,128)S(1)}, f32[136,512]{1,0:T(8,128)S(1)}, u32[]{:S(2)}, u32[]{:S(2)}) collective-permute-start(f32[136,512]{1,0:T(8,128)S(1)} %shard_map.55), channel_id=1, source_target_pairs={{0,16},{1,9},{2,18},{3,11},{4,20},{5,13},{6,22},{7,15},{8,24},{9,1... | collective-permute-start | bytes 835592 | tf_op jit(solution)/shard_map/ppermute | solution.py:194
  27.5 6.4 %collective-permute-start.7 = (f32[128,512]{1,0:T(8,128)S(1)}, f32[128,512]{1,0:T(8,128)S(1)}, u32[]{:S(2)}, u32[]{:S(2)}) collective-permute-start(f32[128,512]{1,0:T(8,128)S(1)} %shard_map.56), channel_id=1, source_target_pairs={{0,16},{1,9},{2,18},{3,11},{4,20},{5,13},{6,22},{7,15},{8,24},{9,1... | collective-permute-start | bytes 786440 | tf_op jit(solution)/shard_map/ppermute | solution.py:194
  31.1 6.0 %collective-permute-start.8 = (f32[72,512]{1,0:T(8,128)S(1)}, f32[72,512]{1,0:T(8,128)S(1)}, u32[]{:S(2)}, u32[]{:S(2)}) collective-permute-start(f32[72,512]{1,0:T(8,128)S(1)} %shard_map.57), channel_id=1, source_target_pairs={{0,2},{1,5},{2,0},{3,7},{4,6},{5,1},{6,4},{7,3},{8,10},{9,13},{10,... | collective-permute-start | bytes 442376 | tf_op jit(solution)/shard_map/ppermute | solution.py:194
  34.0 6.6 %collective-permute-start.9 = (f32[64,512]{1,0:T(8,128)S(1)}, f32[64,512]{1,0:T(8,128)S(1)}, u32[]{:S(2)}, u32[]{:S(2)}) collective-permute-start(f32[64,512]{1,0:T(8,128)S(1)} %shard_map.58), channel_id=1, source_target_pairs={{0,2},{1,5},{2,0},{3,7},{4,6},{5,1},{6,4},{7,3},{8,10},{9,13},{10,... | collective-permute-start | bytes 393224 | tf_op jit(solution)/shard_map/ppermute | solution.py:194
  37.2 8.7 %collective-permute-start.10 = (f32[40,512]{1,0:T(8,128)S(1)}, f32[40,512]{1,0:T(8,128)S(1)}, u32[]{:S(2)}, u32[]{:S(2)}) collective-permute-start(f32[40,512]{1,0:T(8,128)S(1)} %shard_map.59), channel_id=1, source_target_pairs={{0,4},{1,3},{2,6},{3,1},{4,0},{5,7},{6,2},{7,5},{8,12},{9,11},{10,... | collective-permute-start | bytes 245768 | tf_op jit(solution)/shard_map/ppermute | solution.py:194
  40.6 5.3 %collective-permute-start.11 = (f32[32,512]{1,0:T(8,128)S(1)}, f32[32,512]{1,0:T(8,128)S(1)}, u32[]{:S(2)}, u32[]{:S(2)}) collective-permute-start(f32[32,512]{1,0:T(8,128)S(1)} %shard_map.60), channel_id=1, source_target_pairs={{0,4},{1,3},{2,6},{3,1},{4,0},{5,7},{6,2},{7,5},{8,12},{9,11},{10,... | collective-permute-start | bytes 196616 | tf_op jit(solution)/shard_map/ppermute | solution.py:194

commit v4 on v3

--- a/solution.py
+++ b/solution.py
@@ -7,7 +7,9 @@
 from jax.experimental.pallas import tpu as pltpu
 from jax.sharding import PartitionSpec as P
 
+LANES = 128
 EXTRA = 8
+CHAINS = 2
 SMEM = pl.BlockSpec(memory_space=pltpu.SMEM)
 VMEM = pl.BlockSpec(memory_space=pltpu.VMEM)
 HBM = pl.BlockSpec(memory_space=pltpu.HBM)
@@ -51,11 +53,16 @@
             for i, (even, odd) in enumerate(zip(*orders)):
                 relative = jnp.where(owner == 0, even, odd)
                 start = ((member ^ other) ^ relative) * rows
-                at = pl.ds((c * len(orders[0]) + i) * rows, rows)
+                place = (c * len(orders[0]) + i) * rows
+                target = out
+                if isinstance(out, tuple):
+                    target = out[place // out[0].shape[0]]
+                    place %= out[0].shape[0]
+                at = pl.ds(place, rows)
                 for n, key in enumerate(keys):
                     ref, row, column = chunk(owner, n)
                     source = pl.ds(pl.multiple_of(row + start, rows), rows)
-                    out[at, block_columns(group, key, block)] = ref[source, pl.ds(column, block)]
+                    target[at, block_columns(group, key, block)] = ref[source, pl.ds(column, block)]
 
 
 def first_kernel(me_ref, len_hbm, x_hbm, mine_ref, theirs_ref, x_ref, acc_ref,
@@ -105,7 +112,8 @@
     for ref in (mine_ref, theirs_ref):
         ref[pl.ds(block // 2, EXTRA), :] = jnp.full((EXTRA, width), count)
         for line, start in enumerate(range(0, width, pack)):
-            ref[pl.ds(block // 2 + line, 1), 0:pack] = sums_ref[0:1, start:start + pack]
+            size = min(pack, width - start)
+            ref[pl.ds(block // 2 + line, 1), 0:size] = sums_ref[0:1, start:start + size]
 
 
 def second_kernel(x_ref, acc_ref, *, block):
@@ -113,7 +121,8 @@
 
 
 def third_kernel(me_ref, x_ref, first_ref, second_ref, after_ref, mine_ref, theirs_ref,
-                 mine_rest_ref, theirs_rest_ref, acc_ref, *, keys, members, rows):
+                 theirs_later_ref, mine_next_ref, theirs_next_ref, mine_last_ref, theirs_last_ref, acc_ref,
+                 *, keys, members, rows):
     block = members * rows
 
     def cut(n):
@@ -138,8 +147,9 @@
         return acc_ref, 2 * block, n * block
 
     me = me_ref[0]
-    write_rows((mine_ref, theirs_ref), [step_one], me, members, rows, keys)
-    write_rows((mine_rest_ref, theirs_rest_ref), [step_two, kept], me, members, rows, keys)
+    write_rows((mine_ref, (theirs_ref, theirs_later_ref)), [step_one], me, members, rows, keys)
+    write_rows((mine_next_ref, theirs_next_ref), [step_two], me, members, rows, keys)
+    write_rows((mine_last_ref, theirs_last_ref), [kept], me, members, rows, keys)
 
 
 def total_of(refs, terms, height, size):
@@ -155,13 +165,14 @@
         at += height
 
 
-def finish_kernel(me_ref, *refs, chains, extra, rows):
+def finish_kernel(me_ref, *refs, chains, ranges, extra, rows):
     cov_ref, mean_ref, count_ref = refs[-3:]
     width = cov_ref.shape[1]
-    pack = width // len(chains)
+    pack = ranges[0][1]
+    lines = -(-width // pack)
     block = total_of(refs, extra, EXTRA, pack)
-    total = jnp.concatenate([block[i:i + 1] for i in range(len(chains))], axis=1)
-    count = block[len(chains):len(chains) + 1, 0:1]
+    total = jnp.concatenate([block[i:i + 1] for i in range(lines)], axis=1)[:, :width]
+    count = block[lines:lines + 1, 0:1]
     lane = lax.broadcasted_iota(jnp.int32, (rows, width), 1)
     row = lax.broadcasted_iota(jnp.int32, (rows, width), 0)
     own = jnp.sum(
@@ -170,10 +181,18 @@
     mean = total / count
     mean_ref[...] = mean
     count_ref[...] = count
-    for c, terms in enumerate(chains):
-        at = slice(c * pack, (c + 1) * pack)
-        second = total_of(refs, terms, rows, pack) - own * mean[:, at]
-        cov_ref[:, at] = second / (count - 1.0)
+    for (start, size), terms in zip(ranges, chains):
+        second = total_of(refs, terms, rows, size) - own * mean[:, start:start + size]
+        cov_ref[:, start:start + size] = second / (count - 1.0)
+
+
+def column_ranges(width, parts):
+    tiles, ranges, start = width // LANES, [], 0
+    for i in range(parts):
+        size = (tiles + parts - 1 - i) // parts * LANES
+        ranges.append((start, size))
+        start += size
+    return ranges
 
 
 def limit(mebibytes):
@@ -198,7 +217,8 @@
         rows = width // devices
         block = members * rows
         half = block // 2
-        pack = width // 2
+        ranges = column_ranges(width, CHAINS)
+        pack = ranges[0][1]
         me = (lax.axis_index("grp") * members + lax.axis_index("mem")).reshape(1)
 
         def f32(height, size=width):
@@ -261,40 +281,39 @@
         extra = [(one, half), (one_in, half)]
         message = total([(half, [(one, 0), (one_in, 0)]), (EXTRA, extra)], 0, width)
         one_next = put(swap(message, steps[0]))
-        mine, theirs, mine_rest, theirs_rest = pl.pallas_call(
+        mine, theirs, theirs_later, mine_next, theirs_next, mine_last, theirs_last = pl.pallas_call(
             functools.partial(third_kernel, **sizes),
-            out_shape=[f32(half)] * 2 + [f32(2 * half)] * 2,
+            out_shape=[f32(half)] + [f32(half // 2)] * 2 + [f32(half)] * 4,
             in_specs=[SMEM] + [VMEM] * 4,
-            out_specs=[VMEM] * 4,
+            out_specs=[VMEM] * 7,
             scratch_shapes=[pltpu.VMEM((3 * block, width), jnp.float32)],
             compiler_params=limit(32),
             cost_estimate=cost(3),
         )(me, x, acc, acc_next, message)
-        two, two_in = put(mine), put(swap(theirs, (1, 1)))
-        rest, rest_in = put(mine_rest), put(swap(theirs_rest, (1, 1)))
+        two, two_in = put(mine), [put(swap(part, (1, 1))) for part in (theirs, theirs_later)]
+        after, after_in = put(mine_next), put(swap(theirs_next, (1, 1)))
+        last, last_in = put(mine_last), put(swap(theirs_last, (1, 1)))
         extra.append((one_next, half))
-
-        starts = range(0, width, pack)
+        both = [(half // 2, [(two, i * half // 2), (other, 0)]) for i, other in enumerate(two_in)]
         two_next = [
-            put(swap(total([(half, [(two, 0), (two_in, 0)])], start, pack), steps[0]), False)
-            for start in starts
+            put(swap(total(both, *columns), steps[0]), False) for columns in ranges
         ]
         chains = []
-        for start, two_out in zip(starts, two_next):
+        for (start, size), two_out in zip(ranges, two_next):
             carried = [] if start else [(EXTRA, extra)]
             message = total(
-                [(half, [(rest, 0), (rest_in, 0), (one_next, 0)])] + carried, start, pack, [two_out]
+                [(half, [(after, 0), (after_in, 0), (one_next, 0)])] + carried, start, size, [two_out]
             )
             added = put(swap(message, steps[1]), False)
-            chains.append([(rest, half), (rest_in, half), (two_out, 0), (added, 0)])
+            chains.append([(last, 0), (last_in, 0), (two_out, 0), (added, 0)])
             if not start:
                 extra = extra + [(added, half)]
         height = half
         for masks in steps[2:]:
             height //= 2
-            for c, start in enumerate(starts):
+            for c, (start, size) in enumerate(ranges):
                 carried = [] if start else [(EXTRA, extra)]
-                message = total([(height, chains[c])] + carried, start, pack)
+                message = total([(height, chains[c])] + carried, start, size)
                 added = put(swap(message, masks), False)
                 chains[c] = [(i, row + height) for i, row in chains[c]] + [(added, 0)]
                 if not start:
@@ -304,7 +323,8 @@
         covariance, mean, count = pl.pallas_call(
             functools.partial(
                 finish_kernel,
-                chains=[localise(used, terms, start) for terms, start in zip(chains, starts)],
+                chains=[localise(used, terms, start) for terms, (start, _) in zip(chains, ranges)],
+                ranges=ranges,
                 extra=localise(used, extra, 0),
                 rows=rows,
             ),

time: 46.8 us -> 44 us (0.940)
  starting transfers between devices: 20.9 us -> 18.9 us
  waiting for transfers between devices: 14.2 us -> 13.4 us
    ppermute x12 -> x14, starting transfers between devices: 20.9 us -> 18.9 us  [swap(): return lax.ppermute(value, axes, pairs)]
    ppermute x12 -> x14, waiting for transfers between devices: 14.2 us -> 13.4 us  [swap(): return lax.ppermute(value, axes, pairs)]
  transfers between devices with their start and end apart: 12 -> 14, of which waited for: 9 -> 9; matrix products, arithmetic and copies ran while one was open for 0% -> 0% of each run, Pallas kernels for 5% -> 10%
where the time goes in v4:
time: 44 us; the launch traced here: 43.9 us
  starting transfers between devices  18.9 us (43%)
  waiting for transfers between devices  13.4 us (30%)
  Pallas kernels  10.1 us (23%)
  between operations  0.73 us (2%)
  local copies, waits for them, and re-layouts  0.65 us (1%)
    ppermute x14, starting transfers between devices, swap(): return lax.ppermute(value, axes, pairs)  18.9 us
    ppermute x14, waiting for transfers between devices, swap(): return lax.ppermute(value, axes, pairs)  13.4 us
    pallas_call x1, Pallas kernels, body(): pl.pallas_call(functools.partial(first_kernel, tile=tile, pack=pack, **si...  5.02 us
    pallas_call x1, Pallas kernels, body(): pl.pallas_call(functools.partial(third_kernel, **sizes), out_shape=[f32(h...  2.17 us
    pallas_call x1, Pallas kernels, body(): pl.pallas_call(functools.partial(second_kernel, block=block), out_shape=j...  1.88 us
  transfers between devices with their start and end apart: 14, of which 9 were waited for; matrix products, arithmetic and copies ran while one was open for 0% of the time, Pallas kernels for 10%

profile of v4, /device:TPU:0, one launch (start us, length us, event | category | flops | bytes accessed | tf_op | source)
XLA Modules:
  0.0 43.9 jit_solution(8824650744596297829)
XLA Ops:
  0.6 0.0 copy-start
  0.6 0.6 %copy-done = s32[1,2]{1,0:T(1,128)S(1)} copy-done((s32[1,2]{1,0:T(1,128)S(1)}, s32[1,2]{1,0:T(1,128)}, u32[]{:S(2)}) %copy-start) | copy-done | bytes 32
  1.3 5.0 %shard_map.49 = (f32[136,1024]{1,0:T(8,128)S(1)}, f32[136,1024]{1,0:T(8,128)S(1)}, bf16[4096,1024]{1,0:T(8,128)(2,1)S(1)}, f32[256,1024]{1,0:T(8,128)S(1)}) custom-call(s32[1]{0:T(128)} %bitcast.me_ref, s32[1,2]{1,0:T(1,128)S(1)} %copy-done, bf16[4096,1024]{1,0:T(8,128)(2,1)} %x_hbm.1), custom_call_target="tpu_custom_call" | custom-call | flops 2147483648 | bytes 8388608 | tf_op jit(solution)/shard_map/pallas_call | solution.py:236
  6.3 0.5 %collective-permute-start = (f32[136,1024]{1,0:T(8,128)S(1)}, f32[136,1024]{1,0:T(8,128)S(1)}, u32[]{:S(2)}, u32[]{:S(2)}) collective-permute-start(f32[136,1024]{1,0:T(8,128)S(1)} %get-tuple-element.18), channel_id=1, source_target_pairs={{0,1},{1,0},{2,3},{3,2},{4,5},{5,4},{6,7},{7,6},{8,9},{9,8},{10,11... | collective-permute-start | bytes 1671176 | tf_op jit(solution)/shard_map/ppermute | solution.py:213
  6.8 1.9 %shard_map.51.second_ref = f32[256,768]{1,0:T(8,128)S(1)} custom-call(bf16[4096,1024]{1,0:T(8,128)(2,1)S(1)} %get-tuple-element.19.x_ref), custom_call_target="tpu_custom_call" | custom-call | flops 1610612736 | bytes 8388608 | tf_op jit(solution)/shard_map/pallas_call | solution.py:251
  8.7 0.0 collective-permute-done.refs_1_
  8.7 0.1 shard_map.50.after_ref
  8.8 2.6 %collective-permute-start.1 = (f32[136,1024]{1,0:T(8,128)S(1)}, f32[136,1024]{1,0:T(8,128)S(1)}, u32[]{:S(2)}, u32[]{:S(2)}) collective-permute-start(f32[136,1024]{1,0:T(8,128)S(1)} %shard_map.50.after_ref), channel_id=1, source_target_pairs={{0,8},{1,17},{2,10},{3,19},{4,12},{5,21},{6,14},{7,23},{8,0},{9,25... | collective-permute-start | bytes 1671176 | tf_op jit(solution)/shard_map/ppermute | solution.py:213
  11.4 2.2 %shard_map.52 = (f32[128,1024]{1,0:T(8,128)S(1)}, f32[64,1024]{1,0:T(8,128)S(1)}, f32[64,1024]{1,0:T(8,128)S(1)}, f32[128,1024]{1,0:T(8,128)S(1)}, f32[128,1024]...) custom-call(s32[1]{0:T(128)} %bitcast.me_ref, bf16[4096,1024]{1,0:T(8,128)(2,1)S(1)} %get-tuple-element.19.x_ref, ...), custom_call_target="tpu_custom_call" | custom-call | flops 1610612736 | bytes 8388608 | tf_op jit(solution)/shard_map/pallas_call | solution.py:284
  13.6 0.1 collective-permute-start.3
  13.7 0.4 %collective-permute-start.4 = (f32[64,1024]{1,0:T(8,128)S(1)}, f32[64,1024]{1,0:T(8,128)S(1)}, u32[]{:S(2)}, u32[]{:S(2)}) collective-permute-start(f32[64,1024]{1,0:T(8,128)S(1)} %get-tuple-element.25), channel_id=1, source_target_pairs={{0,1},{1,0},{2,3},{3,2},{4,5},{5,4},{6,7},{7,6},{8,9},{9,8},{10,11... | collective-permute-start | bytes 786440 | tf_op jit(solution)/shard_map/ppermute | solution.py:213
  14.2 0.1 collective-permute-start.7
  14.2 0.9 %collective-permute-done.3.refs_1_ = f32[64,1024]{1,0:T(8,128)S(1)} collective-permute-done((f32[64,1024]{1,0:T(8,128)S(1)}, f32[64,1024]{1,0:T(8,128)S(1)}, u32[]{:S(2)}, u32[]{:S(2)}) %collective-permute-start.3) | collective-permute-done | bytes 262176 | tf_op jit(solution)/shard_map/ppermute | solution.py:213
  15.2 0.4 collective-permute-done.4.refs_2_
  15.6 1.1 %collective-permute-start.5 = (f32[128,512]{1,0:T(8,128)S(1)}, f32[128,512]{1,0:T(8,128)S(1)}, u32[]{:S(2)}, u32[]{:S(2)}) collective-permute-start(f32[128,512]{1,0:T(8,128)S(1)} %shard_map.53), channel_id=1, source_target_pairs={{0,8},{1,17},{2,10},{3,19},{4,12},{5,21},{6,14},{7,23},{8,0},{9,25... | collective-permute-start | bytes 786440 | tf_op jit(solution)/shard_map/ppermute | solution.py:213
  16.7 0.0 collective-permute-start.2
  16.8 1.0 %collective-permute-start.6 = (f32[128,512]{1,0:T(8,128)S(1)}, f32[128,512]{1,0:T(8,128)S(1)}, u32[]{:S(2)}, u32[]{:S(2)}) collective-permute-start(f32[128,512]{1,0:T(8,128)S(1)} %shard_map.54), channel_id=1, source_target_pairs={{0,8},{1,17},{2,10},{3,19},{4,12},{5,21},{6,14},{7,23},{8,0},{9,25... | collective-permute-start | bytes 786440 | tf_op jit(solution)/shard_map/ppermute | solution.py:213
  17.8 0.0 collective-permute-done.7.refs_4_.refs_2_
  17.8 4.2 %collective-permute-done.5.refs_5_ = f32[128,512]{1,0:T(8,128)S(1)} collective-permute-done((f32[128,512]{1,0:T(8,128)S(1)}, f32[128,512]{1,0:T(8,128)S(1)}, u32[]{:S(2)}, u32[]{:S(2)}) %collective-permute-start.5) | collective-permute-done | bytes 262176 | tf_op jit(solution)/shard_map/ppermute | solution.py:213
  22.0 0.0 collective-permute-done.1.refs_2_.refs_0_
  22.1 1.7 %collective-permute-start.8 = (f32[136,512]{1,0:T(8,128)S(1)}, f32[136,512]{1,0:T(8,128)S(1)}, u32[]{:S(2)}, u32[]{:S(2)}) collective-permute-start(f32[136,512]{1,0:T(8,128)S(1)} %shard_map.55), channel_id=1, source_target_pairs={{0,16},{1,9},{2,18},{3,11},{4,20},{5,13},{6,22},{7,15},{8,24},{9,1... | collective-permute-start | bytes 835592 | tf_op jit(solution)/shard_map/ppermute | solution.py:213
  23.8 1.5 %collective-permute-done.6.refs_3_.refs_2_.refs_6_ = f32[128,512]{1,0:T(8,128)S(1)} collective-permute-done((f32[128,512]{1,0:T(8,128)S(1)}, f32[128,512]{1,0:T(8,128)S(1)}, u32[]{:S(2)}, u32[]{:S(2)}) %collective-permute-start.6) | collective-permute-done | bytes 262176 | tf_op jit(solution)/shard_map/ppermute | solution.py:213
  25.3 1.6 %collective-permute-start.9 = (f32[128,512]{1,0:T(8,128)S(1)}, f32[128,512]{1,0:T(8,128)S(1)}, u32[]{:S(2)}, u32[]{:S(2)}) collective-permute-start(f32[128,512]{1,0:T(8,128)S(1)} %shard_map.56), channel_id=1, source_target_pairs={{0,16},{1,9},{2,18},{3,11},{4,20},{5,13},{6,22},{7,15},{8,24},{9,1... | collective-permute-start | bytes 786440 | tf_op jit(solution)/shard_map/ppermute | solution.py:213
  27.0 0.0 collective-permute-done.2.refs_4_.refs_1_
  27.0 1.7 %collective-permute-done.8.refs_6_.refs_7_ = f32[136,512]{1,0:T(8,128)S(1)} collective-permute-done((f32[136,512]{1,0:T(8,128)S(1)}, f32[136,512]{1,0:T(8,128)S(1)}, u32[]{:S(2)}, u32[]{:S(2)}) %collective-permute-start.8) | collective-permute-done | bytes 278560 | tf_op jit(solution)/shard_map/ppermute | solution.py:213
  28.7 1.9 %collective-permute-start.10 = (f32[72,512]{1,0:T(8,128)S(1)}, f32[72,512]{1,0:T(8,128)S(1)}, u32[]{:S(2)}, u32[]{:S(2)}) collective-permute-start(f32[72,512]{1,0:T(8,128)S(1)} %shard_map.57), channel_id=1, source_target_pairs={{0,2},{1,5},{2,0},{3,7},{4,6},{5,1},{6,4},{7,3},{8,10},{9,13},{10,... | collective-permute-start | bytes 442376 | tf_op jit(solution)/shard_map/ppermute | solution.py:213
  30.6 1.2 %collective-permute-done.9.refs_3_.refs_8_ = f32[128,512]{1,0:T(8,128)S(1)} collective-permute-done((f32[128,512]{1,0:T(8,128)S(1)}, f32[128,512]{1,0:T(8,128)S(1)}, u32[]{:S(2)}, u32[]{:S(2)}) %collective-permute-start.9) | collective-permute-done | bytes 262176 | tf_op jit(solution)/shard_map/ppermute | solution.py:213
  31.8 1.8 %collective-permute-start.11 = (f32[64,512]{1,0:T(8,128)S(1)}, f32[64,512]{1,0:T(8,128)S(1)}, u32[]{:S(2)}, u32[]{:S(2)}) collective-permute-start(f32[64,512]{1,0:T(8,128)S(1)} %shard_map.58), channel_id=1, source_target_pairs={{0,2},{1,5},{2,0},{3,7},{4,6},{5,1},{6,4},{7,3},{8,10},{9,13},{10,... | collective-permute-start | bytes 393224 | tf_op jit(solution)/shard_map/ppermute | solution.py:213
  33.6 0.8 %collective-permute-done.10.refs_7_.refs_9_ = f32[72,512]{1,0:T(8,128)S(1)} collective-permute-done((f32[72,512]{1,0:T(8,128)S(1)}, f32[72,512]{1,0:T(8,128)S(1)}, u32[]{:S(2)}, u32[]{:S(2)}) %collective-permute-start.10) | collective-permute-done | bytes 147488 | tf_op jit(solution)/shard_map/ppermute | solution.py:213
  34.5 3.0 %collective-permute-start.12 = (f32[40,512]{1,0:T(8,128)S(1)}, f32[40,512]{1,0:T(8,128)S(1)}, u32[]{:S(2)}, u32[]{:S(2)}) collective-permute-start(f32[40,512]{1,0:T(8,128)S(1)} %shard_map.59), channel_id=1, source_target_pairs={{0,4},{1,3},{2,6},{3,1},{4,0},{5,7},{6,2},{7,5},{8,12},{9,11},{10,... | collective-permute-start | bytes 245768 | tf_op jit(solution)/shard_map/ppermute | solution.py:213
  37.5 0.4 collective-permute-done.11.refs_4_.refs_10_
  37.9 3.0 %collective-permute-start.13 = (f32[32,512]{1,0:T(8,128)S(1)}, f32[32,512]{1,0:T(8,128)S(1)}, u32[]{:S(2)}, u32[]{:S(2)}) collective-permute-start(f32[32,512]{1,0:T(8,128)S(1)} %shard_map.60), channel_id=1, source_target_pairs={{0,4},{1,3},{2,6},{3,1},{4,0},{5,7},{6,2},{7,5},{8,12},{9,11},{10,... | collective-permute-start | bytes 196616 | tf_op jit(solution)/shard_map/ppermute | solution.py:213
  40.9 2.2 %collective-permute-done.13.refs_12_ = f32[32,512]{1,0:T(8,128)S(1)} collective-permute-done((f32[32,512]{1,0:T(8,128)S(1)}, f32[32,512]{1,0:T(8,128)S(1)}, u32[]{:S(2)}, u32[]{:S(2)}) %collective-permute-start.13) | collective-permute-done | bytes 65568 | tf_op jit(solution)/shard_map/ppermute | solution.py:213
  43.1 0.0 collective-permute-done.12.refs_11_
  43.1 0.8 %shard_map.61 = (f32[32,1024]{1,0:T(8,128)}, f32[1,1024]{1,0:T(1,128)}, f32[1,1]{1,0:T(1,128)}) custom-call(s32[1]{0:T(128)} %bitcast.me_ref, f32[136,1024]{1,0:T(8,128)S(1)} %get-tuple-element.17.refs_0_, f32[136,1024]{1,0:T(8,128)S(1)} %collective-permute-done.refs_1_, f32[136,1024]{1,0:T(8,128)S(1)} %collective-permute-done.1.refs_2_.refs_0_, ...), custom_call_target="tpu_custom_call" | custom-call | flops 1 | bytes 1 | tf_op jit(solution)/shard_map/pallas_call | solution.py:323
  (8 shorter events, 0.2 us)
Async XLA Ops:
  0.6 0.7 %copy-start = (s32[1,2]{1,0:T(1,128)S(1)}, s32[1,2]{1,0:T(1,128)}, u32[]{:S(2)}) copy-start(s32[1,2]{1,0:T(1,128)} %len_hbm.1) | copy-start | bytes 28
  6.3 2.4 %collective-permute-start = (f32[136,1024]{1,0:T(8,128)S(1)}, f32[136,1024]{1,0:T(8,128)S(1)}, u32[]{:S(2)}, u32[]{:S(2)}) collective-permute-start(f32[136,1024]{1,0:T(8,128)S(1)} %get-tuple-element.18), channel_id=1, source_target_pairs={{0,1},{1,0},{2,3},{3,2},{4,5},{5,4},{6,7},{7,6},{8,9},{9,8},{10,11... | collective-permute-start | bytes 1671176 | tf_op jit(solution)/shard_map/ppermute | solution.py:213
  8.8 13.2 %collective-permute-start.1 = (f32[136,1024]{1,0:T(8,128)S(1)}, f32[136,1024]{1,0:T(8,128)S(1)}, u32[]{:S(2)}, u32[]{:S(2)}) collective-permute-start(f32[136,1024]{1,0:T(8,128)S(1)} %shard_map.50.after_ref), channel_id=1, source_target_pairs={{0,8},{1,17},{2,10},{3,19},{4,12},{5,21},{6,14},{7,23},{8,0},{9,25... | collective-permute-start | bytes 1671176 | tf_op jit(solution)/shard_map/ppermute | solution.py:213
  13.6 1.6 %collective-permute-start.3 = (f32[64,1024]{1,0:T(8,128)S(1)}, f32[64,1024]{1,0:T(8,128)S(1)}, u32[]{:S(2)}, u32[]{:S(2)}) collective-permute-start(f32[64,1024]{1,0:T(8,128)S(1)} %get-tuple-element.24), channel_id=1, source_target_pairs={{0,1},{1,0},{2,3},{3,2},{4,5},{5,4},{6,7},{7,6},{8,9},{9,8},{10,11... | collective-permute-start | bytes 786440 | tf_op jit(solution)/shard_map/ppermute | solution.py:213
  13.7 1.8 %collective-permute-start.4 = (f32[64,1024]{1,0:T(8,128)S(1)}, f32[64,1024]{1,0:T(8,128)S(1)}, u32[]{:S(2)}, u32[]{:S(2)}) collective-permute-start(f32[64,1024]{1,0:T(8,128)S(1)} %get-tuple-element.25), channel_id=1, source_target_pairs={{0,1},{1,0},{2,3},{3,2},{4,5},{5,4},{6,7},{7,6},{8,9},{9,8},{10,11... | collective-permute-start | bytes 786440 | tf_op jit(solution)/shard_map/ppermute | solution.py:213
  14.2 3.6 %collective-permute-start.7 = (f32[128,1024]{1,0:T(8,128)S(1)}, f32[128,1024]{1,0:T(8,128)S(1)}, u32[]{:S(2)}, u32[]{:S(2)}) collective-permute-start(f32[128,1024]{1,0:T(8,128)S(1)} %get-tuple-element.27), channel_id=1, source_target_pairs={{0,1},{1,0},{2,3},{3,2},{4,5},{5,4},{6,7},{7,6},{8,9},{9,8},{10,11... | collective-permute-start | bytes 1572872 | tf_op jit(solution)/shard_map/ppermute | solution.py:213
  15.6 6.4 %collective-permute-start.5 = (f32[128,512]{1,0:T(8,128)S(1)}, f32[128,512]{1,0:T(8,128)S(1)}, u32[]{:S(2)}, u32[]{:S(2)}) collective-permute-start(f32[128,512]{1,0:T(8,128)S(1)} %shard_map.53), channel_id=1, source_target_pairs={{0,8},{1,17},{2,10},{3,19},{4,12},{5,21},{6,14},{7,23},{8,0},{9,25... | collective-permute-start | bytes 786440 | tf_op jit(solution)/shard_map/ppermute | solution.py:213
  16.7 10.3 %collective-permute-start.2 = (f32[128,1024]{1,0:T(8,128)S(1)}, f32[128,1024]{1,0:T(8,128)S(1)}, u32[]{:S(2)}, u32[]{:S(2)}) collective-permute-start(f32[128,1024]{1,0:T(8,128)S(1)} %get-tuple-element.22), channel_id=1, source_target_pairs={{0,1},{1,0},{2,3},{3,2},{4,5},{5,4},{6,7},{7,6},{8,9},{9,8},{10,11... | collective-permute-start | bytes 1572872 | tf_op jit(solution)/shard_map/ppermute | solution.py:213
  16.8 8.5 %collective-permute-start.6 = (f32[128,512]{1,0:T(8,128)S(1)}, f32[128,512]{1,0:T(8,128)S(1)}, u32[]{:S(2)}, u32[]{:S(2)}) collective-permute-start(f32[128,512]{1,0:T(8,128)S(1)} %shard_map.54), channel_id=1, source_target_pairs={{0,8},{1,17},{2,10},{3,19},{4,12},{5,21},{6,14},{7,23},{8,0},{9,25... | collective-permute-start | bytes 786440 | tf_op jit(solution)/shard_map/ppermute | solution.py:213
  22.1 6.6 %collective-permute-start.8 = (f32[136,512]{1,0:T(8,128)S(1)}, f32[136,512]{1,0:T(8,128)S(1)}, u32[]{:S(2)}, u32[]{:S(2)}) collective-permute-start(f32[136,512]{1,0:T(8,128)S(1)} %shard_map.55), channel_id=1, source_target_pairs={{0,16},{1,9},{2,18},{3,11},{4,20},{5,13},{6,22},{7,15},{8,24},{9,1... | collective-permute-start | bytes 835592 | tf_op jit(solution)/shard_map/ppermute | solution.py:213
  25.3 6.4 %collective-permute-start.9 = (f32[128,512]{1,0:T(8,128)S(1)}, f32[128,512]{1,0:T(8,128)S(1)}, u32[]{:S(2)}, u32[]{:S(2)}) collective-permute-start(f32[128,512]{1,0:T(8,128)S(1)} %shard_map.56), channel_id=1, source_target_pairs={{0,16},{1,9},{2,18},{3,11},{4,20},{5,13},{6,22},{7,15},{8,24},{9,1... | collective-permute-start | bytes 786440 | tf_op jit(solution)/shard_map/ppermute | solution.py:213
  28.7 5.7 %collective-permute-start.10 = (f32[72,512]{1,0:T(8,128)S(1)}, f32[72,512]{1,0:T(8,128)S(1)}, u32[]{:S(2)}, u32[]{:S(2)}) collective-permute-start(f32[72,512]{1,0:T(8,128)S(1)} %shard_map.57), channel_id=1, source_target_pairs={{0,2},{1,5},{2,0},{3,7},{4,6},{5,1},{6,4},{7,3},{8,10},{9,13},{10,... | collective-permute-start | bytes 442376 | tf_op jit(solution)/shard_map/ppermute | solution.py:213
  31.8 6.0 %collective-permute-start.11 = (f32[64,512]{1,0:T(8,128)S(1)}, f32[64,512]{1,0:T(8,128)S(1)}, u32[]{:S(2)}, u32[]{:S(2)}) collective-permute-start(f32[64,512]{1,0:T(8,128)S(1)} %shard_map.58), channel_id=1, source_target_pairs={{0,2},{1,5},{2,0},{3,7},{4,6},{5,1},{6,4},{7,3},{8,10},{9,13},{10,... | collective-permute-start | bytes 393224 | tf_op jit(solution)/shard_map/ppermute | solution.py:213
  34.5 8.7 %collective-permute-start.12 = (f32[40,512]{1,0:T(8,128)S(1)}, f32[40,512]{1,0:T(8,128)S(1)}, u32[]{:S(2)}, u32[]{:S(2)}) collective-permute-start(f32[40,512]{1,0:T(8,128)S(1)} %shard_map.59), channel_id=1, source_target_pairs={{0,4},{1,3},{2,6},{3,1},{4,0},{5,7},{6,2},{7,5},{8,12},{9,11},{10,... | collective-permute-start | bytes 245768 | tf_op jit(solution)/shard_map/ppermute | solution.py:213
  37.9 5.3 %collective-permute-start.13 = (f32[32,512]{1,0:T(8,128)S(1)}, f32[32,512]{1,0:T(8,128)S(1)}, u32[]{:S(2)}, u32[]{:S(2)}) collective-permute-start(f32[32,512]{1,0:T(8,128)S(1)} %shard_map.60), channel_id=1, source_target_pairs={{0,4},{1,3},{2,6},{3,1},{4,0},{5,7},{6,2},{7,5},{8,12},{9,11},{10,... | collective-permute-start | bytes 196616 | tf_op jit(solution)/shard_map/ppermute | solution.py:213

commit v5 on v4

--- a/solution.py
+++ b/solution.py
@@ -16,11 +16,7 @@
 
 
 def member_masks(members):
-    near = [1 << bit for bit in range(1, members.bit_length() - 1)]
-    far = list(near)
-    for i in range(0, len(far) - 1, 2):
-        far[i], far[i + 1] = far[i + 1], far[i]
-    return near, far
+    return [1 << bit for bit in range(1, members.bit_length() - 1)]
 
 
 def member_order(masks):
@@ -46,14 +42,13 @@
     group, member = me // members, me % members
     core = me % 2
     block = members * rows
-    orders = [member_order(masks) for masks in member_masks(members)]
+    order = member_order(member_masks(members))
     for out, other in zip(outs, (0, 1)):
         owner = core ^ other
         for c, chunk in enumerate(chunks):
-            for i, (even, odd) in enumerate(zip(*orders)):
-                relative = jnp.where(owner == 0, even, odd)
-                start = ((member ^ other) ^ relative) * rows
-                place = (c * len(orders[0]) + i) * rows
+            for i, relative in enumerate(order):
+                start = (member ^ other ^ relative) * rows
+                place = (c * len(order) + i) * rows
                 target = out
                 if isinstance(out, tuple):
                     target = out[place // out[0].shape[0]]
@@ -205,8 +200,8 @@
     devices = groups * members
     keys = (3, 1, 2, 0)
     assert groups == len(keys)
-    near, far = member_masks(members)
-    steps = [(members, 2 * members), (2 * members, members), *zip(near, far)]
+    steps = [(members, 2 * members), (2 * members, members)]
+    steps += [(mask, mask) for mask in member_masks(members)]
 
     def swap(value, masks):
         pairs = [(i, i ^ masks[i % 2]) for i in range(devices)]
@@ -295,14 +290,13 @@
         last, last_in = put(mine_last), put(swap(theirs_last, (1, 1)))
         extra.append((one_next, half))
         both = [(half // 2, [(two, i * half // 2), (other, 0)]) for i, other in enumerate(two_in)]
-        two_next = [
-            put(swap(total(both, *columns), steps[0]), False) for columns in ranges
-        ]
+        two_sent = [put(total(both, *columns), False) for columns in ranges]
+        two_next = [put(swap(arrays[i], steps[0]), False) for i in two_sent]
         chains = []
         for (start, size), two_out in zip(ranges, two_next):
             carried = [] if start else [(EXTRA, extra)]
             message = total(
-                [(half, [(after, 0), (after_in, 0), (one_next, 0)])] + carried, start, size, [two_out]
+                [(half, [(after, 0), (after_in, 0), (one_next, 0)])] + carried, start, size, two_next[:1] if start else two_sent
             )
             added = put(swap(message, steps[1]), False)
             chains.append([(last, 0), (last_in, 0), (two_out, 0), (added, 0)])

time: 44 us -> 43.9 us (level)
  waiting for transfers between devices: 13.4 us -> 12 us
  starting transfers between devices: 18.9 us -> 20.2 us
    ppermute x14, waiting for transfers between devices: 13.4 us -> 12 us  [swap(): return lax.ppermute(value, axes, pairs)]
    ppermute x14, starting transfers between devices: 18.9 us -> 20.2 us  [swap(): return lax.ppermute(value, axes, pairs)]
where the time goes in v5:
time: 43.9 us; the launch traced here: 43.7 us
  starting transfers between devices  20.2 us (46%)
  waiting for transfers between devices  12 us (27%)
  Pallas kernels  10.2 us (23%)
  between operations  0.74 us (2%)
  local copies, waits for them, and re-layouts  0.65 us (1%)
    ppermute x14, starting transfers between devices, swap(): return lax.ppermute(value, axes, pairs)  20.2 us
    ppermute x14, waiting for transfers between devices, swap(): return lax.ppermute(value, axes, pairs)  12 us
    pallas_call x1, Pallas kernels, body(): pl.pallas_call(functools.partial(first_kernel, tile=tile, pack=pack, **si...  5.02 us
    pallas_call x1, Pallas kernels, body(): pl.pallas_call(functools.partial(third_kernel, **sizes), out_shape=[f32(h...  2.17 us
    pallas_call x1, Pallas kernels, body(): pl.pallas_call(functools.partial(second_kernel, block=block), out_shape=j...  1.88 us
  transfers between devices with their start and end apart: 14, of which 9 were waited for; matrix products, arithmetic and copies ran while one was open for 0% of the time, Pallas kernels for 10%

profile of v5, /device:TPU:0, one launch (start us, length us, event | category | flops | bytes accessed | tf_op | source)
XLA Modules:
  0.0 43.7 jit_solution(3965628628100154998)
XLA Ops:
  0.6 0.0 copy-start
  0.6 0.6 %copy-done = s32[1,2]{1,0:T(1,128)S(1)} copy-done((s32[1,2]{1,0:T(1,128)S(1)}, s32[1,2]{1,0:T(1,128)}, u32[]{:S(2)}) %copy-start) | copy-done | bytes 32
  1.3 5.0 %shard_map.49 = (f32[136,1024]{1,0:T(8,128)S(1)}, f32[136,1024]{1,0:T(8,128)S(1)}, bf16[4096,1024]{1,0:T(8,128)(2,1)S(1)}, f32[256,1024]{1,0:T(8,128)S(1)}) custom-call(s32[1]{0:T(128)} %bitcast.me_ref, s32[1,2]{1,0:T(1,128)S(1)} %copy-done, bf16[4096,1024]{1,0:T(8,128)(2,1)} %x_hbm.1), custom_call_target="tpu_custom_call" | custom-call | flops 2147483648 | bytes 8388608 | tf_op jit(solution)/shard_map/pallas_call | solution.py:231
  6.3 0.5 %collective-permute-start = (f32[136,1024]{1,0:T(8,128)S(1)}, f32[136,1024]{1,0:T(8,128)S(1)}, u32[]{:S(2)}, u32[]{:S(2)}) collective-permute-start(f32[136,1024]{1,0:T(8,128)S(1)} %get-tuple-element.18), channel_id=1, source_target_pairs={{0,1},{1,0},{2,3},{3,2},{4,5},{5,4},{6,7},{7,6},{8,9},{9,8},{10,11... | collective-permute-start | bytes 1671176 | tf_op jit(solution)/shard_map/ppermute | solution.py:208
  6.8 1.9 %shard_map.51.second_ref = f32[256,768]{1,0:T(8,128)S(1)} custom-call(bf16[4096,1024]{1,0:T(8,128)(2,1)S(1)} %get-tuple-element.19.x_ref), custom_call_target="tpu_custom_call" | custom-call | flops 1610612736 | bytes 8388608 | tf_op jit(solution)/shard_map/pallas_call | solution.py:246
  8.7 0.0 collective-permute-done.refs_1_
  8.7 0.1 shard_map.50.after_ref
  8.8 2.6 %collective-permute-start.1 = (f32[136,1024]{1,0:T(8,128)S(1)}, f32[136,1024]{1,0:T(8,128)S(1)}, u32[]{:S(2)}, u32[]{:S(2)}) collective-permute-start(f32[136,1024]{1,0:T(8,128)S(1)} %shard_map.50.after_ref), channel_id=1, source_target_pairs={{0,8},{1,17},{2,10},{3,19},{4,12},{5,21},{6,14},{7,23},{8,0},{9,25... | collective-permute-start | bytes 1671176 | tf_op jit(solution)/shard_map/ppermute | solution.py:208
  11.4 2.2 %shard_map.52 = (f32[128,1024]{1,0:T(8,128)S(1)}, f32[64,1024]{1,0:T(8,128)S(1)}, f32[64,1024]{1,0:T(8,128)S(1)}, f32[128,1024]{1,0:T(8,128)S(1)}, f32[128,1024]...) custom-call(s32[1]{0:T(128)} %bitcast.me_ref, bf16[4096,1024]{1,0:T(8,128)(2,1)S(1)} %get-tuple-element.19.x_ref, ...), custom_call_target="tpu_custom_call" | custom-call | flops 1610612736 | bytes 8388608 | tf_op jit(solution)/shard_map/pallas_call | solution.py:279
  13.6 0.1 collective-permute-start.7
  13.7 0.5 %collective-permute-start.3 = (f32[64,1024]{1,0:T(8,128)S(1)}, f32[64,1024]{1,0:T(8,128)S(1)}, u32[]{:S(2)}, u32[]{:S(2)}) collective-permute-start(f32[64,1024]{1,0:T(8,128)S(1)} %get-tuple-element.24), channel_id=1, source_target_pairs={{0,1},{1,0},{2,3},{3,2},{4,5},{5,4},{6,7},{7,6},{8,9},{9,8},{10,11... | collective-permute-start | bytes 786440 | tf_op jit(solution)/shard_map/ppermute | solution.py:208
  14.2 0.1 collective-permute-start.4
  14.2 0.4 collective-permute-start.2
  14.7 1.3 %collective-permute-done.3.refs_1_ = f32[64,1024]{1,0:T(8,128)S(1)} collective-permute-done((f32[64,1024]{1,0:T(8,128)S(1)}, f32[64,1024]{1,0:T(8,128)S(1)}, u32[]{:S(2)}, u32[]{:S(2)}) %collective-permute-start.3) | collective-permute-done | bytes 262176 | tf_op jit(solution)/shard_map/ppermute | solution.py:208
  15.9 0.4 collective-permute-done.4.refs_2_
  16.4 1.2 %collective-permute-start.5 = (f32[128,512]{1,0:T(8,128)S(1)}, f32[128,512]{1,0:T(8,128)S(1)}, u32[]{:S(2)}, u32[]{:S(2)}) collective-permute-start(f32[128,512]{1,0:T(8,128)S(1)} %shard_map.53.refs_5_), channel_id=1, source_target_pairs={{0,8},{1,17},{2,10},{3,19},{4,12},{5,21},{6,14},{7,23},{8,0},{9,25... | collective-permute-start | bytes 786440 | tf_op jit(solution)/shard_map/ppermute | solution.py:208
  17.6 0.0 collective-permute-done.7.refs_4_.refs_2_
  17.6 1.3 %collective-permute-done.1.refs_2_.refs_0_ = f32[136,1024]{1,0:T(8,128)S(1)} collective-permute-done((f32[136,1024]{1,0:T(8,128)S(1)}, f32[136,1024]{1,0:T(8,128)S(1)}, u32[]{:S(2)}, u32[]{:S(2)}) %collective-permute-start.1) | collective-permute-done | bytes 557088 | tf_op jit(solution)/shard_map/ppermute | solution.py:208
  19.0 1.8 %collective-permute-start.8 = (f32[136,512]{1,0:T(8,128)S(1)}, f32[136,512]{1,0:T(8,128)S(1)}, u32[]{:S(2)}, u32[]{:S(2)}) collective-permute-start(f32[136,512]{1,0:T(8,128)S(1)} %shard_map.55), channel_id=1, source_target_pairs={{0,16},{1,9},{2,18},{3,11},{4,20},{5,13},{6,22},{7,15},{8,24},{9,1... | collective-permute-start | bytes 835592 | tf_op jit(solution)/shard_map/ppermute | solution.py:208
  20.8 1.6 %collective-permute-start.6 = (f32[128,512]{1,0:T(8,128)S(1)}, f32[128,512]{1,0:T(8,128)S(1)}, u32[]{:S(2)}, u32[]{:S(2)}) collective-permute-start(f32[128,512]{1,0:T(8,128)S(1)} %shard_map.54.refs_6_), channel_id=1, source_target_pairs={{0,8},{1,17},{2,10},{3,19},{4,12},{5,21},{6,14},{7,23},{8,0},{9,25... | collective-permute-start | bytes 786440 | tf_op jit(solution)/shard_map/ppermute | solution.py:208
  22.4 1.6 %collective-permute-done.5.refs_3_.refs_5_ = f32[128,512]{1,0:T(8,128)S(1)} collective-permute-done((f32[128,512]{1,0:T(8,128)S(1)}, f32[128,512]{1,0:T(8,128)S(1)}, u32[]{:S(2)}, u32[]{:S(2)}) %collective-permute-start.5) | collective-permute-done | bytes 262176 | tf_op jit(solution)/shard_map/ppermute | solution.py:208
  24.0 1.3 %collective-permute-start.9 = (f32[128,512]{1,0:T(8,128)S(1)}, f32[128,512]{1,0:T(8,128)S(1)}, u32[]{:S(2)}, u32[]{:S(2)}) collective-permute-start(f32[128,512]{1,0:T(8,128)S(1)} %shard_map.56), channel_id=1, source_target_pairs={{0,16},{1,9},{2,18},{3,11},{4,20},{5,13},{6,22},{7,15},{8,24},{9,1... | collective-permute-start | bytes 786440 | tf_op jit(solution)/shard_map/ppermute | solution.py:208
  25.4 0.0 collective-permute-done.2.refs_4_.refs_1_
  25.4 2.9 %collective-permute-done.8.refs_6_.refs_7_ = f32[136,512]{1,0:T(8,128)S(1)} collective-permute-done((f32[136,512]{1,0:T(8,128)S(1)}, f32[136,512]{1,0:T(8,128)S(1)}, u32[]{:S(2)}, u32[]{:S(2)}) %collective-permute-start.8) | collective-permute-done | bytes 278560 | tf_op jit(solution)/shard_map/ppermute | solution.py:208
  28.3 2.1 %collective-permute-start.10 = (f32[72,512]{1,0:T(8,128)S(1)}, f32[72,512]{1,0:T(8,128)S(1)}, u32[]{:S(2)}, u32[]{:S(2)}) collective-permute-start(f32[72,512]{1,0:T(8,128)S(1)} %shard_map.57), channel_id=1, source_target_pairs={{0,2},{1,3},{2,0},{3,1},{4,6},{5,7},{6,4},{7,5},{8,10},{9,11},{10,... | collective-permute-start | bytes 442376 | tf_op jit(solution)/shard_map/ppermute | solution.py:208
  30.4 0.0 collective-permute-done.6.refs_2_.refs_6_
  30.4 0.7 %collective-permute-done.9.refs_3_.refs_8_ = f32[128,512]{1,0:T(8,128)S(1)} collective-permute-done((f32[128,512]{1,0:T(8,128)S(1)}, f32[128,512]{1,0:T(8,128)S(1)}, u32[]{:S(2)}, u32[]{:S(2)}) %collective-permute-start.9) | collective-permute-done | bytes 262176 | tf_op jit(solution)/shard_map/ppermute | solution.py:208
  31.2 2.0 %collective-permute-start.11 = (f32[64,512]{1,0:T(8,128)S(1)}, f32[64,512]{1,0:T(8,128)S(1)}, u32[]{:S(2)}, u32[]{:S(2)}) collective-permute-start(f32[64,512]{1,0:T(8,128)S(1)} %shard_map.58), channel_id=1, source_target_pairs={{0,2},{1,3},{2,0},{3,1},{4,6},{5,7},{6,4},{7,5},{8,10},{9,11},{10,... | collective-permute-start | bytes 393224 | tf_op jit(solution)/shard_map/ppermute | solution.py:208
  33.3 0.3 collective-permute-done.10.refs_7_.refs_9_
  33.6 3.1 %collective-permute-start.12 = (f32[40,512]{1,0:T(8,128)S(1)}, f32[40,512]{1,0:T(8,128)S(1)}, u32[]{:S(2)}, u32[]{:S(2)}) collective-permute-start(f32[40,512]{1,0:T(8,128)S(1)} %shard_map.59), channel_id=1, source_target_pairs={{0,4},{1,5},{2,6},{3,7},{4,0},{5,1},{6,2},{7,3},{8,12},{9,13},{10,... | collective-permute-start | bytes 245768 | tf_op jit(solution)/shard_map/ppermute | solution.py:208
  36.7 1.0 %collective-permute-done.11.refs_4_.refs_10_ = f32[64,512]{1,0:T(8,128)S(1)} collective-permute-done((f32[64,512]{1,0:T(8,128)S(1)}, f32[64,512]{1,0:T(8,128)S(1)}, u32[]{:S(2)}, u32[]{:S(2)}) %collective-permute-start.11) | collective-permute-done | bytes 131104 | tf_op jit(solution)/shard_map/ppermute | solution.py:208
  37.7 2.8 %collective-permute-start.13 = (f32[32,512]{1,0:T(8,128)S(1)}, f32[32,512]{1,0:T(8,128)S(1)}, u32[]{:S(2)}, u32[]{:S(2)}) collective-permute-start(f32[32,512]{1,0:T(8,128)S(1)} %shard_map.60), channel_id=1, source_target_pairs={{0,4},{1,5},{2,6},{3,7},{4,0},{5,1},{6,2},{7,3},{8,12},{9,13},{10,... | collective-permute-start | bytes 196616 | tf_op jit(solution)/shard_map/ppermute | solution.py:208
  40.5 2.4 %collective-permute-done.13.refs_12_ = f32[32,512]{1,0:T(8,128)S(1)} collective-permute-done((f32[32,512]{1,0:T(8,128)S(1)}, f32[32,512]{1,0:T(8,128)S(1)}, u32[]{:S(2)}, u32[]{:S(2)}) %collective-permute-start.13) | collective-permute-done | bytes 65568 | tf_op jit(solution)/shard_map/ppermute | solution.py:208
  43.0 0.0 collective-permute-done.12.refs_11_
  43.0 0.8 %shard_map.61 = (f32[32,1024]{1,0:T(8,128)}, f32[1,1024]{1,0:T(1,128)}, f32[1,1]{1,0:T(1,128)}) custom-call(s32[1]{0:T(128)} %bitcast.me_ref, f32[136,1024]{1,0:T(8,128)S(1)} %get-tuple-element.17.refs_0_, f32[136,1024]{1,0:T(8,128)S(1)} %collective-permute-done.refs_1_, f32[136,1024]{1,0:T(8,128)S(1)} %collective-permute-done.1.refs_2_.refs_0_, ...), custom_call_target="tpu_custom_call" | custom-call | flops 1 | bytes 1 | tf_op jit(solution)/shard_map/pallas_call | solution.py:317
  (8 shorter events, 0.2 us)
Async XLA Ops:
  0.6 0.7 %copy-start = (s32[1,2]{1,0:T(1,128)S(1)}, s32[1,2]{1,0:T(1,128)}, u32[]{:S(2)}) copy-start(s32[1,2]{1,0:T(1,128)} %len_hbm.1) | copy-start | bytes 28
  6.3 2.4 %collective-permute-start = (f32[136,1024]{1,0:T(8,128)S(1)}, f32[136,1024]{1,0:T(8,128)S(1)}, u32[]{:S(2)}, u32[]{:S(2)}) collective-permute-start(f32[136,1024]{1,0:T(8,128)S(1)} %get-tuple-element.18), channel_id=1, source_target_pairs={{0,1},{1,0},{2,3},{3,2},{4,5},{5,4},{6,7},{7,6},{8,9},{9,8},{10,11... | collective-permute-start | bytes 1671176 | tf_op jit(solution)/shard_map/ppermute | solution.py:208
  8.8 10.1 %collective-permute-start.1 = (f32[136,1024]{1,0:T(8,128)S(1)}, f32[136,1024]{1,0:T(8,128)S(1)}, u32[]{:S(2)}, u32[]{:S(2)}) collective-permute-start(f32[136,1024]{1,0:T(8,128)S(1)} %shard_map.50.after_ref), channel_id=1, source_target_pairs={{0,8},{1,17},{2,10},{3,19},{4,12},{5,21},{6,14},{7,23},{8,0},{9,25... | collective-permute-start | bytes 1671176 | tf_op jit(solution)/shard_map/ppermute | solution.py:208
  13.6 4.0 %collective-permute-start.7 = (f32[128,1024]{1,0:T(8,128)S(1)}, f32[128,1024]{1,0:T(8,128)S(1)}, u32[]{:S(2)}, u32[]{:S(2)}) collective-permute-start(f32[128,1024]{1,0:T(8,128)S(1)} %get-tuple-element.27), channel_id=1, source_target_pairs={{0,1},{1,0},{2,3},{3,2},{4,5},{5,4},{6,7},{7,6},{8,9},{9,8},{10,11... | collective-permute-start | bytes 1572872 | tf_op jit(solution)/shard_map/ppermute | solution.py:208
  13.7 2.3 %collective-permute-start.3 = (f32[64,1024]{1,0:T(8,128)S(1)}, f32[64,1024]{1,0:T(8,128)S(1)}, u32[]{:S(2)}, u32[]{:S(2)}) collective-permute-start(f32[64,1024]{1,0:T(8,128)S(1)} %get-tuple-element.24), channel_id=1, source_target_pairs={{0,1},{1,0},{2,3},{3,2},{4,5},{5,4},{6,7},{7,6},{8,9},{9,8},{10,11... | collective-permute-start | bytes 786440 | tf_op jit(solution)/shard_map/ppermute | solution.py:208
  14.2 2.1 %collective-permute-start.4 = (f32[64,1024]{1,0:T(8,128)S(1)}, f32[64,1024]{1,0:T(8,128)S(1)}, u32[]{:S(2)}, u32[]{:S(2)}) collective-permute-start(f32[64,1024]{1,0:T(8,128)S(1)} %get-tuple-element.25), channel_id=1, source_target_pairs={{0,1},{1,0},{2,3},{3,2},{4,5},{5,4},{6,7},{7,6},{8,9},{9,8},{10,11... | collective-permute-start | bytes 786440 | tf_op jit(solution)/shard_map/ppermute | solution.py:208
  14.2 11.1 %collective-permute-start.2 = (f32[128,1024]{1,0:T(8,128)S(1)}, f32[128,1024]{1,0:T(8,128)S(1)}, u32[]{:S(2)}, u32[]{:S(2)}) collective-permute-start(f32[128,1024]{1,0:T(8,128)S(1)} %get-tuple-element.22), channel_id=1, source_target_pairs={{0,1},{1,0},{2,3},{3,2},{4,5},{5,4},{6,7},{7,6},{8,9},{9,8},{10,11... | collective-permute-start | bytes 1572872 | tf_op jit(solution)/shard_map/ppermute | solution.py:208
  16.4 7.6 %collective-permute-start.5 = (f32[128,512]{1,0:T(8,128)S(1)}, f32[128,512]{1,0:T(8,128)S(1)}, u32[]{:S(2)}, u32[]{:S(2)}) collective-permute-start(f32[128,512]{1,0:T(8,128)S(1)} %shard_map.53.refs_5_), channel_id=1, source_target_pairs={{0,8},{1,17},{2,10},{3,19},{4,12},{5,21},{6,14},{7,23},{8,0},{9,25... | collective-permute-start | bytes 786440 | tf_op jit(solution)/shard_map/ppermute | solution.py:208
  19.0 9.3 %collective-permute-start.8 = (f32[136,512]{1,0:T(8,128)S(1)}, f32[136,512]{1,0:T(8,128)S(1)}, u32[]{:S(2)}, u32[]{:S(2)}) collective-permute-start(f32[136,512]{1,0:T(8,128)S(1)} %shard_map.55), channel_id=1, source_target_pairs={{0,16},{1,9},{2,18},{3,11},{4,20},{5,13},{6,22},{7,15},{8,24},{9,1... | collective-permute-start | bytes 835592 | tf_op jit(solution)/shard_map/ppermute | solution.py:208
  20.8 9.7 %collective-permute-start.6 = (f32[128,512]{1,0:T(8,128)S(1)}, f32[128,512]{1,0:T(8,128)S(1)}, u32[]{:S(2)}, u32[]{:S(2)}) collective-permute-start(f32[128,512]{1,0:T(8,128)S(1)} %shard_map.54.refs_6_), channel_id=1, source_target_pairs={{0,8},{1,17},{2,10},{3,19},{4,12},{5,21},{6,14},{7,23},{8,0},{9,25... | collective-permute-start | bytes 786440 | tf_op jit(solution)/shard_map/ppermute | solution.py:208
  24.0 7.2 %collective-permute-start.9 = (f32[128,512]{1,0:T(8,128)S(1)}, f32[128,512]{1,0:T(8,128)S(1)}, u32[]{:S(2)}, u32[]{:S(2)}) collective-permute-start(f32[128,512]{1,0:T(8,128)S(1)} %shard_map.56), channel_id=1, source_target_pairs={{0,16},{1,9},{2,18},{3,11},{4,20},{5,13},{6,22},{7,15},{8,24},{9,1... | collective-permute-start | bytes 786440 | tf_op jit(solution)/shard_map/ppermute | solution.py:208
  28.3 5.3 %collective-permute-start.10 = (f32[72,512]{1,0:T(8,128)S(1)}, f32[72,512]{1,0:T(8,128)S(1)}, u32[]{:S(2)}, u32[]{:S(2)}) collective-permute-start(f32[72,512]{1,0:T(8,128)S(1)} %shard_map.57), channel_id=1, source_target_pairs={{0,2},{1,3},{2,0},{3,1},{4,6},{5,7},{6,4},{7,5},{8,10},{9,11},{10,... | collective-permute-start | bytes 442376 | tf_op jit(solution)/shard_map/ppermute | solution.py:208
  31.2 6.5 %collective-permute-start.11 = (f32[64,512]{1,0:T(8,128)S(1)}, f32[64,512]{1,0:T(8,128)S(1)}, u32[]{:S(2)}, u32[]{:S(2)}) collective-permute-start(f32[64,512]{1,0:T(8,128)S(1)} %shard_map.58), channel_id=1, source_target_pairs={{0,2},{1,3},{2,0},{3,1},{4,6},{5,7},{6,4},{7,5},{8,10},{9,11},{10,... | collective-permute-start | bytes 393224 | tf_op jit(solution)/shard_map/ppermute | solution.py:208
  33.6 9.4 %collective-permute-start.12 = (f32[40,512]{1,0:T(8,128)S(1)}, f32[40,512]{1,0:T(8,128)S(1)}, u32[]{:S(2)}, u32[]{:S(2)}) collective-permute-start(f32[40,512]{1,0:T(8,128)S(1)} %shard_map.59), channel_id=1, source_target_pairs={{0,4},{1,5},{2,6},{3,7},{4,0},{5,1},{6,2},{7,3},{8,12},{9,13},{10,... | collective-permute-start | bytes 245768 | tf_op jit(solution)/shard_map/ppermute | solution.py:208
  37.7 5.2 %collective-permute-start.13 = (f32[32,512]{1,0:T(8,128)S(1)}, f32[32,512]{1,0:T(8,128)S(1)}, u32[]{:S(2)}, u32[]{:S(2)}) collective-permute-start(f32[32,512]{1,0:T(8,128)S(1)} %shard_map.60), channel_id=1, source_target_pairs={{0,4},{1,5},{2,6},{3,7},{4,0},{5,1},{6,2},{7,3},{8,12},{9,13},{10,... | collective-permute-start | bytes 196616 | tf_op jit(solution)/shard_map/ppermute | solution.py:208

commit v6 on v4

--- a/solution.py
+++ b/solution.py
@@ -42,17 +42,16 @@
     return pl.ds(pl.multiple_of((group ^ key) * block, block), block)
 
 
-def write_rows(outs, chunks, me, members, rows, keys):
+def write_rows(outs, chunks, me, members, rows, keys, pack):
     group, member = me // members, me % members
     core = me % 2
     block = members * rows
     orders = [member_order(masks) for masks in member_masks(members)]
     for out, other in zip(outs, (0, 1)):
         owner = core ^ other
+        lanes = [owner ^ ((group ^ key) * block // pack) for key in keys]
         for c, chunk in enumerate(chunks):
             for i, (even, odd) in enumerate(zip(*orders)):
-                relative = jnp.where(owner == 0, even, odd)
-                start = ((member ^ other) ^ relative) * rows
                 place = (c * len(orders[0]) + i) * rows
                 target = out
                 if isinstance(out, tuple):
@@ -60,6 +59,8 @@
                     place %= out[0].shape[0]
                 at = pl.ds(place, rows)
                 for n, key in enumerate(keys):
+                    relative = jnp.where(lanes[n] == 0, even, odd)
+                    start = ((member ^ other) ^ relative) * rows
                     ref, row, column = chunk(owner, n)
                     source = pl.ds(pl.multiple_of(row + start, rows), rows)
                     target[at, block_columns(group, key, block)] = ref[source, pl.ds(column, block)]
@@ -104,7 +105,7 @@
         else:
             acc_ref[...] = product
     write_rows(
-        (mine_ref, theirs_ref), [lambda owner, n: (acc_ref, 0, n * block)], me, members, rows, keys
+        (mine_ref, theirs_ref), [lambda owner, n: (acc_ref, 0, n * block)], me, members, rows, keys, pack
     )
     for n, key in enumerate(keys):
         sums_ref[0:1, block_columns(group, key, block)] = total[:, n * block:(n + 1) * block]
@@ -122,7 +123,7 @@
 
 def third_kernel(me_ref, x_ref, first_ref, second_ref, after_ref, mine_ref, theirs_ref,
                  theirs_later_ref, mine_next_ref, theirs_next_ref, mine_last_ref, theirs_last_ref, acc_ref,
-                 *, keys, members, rows):
+                 *, keys, members, rows, pack):
     block = members * rows
 
     def cut(n):
@@ -147,9 +148,9 @@
         return acc_ref, 2 * block, n * block
 
     me = me_ref[0]
-    write_rows((mine_ref, (theirs_ref, theirs_later_ref)), [step_one], me, members, rows, keys)
-    write_rows((mine_next_ref, theirs_next_ref), [step_two], me, members, rows, keys)
-    write_rows((mine_last_ref, theirs_last_ref), [kept], me, members, rows, keys)
+    write_rows((mine_ref, (theirs_ref, theirs_later_ref)), [step_one], me, members, rows, keys, pack)
+    write_rows((mine_next_ref, theirs_next_ref), [step_two], me, members, rows, keys, pack)
+    write_rows((mine_last_ref, theirs_last_ref), [kept], me, members, rows, keys, pack)
 
 
 def total_of(refs, terms, height, size):
@@ -232,9 +233,9 @@
             )
 
         tile = depth // 4
-        sizes = dict(keys=keys, members=members, rows=rows)
+        sizes = dict(keys=keys, members=members, rows=rows, pack=pack)
         mine, theirs, x, acc = pl.pallas_call(
-            functools.partial(first_kernel, tile=tile, pack=pack, **sizes),
+            functools.partial(first_kernel, tile=tile, **sizes),
             out_shape=[f32(half + EXTRA)] * 2
             + [jax.ShapeDtypeStruct(features.shape, features.dtype), f32(block)],
             in_specs=[SMEM, HBM, HBM],
@@ -295,14 +296,13 @@
         last, last_in = put(mine_last), put(swap(theirs_last, (1, 1)))
         extra.append((one_next, half))
         both = [(half // 2, [(two, i * half // 2), (other, 0)]) for i, other in enumerate(two_in)]
-        two_next = [
-            put(swap(total(both, *columns), steps[0]), False) for columns in ranges
-        ]
+        two_sent = [put(total(both, *columns), False) for columns in ranges]
+        two_next = [put(swap(arrays[i], steps[0]), False) for i in two_sent]
         chains = []
         for (start, size), two_out in zip(ranges, two_next):
             carried = [] if start else [(EXTRA, extra)]
             message = total(
-                [(half, [(after, 0), (after_in, 0), (one_next, 0)])] + carried, start, size, [two_out]
+                [(half, [(after, 0), (after_in, 0), (one_next, 0)])] + carried, start, size, two_next[:1] if start else two_sent
             )
             added = put(swap(message, steps[1]), False)
             chains.append([(last, 0), (last_in, 0), (two_out, 0), (added, 0)])
@@ -314,7 +314,7 @@
             for c, (start, size) in enumerate(ranges):
                 carried = [] if start else [(EXTRA, extra)]
                 message = total([(height, chains[c])] + carried, start, size)
-                added = put(swap(message, masks), False)
+                added = put(swap(message, masks[::-1] if c else masks), False)
                 chains[c] = [(i, row + height) for i, row in chains[c]] + [(added, 0)]
                 if not start:
                     extra = extra + [(added, height)]

time: 44 us -> 43.7 us (level)
  waiting for transfers between devices: 13.4 us -> 11.1 us
  starting transfers between devices: 18.9 us -> 21 us
    ppermute x14, waiting for transfers between devices: 13.4 us -> 11.1 us  [swap(): return lax.ppermute(value, axes, pairs)]
    ppermute x14, starting transfers between devices: 18.9 us -> 21 us  [swap(): return lax.ppermute(value, axes, pairs)]
  transfers between devices with their start and end apart: 14 -> 14, of which waited for: 9 -> 7; matrix products, arithmetic and copies ran while one was open for 0% -> 0% of each run, Pallas kernels for 10% -> 10%
where the time goes in v6:
time: 43.7 us; the launch traced here: 43.6 us
  starting transfers between devices  21 us (48%)
  waiting for transfers between devices  11.1 us (25%)
  Pallas kernels  10.2 us (23%)
  between operations  0.74 us (2%)
  local copies, waits for them, and re-layouts  0.65 us (1%)
    ppermute x14, starting transfers between devices, swap(): return lax.ppermute(value, axes, pairs)  21 us
    ppermute x14, waiting for transfers between devices, swap(): return lax.ppermute(value, axes, pairs)  11.1 us
    pallas_call x1, Pallas kernels, body(): pl.pallas_call(functools.partial(first_kernel, tile=tile, **sizes), out_s...  5.02 us
    pallas_call x1, Pallas kernels, body(): pl.pallas_call(functools.partial(third_kernel, **sizes), out_shape=[f32(h...  2.17 us
    pallas_call x1, Pallas kernels, body(): pl.pallas_call(functools.partial(second_kernel, block=block), out_shape=j...  1.88 us
  transfers between devices with their start and end apart: 14, of which 7 were waited for; matrix products, arithmetic and copies ran while one was open for 0% of the time, Pallas kernels for 10%

profile of v6, /device:TPU:0, one launch (start us, length us, event | category | flops | bytes accessed | tf_op | source)
XLA Modules:
  0.0 43.6 jit_solution(14671025079188808328)
XLA Ops:
  0.6 0.0 copy-start
  0.6 0.6 %copy-done = s32[1,2]{1,0:T(1,128)S(1)} copy-done((s32[1,2]{1,0:T(1,128)S(1)}, s32[1,2]{1,0:T(1,128)}, u32[]{:S(2)}) %copy-start) | copy-done | bytes 32
  1.3 5.0 %shard_map.49 = (f32[136,1024]{1,0:T(8,128)S(1)}, f32[136,1024]{1,0:T(8,128)S(1)}, bf16[4096,1024]{1,0:T(8,128)(2,1)S(1)}, f32[256,1024]{1,0:T(8,128)S(1)}) custom-call(s32[1]{0:T(128)} %bitcast.me_ref, s32[1,2]{1,0:T(1,128)S(1)} %copy-done, bf16[4096,1024]{1,0:T(8,128)(2,1)} %x_hbm.1), custom_call_target="tpu_custom_call" | custom-call | flops 2147483648 | bytes 8388608 | tf_op jit(solution)/shard_map/pallas_call | solution.py:237
  6.3 0.5 %collective-permute-start = (f32[136,1024]{1,0:T(8,128)S(1)}, f32[136,1024]{1,0:T(8,128)S(1)}, u32[]{:S(2)}, u32[]{:S(2)}) collective-permute-start(f32[136,1024]{1,0:T(8,128)S(1)} %get-tuple-element.18), channel_id=1, source_target_pairs={{0,1},{1,0},{2,3},{3,2},{4,5},{5,4},{6,7},{7,6},{8,9},{9,8},{10,11... | collective-permute-start | bytes 1671176 | tf_op jit(solution)/shard_map/ppermute | solution.py:214
  6.8 1.9 %shard_map.51.second_ref = f32[256,768]{1,0:T(8,128)S(1)} custom-call(bf16[4096,1024]{1,0:T(8,128)(2,1)S(1)} %get-tuple-element.19.x_ref), custom_call_target="tpu_custom_call" | custom-call | flops 1610612736 | bytes 8388608 | tf_op jit(solution)/shard_map/pallas_call | solution.py:252
  8.7 0.0 collective-permute-done.refs_1_
  8.7 0.1 shard_map.50.after_ref
  8.8 2.6 %collective-permute-start.1 = (f32[136,1024]{1,0:T(8,128)S(1)}, f32[136,1024]{1,0:T(8,128)S(1)}, u32[]{:S(2)}, u32[]{:S(2)}) collective-permute-start(f32[136,1024]{1,0:T(8,128)S(1)} %shard_map.50.after_ref), channel_id=1, source_target_pairs={{0,8},{1,17},{2,10},{3,19},{4,12},{5,21},{6,14},{7,23},{8,0},{9,25... | collective-permute-start | bytes 1671176 | tf_op jit(solution)/shard_map/ppermute | solution.py:214
  11.4 2.2 %shard_map.52 = (f32[128,1024]{1,0:T(8,128)S(1)}, f32[64,1024]{1,0:T(8,128)S(1)}, f32[64,1024]{1,0:T(8,128)S(1)}, f32[128,1024]{1,0:T(8,128)S(1)}, f32[128,1024]...) custom-call(s32[1]{0:T(128)} %bitcast.me_ref, bf16[4096,1024]{1,0:T(8,128)(2,1)S(1)} %get-tuple-element.19.x_ref, ...), custom_call_target="tpu_custom_call" | custom-call | flops 1610612736 | bytes 8388608 | tf_op jit(solution)/shard_map/pallas_call | solution.py:285
  13.6 0.1 collective-permute-start.7
  13.7 0.5 %collective-permute-start.3 = (f32[64,1024]{1,0:T(8,128)S(1)}, f32[64,1024]{1,0:T(8,128)S(1)}, u32[]{:S(2)}, u32[]{:S(2)}) collective-permute-start(f32[64,1024]{1,0:T(8,128)S(1)} %get-tuple-element.24), channel_id=1, source_target_pairs={{0,1},{1,0},{2,3},{3,2},{4,5},{5,4},{6,7},{7,6},{8,9},{9,8},{10,11... | collective-permute-start | bytes 786440 | tf_op jit(solution)/shard_map/ppermute | solution.py:214
  14.2 0.1 collective-permute-start.4
  14.2 0.4 collective-permute-start.2
  14.7 1.3 %collective-permute-done.3.refs_1_ = f32[64,1024]{1,0:T(8,128)S(1)} collective-permute-done((f32[64,1024]{1,0:T(8,128)S(1)}, f32[64,1024]{1,0:T(8,128)S(1)}, u32[]{:S(2)}, u32[]{:S(2)}) %collective-permute-start.3) | collective-permute-done | bytes 262176 | tf_op jit(solution)/shard_map/ppermute | solution.py:214
  15.9 0.4 collective-permute-done.4.refs_2_
  16.4 1.1 %collective-permute-start.5 = (f32[128,512]{1,0:T(8,128)S(1)}, f32[128,512]{1,0:T(8,128)S(1)}, u32[]{:S(2)}, u32[]{:S(2)}) collective-permute-start(f32[128,512]{1,0:T(8,128)S(1)} %shard_map.53.refs_5_), channel_id=1, source_target_pairs={{0,8},{1,17},{2,10},{3,19},{4,12},{5,21},{6,14},{7,23},{8,0},{9,25... | collective-permute-start | bytes 786440 | tf_op jit(solution)/shard_map/ppermute | solution.py:214
  17.5 0.0 collective-permute-done.7.refs_4_.refs_2_
  17.5 1.5 %collective-permute-done.1.refs_2_.refs_0_ = f32[136,1024]{1,0:T(8,128)S(1)} collective-permute-done((f32[136,1024]{1,0:T(8,128)S(1)}, f32[136,1024]{1,0:T(8,128)S(1)}, u32[]{:S(2)}, u32[]{:S(2)}) %collective-permute-start.1) | collective-permute-done | bytes 557088 | tf_op jit(solution)/shard_map/ppermute | solution.py:214
  19.0 1.8 %collective-permute-start.8 = (f32[136,512]{1,0:T(8,128)S(1)}, f32[136,512]{1,0:T(8,128)S(1)}, u32[]{:S(2)}, u32[]{:S(2)}) collective-permute-start(f32[136,512]{1,0:T(8,128)S(1)} %shard_map.55), channel_id=1, source_target_pairs={{0,16},{1,9},{2,18},{3,11},{4,20},{5,13},{6,22},{7,15},{8,24},{9,1... | collective-permute-start | bytes 835592 | tf_op jit(solution)/shard_map/ppermute | solution.py:214
  20.8 1.5 %collective-permute-start.6 = (f32[128,512]{1,0:T(8,128)S(1)}, f32[128,512]{1,0:T(8,128)S(1)}, u32[]{:S(2)}, u32[]{:S(2)}) collective-permute-start(f32[128,512]{1,0:T(8,128)S(1)} %shard_map.54.refs_6_), channel_id=1, source_target_pairs={{0,8},{1,17},{2,10},{3,19},{4,12},{5,21},{6,14},{7,23},{8,0},{9,25... | collective-permute-start | bytes 786440 | tf_op jit(solution)/shard_map/ppermute | solution.py:214
  22.3 1.7 %collective-permute-done.5.refs_3_.refs_5_ = f32[128,512]{1,0:T(8,128)S(1)} collective-permute-done((f32[128,512]{1,0:T(8,128)S(1)}, f32[128,512]{1,0:T(8,128)S(1)}, u32[]{:S(2)}, u32[]{:S(2)}) %collective-permute-start.5) | collective-permute-done | bytes 262176 | tf_op jit(solution)/shard_map/ppermute | solution.py:214
  24.0 1.0 %collective-permute-start.9 = (f32[128,512]{1,0:T(8,128)S(1)}, f32[128,512]{1,0:T(8,128)S(1)}, u32[]{:S(2)}, u32[]{:S(2)}) collective-permute-start(f32[128,512]{1,0:T(8,128)S(1)} %shard_map.56), channel_id=1, source_target_pairs={{0,16},{1,9},{2,18},{3,11},{4,20},{5,13},{6,22},{7,15},{8,24},{9,1... | collective-permute-start | bytes 786440 | tf_op jit(solution)/shard_map/ppermute | solution.py:214
  25.1 0.0 collective-permute-done.2.refs_4_.refs_1_
  25.1 3.2 %collective-permute-done.8.refs_6_.refs_7_ = f32[136,512]{1,0:T(8,128)S(1)} collective-permute-done((f32[136,512]{1,0:T(8,128)S(1)}, f32[136,512]{1,0:T(8,128)S(1)}, u32[]{:S(2)}, u32[]{:S(2)}) %collective-permute-start.8) | collective-permute-done | bytes 278560 | tf_op jit(solution)/shard_map/ppermute | solution.py:214
  28.3 2.1 %collective-permute-start.10 = (f32[72,512]{1,0:T(8,128)S(1)}, f32[72,512]{1,0:T(8,128)S(1)}, u32[]{:S(2)}, u32[]{:S(2)}) collective-permute-start(f32[72,512]{1,0:T(8,128)S(1)} %shard_map.57), channel_id=1, source_target_pairs={{0,2},{1,5},{2,0},{3,7},{4,6},{5,1},{6,4},{7,3},{8,10},{9,13},{10,... | collective-permute-start | bytes 442376 | tf_op jit(solution)/shard_map/ppermute | solution.py:214
  30.4 0.0 collective-permute-done.6.refs_2_.refs_6_
  30.4 0.7 %collective-permute-done.9.refs_3_.refs_8_ = f32[128,512]{1,0:T(8,128)S(1)} collective-permute-done((f32[128,512]{1,0:T(8,128)S(1)}, f32[128,512]{1,0:T(8,128)S(1)}, u32[]{:S(2)}, u32[]{:S(2)}) %collective-permute-start.9) | collective-permute-done | bytes 262176 | tf_op jit(solution)/shard_map/ppermute | solution.py:214
  31.2 3.0 %collective-permute-start.11 = (f32[64,512]{1,0:T(8,128)S(1)}, f32[64,512]{1,0:T(8,128)S(1)}, u32[]{:S(2)}, u32[]{:S(2)}) collective-permute-start(f32[64,512]{1,0:T(8,128)S(1)} %shard_map.58), channel_id=1, source_target_pairs={{0,4},{1,3},{2,6},{3,1},{4,0},{5,7},{6,2},{7,5},{8,12},{9,11},{10,... | collective-permute-start | bytes 393224 | tf_op jit(solution)/shard_map/ppermute | solution.py:214
  34.3 0.0 collective-permute-done.10.refs_7_.refs_9_
  34.3 3.5 %collective-permute-start.12 = (f32[40,512]{1,0:T(8,128)S(1)}, f32[40,512]{1,0:T(8,128)S(1)}, u32[]{:S(2)}, u32[]{:S(2)}) collective-permute-start(f32[40,512]{1,0:T(8,128)S(1)} %shard_map.59), channel_id=1, source_target_pairs={{0,4},{1,3},{2,6},{3,1},{4,0},{5,7},{6,2},{7,5},{8,12},{9,11},{10,... | collective-permute-start | bytes 245768 | tf_op jit(solution)/shard_map/ppermute | solution.py:214
  37.8 0.0 collective-permute-done.11.refs_4_.refs_10_
  37.8 2.8 %collective-permute-start.13 = (f32[32,512]{1,0:T(8,128)S(1)}, f32[32,512]{1,0:T(8,128)S(1)}, u32[]{:S(2)}, u32[]{:S(2)}) collective-permute-start(f32[32,512]{1,0:T(8,128)S(1)} %shard_map.60), channel_id=1, source_target_pairs={{0,2},{1,5},{2,0},{3,7},{4,6},{5,1},{6,4},{7,3},{8,10},{9,13},{10,... | collective-permute-start | bytes 196616 | tf_op jit(solution)/shard_map/ppermute | solution.py:214
  40.6 2.2 %collective-permute-done.13.refs_12_ = f32[32,512]{1,0:T(8,128)S(1)} collective-permute-done((f32[32,512]{1,0:T(8,128)S(1)}, f32[32,512]{1,0:T(8,128)S(1)}, u32[]{:S(2)}, u32[]{:S(2)}) %collective-permute-start.13) | collective-permute-done | bytes 65568 | tf_op jit(solution)/shard_map/ppermute | solution.py:214
  42.8 0.0 collective-permute-done.12.refs_11_
  42.8 0.8 %shard_map.61 = (f32[32,1024]{1,0:T(8,128)}, f32[1,1024]{1,0:T(1,128)}, f32[1,1]{1,0:T(1,128)}) custom-call(s32[1]{0:T(128)} %bitcast.me_ref, f32[136,1024]{1,0:T(8,128)S(1)} %get-tuple-element.17.refs_0_, f32[136,1024]{1,0:T(8,128)S(1)} %collective-permute-done.refs_1_, f32[136,1024]{1,0:T(8,128)S(1)} %collective-permute-done.1.refs_2_.refs_0_, ...), custom_call_target="tpu_custom_call" | custom-call | flops 1 | bytes 1 | tf_op jit(solution)/shard_map/pallas_call | solution.py:323
  (8 shorter events, 0.2 us)
Async XLA Ops:
  0.6 0.7 %copy-start = (s32[1,2]{1,0:T(1,128)S(1)}, s32[1,2]{1,0:T(1,128)}, u32[]{:S(2)}) copy-start(s32[1,2]{1,0:T(1,128)} %len_hbm.1) | copy-start | bytes 28
  6.3 2.4 %collective-permute-start = (f32[136,1024]{1,0:T(8,128)S(1)}, f32[136,1024]{1,0:T(8,128)S(1)}, u32[]{:S(2)}, u32[]{:S(2)}) collective-permute-start(f32[136,1024]{1,0:T(8,128)S(1)} %get-tuple-element.18), channel_id=1, source_target_pairs={{0,1},{1,0},{2,3},{3,2},{4,5},{5,4},{6,7},{7,6},{8,9},{9,8},{10,11... | collective-permute-start | bytes 1671176 | tf_op jit(solution)/shard_map/ppermute | solution.py:214
  8.8 10.1 %collective-permute-start.1 = (f32[136,1024]{1,0:T(8,128)S(1)}, f32[136,1024]{1,0:T(8,128)S(1)}, u32[]{:S(2)}, u32[]{:S(2)}) collective-permute-start(f32[136,1024]{1,0:T(8,128)S(1)} %shard_map.50.after_ref), channel_id=1, source_target_pairs={{0,8},{1,17},{2,10},{3,19},{4,12},{5,21},{6,14},{7,23},{8,0},{9,25... | collective-permute-start | bytes 1671176 | tf_op jit(solution)/shard_map/ppermute | solution.py:214
  13.6 3.9 %collective-permute-start.7 = (f32[128,1024]{1,0:T(8,128)S(1)}, f32[128,1024]{1,0:T(8,128)S(1)}, u32[]{:S(2)}, u32[]{:S(2)}) collective-permute-start(f32[128,1024]{1,0:T(8,128)S(1)} %get-tuple-element.27), channel_id=1, source_target_pairs={{0,1},{1,0},{2,3},{3,2},{4,5},{5,4},{6,7},{7,6},{8,9},{9,8},{10,11... | collective-permute-start | bytes 1572872 | tf_op jit(solution)/shard_map/ppermute | solution.py:214
  13.7 2.3 %collective-permute-start.3 = (f32[64,1024]{1,0:T(8,128)S(1)}, f32[64,1024]{1,0:T(8,128)S(1)}, u32[]{:S(2)}, u32[]{:S(2)}) collective-permute-start(f32[64,1024]{1,0:T(8,128)S(1)} %get-tuple-element.24), channel_id=1, source_target_pairs={{0,1},{1,0},{2,3},{3,2},{4,5},{5,4},{6,7},{7,6},{8,9},{9,8},{10,11... | collective-permute-start | bytes 786440 | tf_op jit(solution)/shard_map/ppermute | solution.py:214
  14.2 2.1 %collective-permute-start.4 = (f32[64,1024]{1,0:T(8,128)S(1)}, f32[64,1024]{1,0:T(8,128)S(1)}, u32[]{:S(2)}, u32[]{:S(2)}) collective-permute-start(f32[64,1024]{1,0:T(8,128)S(1)} %get-tuple-element.25), channel_id=1, source_target_pairs={{0,1},{1,0},{2,3},{3,2},{4,5},{5,4},{6,7},{7,6},{8,9},{9,8},{10,11... | collective-permute-start | bytes 786440 | tf_op jit(solution)/shard_map/ppermute | solution.py:214
  14.2 10.8 %collective-permute-start.2 = (f32[128,1024]{1,0:T(8,128)S(1)}, f32[128,1024]{1,0:T(8,128)S(1)}, u32[]{:S(2)}, u32[]{:S(2)}) collective-permute-start(f32[128,1024]{1,0:T(8,128)S(1)} %get-tuple-element.22), channel_id=1, source_target_pairs={{0,1},{1,0},{2,3},{3,2},{4,5},{5,4},{6,7},{7,6},{8,9},{9,8},{10,11... | collective-permute-start | bytes 1572872 | tf_op jit(solution)/shard_map/ppermute | solution.py:214
  16.4 7.6 %collective-permute-start.5 = (f32[128,512]{1,0:T(8,128)S(1)}, f32[128,512]{1,0:T(8,128)S(1)}, u32[]{:S(2)}, u32[]{:S(2)}) collective-permute-start(f32[128,512]{1,0:T(8,128)S(1)} %shard_map.53.refs_5_), channel_id=1, source_target_pairs={{0,8},{1,17},{2,10},{3,19},{4,12},{5,21},{6,14},{7,23},{8,0},{9,25... | collective-permute-start | bytes 786440 | tf_op jit(solution)/shard_map/ppermute | solution.py:214
  19.0 9.3 %collective-permute-start.8 = (f32[136,512]{1,0:T(8,128)S(1)}, f32[136,512]{1,0:T(8,128)S(1)}, u32[]{:S(2)}, u32[]{:S(2)}) collective-permute-start(f32[136,512]{1,0:T(8,128)S(1)} %shard_map.55), channel_id=1, source_target_pairs={{0,16},{1,9},{2,18},{3,11},{4,20},{5,13},{6,22},{7,15},{8,24},{9,1... | collective-permute-start | bytes 835592 | tf_op jit(solution)/shard_map/ppermute | solution.py:214
  20.8 9.7 %collective-permute-start.6 = (f32[128,512]{1,0:T(8,128)S(1)}, f32[128,512]{1,0:T(8,128)S(1)}, u32[]{:S(2)}, u32[]{:S(2)}) collective-permute-start(f32[128,512]{1,0:T(8,128)S(1)} %shard_map.54.refs_6_), channel_id=1, source_target_pairs={{0,8},{1,17},{2,10},{3,19},{4,12},{5,21},{6,14},{7,23},{8,0},{9,25... | collective-permute-start | bytes 786440 | tf_op jit(solution)/shard_map/ppermute | solution.py:214
  24.0 7.2 %collective-permute-start.9 = (f32[128,512]{1,0:T(8,128)S(1)}, f32[128,512]{1,0:T(8,128)S(1)}, u32[]{:S(2)}, u32[]{:S(2)}) collective-permute-start(f32[128,512]{1,0:T(8,128)S(1)} %shard_map.56), channel_id=1, source_target_pairs={{0,16},{1,9},{2,18},{3,11},{4,20},{5,13},{6,22},{7,15},{8,24},{9,1... | collective-permute-start | bytes 786440 | tf_op jit(solution)/shard_map/ppermute | solution.py:214
  28.3 6.0 %collective-permute-start.10 = (f32[72,512]{1,0:T(8,128)S(1)}, f32[72,512]{1,0:T(8,128)S(1)}, u32[]{:S(2)}, u32[]{:S(2)}) collective-permute-start(f32[72,512]{1,0:T(8,128)S(1)} %shard_map.57), channel_id=1, source_target_pairs={{0,2},{1,5},{2,0},{3,7},{4,6},{5,1},{6,4},{7,3},{8,10},{9,13},{10,... | collective-permute-start | bytes 442376 | tf_op jit(solution)/shard_map/ppermute | solution.py:214
  31.2 6.5 %collective-permute-start.11 = (f32[64,512]{1,0:T(8,128)S(1)}, f32[64,512]{1,0:T(8,128)S(1)}, u32[]{:S(2)}, u32[]{:S(2)}) collective-permute-start(f32[64,512]{1,0:T(8,128)S(1)} %shard_map.58), channel_id=1, source_target_pairs={{0,4},{1,3},{2,6},{3,1},{4,0},{5,7},{6,2},{7,5},{8,12},{9,11},{10,... | collective-permute-start | bytes 393224 | tf_op jit(solution)/shard_map/ppermute | solution.py:214
  34.3 8.5 %collective-permute-start.12 = (f32[40,512]{1,0:T(8,128)S(1)}, f32[40,512]{1,0:T(8,128)S(1)}, u32[]{:S(2)}, u32[]{:S(2)}) collective-permute-start(f32[40,512]{1,0:T(8,128)S(1)} %shard_map.59), channel_id=1, source_target_pairs={{0,4},{1,3},{2,6},{3,1},{4,0},{5,7},{6,2},{7,5},{8,12},{9,11},{10,... | collective-permute-start | bytes 245768 | tf_op jit(solution)/shard_map/ppermute | solution.py:214
  37.8 5.0 %collective-permute-start.13 = (f32[32,512]{1,0:T(8,128)S(1)}, f32[32,512]{1,0:T(8,128)S(1)}, u32[]{:S(2)}, u32[]{:S(2)}) collective-permute-start(f32[32,512]{1,0:T(8,128)S(1)} %shard_map.60), channel_id=1, source_target_pairs={{0,2},{1,5},{2,0},{3,7},{4,6},{5,1},{6,4},{7,3},{8,10},{9,13},{10,... | collective-permute-start | bytes 196616 | tf_op jit(solution)/shard_map/ppermute | solution.py:214

commit v7 on v5

--- a/solution.py
+++ b/solution.py
@@ -198,9 +198,9 @@
     axes = ("grp", "mem")
     groups, members = mesh.shape["grp"], mesh.shape["mem"]
     devices = groups * members
-    keys = (3, 1, 2, 0)
+    keys = (3, 2, 1, 0)
     assert groups == len(keys)
-    steps = [(members, 2 * members), (2 * members, members)]
+    steps = [(2 * members, members), (members, 2 * members)]
     steps += [(mask, mask) for mask in member_masks(members)]
 
     def swap(value, masks):

time: 43.9 us -> 43.9 us (level)
  waiting for transfers between devices: 12 us -> 12.6 us
  starting transfers between devices: 20.2 us -> 19.6 us
    ppermute x14, starting transfers between devices: 20.2 us -> 19.6 us  [swap(): return lax.ppermute(value, axes, pairs)]
    ppermute x14, waiting for transfers between devices: 12 us -> 12.6 us  [swap(): return lax.ppermute(value, axes, pairs)]
where the time goes in v7:
time: 43.9 us; the launch traced here: 43.7 us
  starting transfers between devices  19.6 us (45%)
  waiting for transfers between devices  12.6 us (29%)
  Pallas kernels  10.1 us (23%)
  between operations  0.73 us (2%)
  local copies, waits for them, and re-layouts  0.65 us (1%)
    ppermute x14, starting transfers between devices, swap(): return lax.ppermute(value, axes, pairs)  19.6 us
    ppermute x14, waiting for transfers between devices, swap(): return lax.ppermute(value, axes, pairs)  12.6 us
    pallas_call x1, Pallas kernels, body(): pl.pallas_call(functools.partial(first_kernel, tile=tile, pack=pack, **si...  5.02 us
    pallas_call x1, Pallas kernels, body(): pl.pallas_call(functools.partial(third_kernel, **sizes), out_shape=[f32(h...  2.17 us
    pallas_call x1, Pallas kernels, body(): pl.pallas_call(functools.partial(second_kernel, block=block), out_shape=j...  1.88 us
  transfers between devices with their start and end apart: 14, of which 9 were waited for; matrix products, arithmetic and copies ran while one was open for 0% of the time, Pallas kernels for 10%

profile of v7, /device:TPU:0, one launch (start us, length us, event | category | flops | bytes accessed | tf_op | source)
XLA Modules:
  0.0 43.7 jit_solution(12968961487912198738)
XLA Ops:
  0.6 0.0 copy-start
  0.6 0.6 %copy-done = s32[1,2]{1,0:T(1,128)S(1)} copy-done((s32[1,2]{1,0:T(1,128)S(1)}, s32[1,2]{1,0:T(1,128)}, u32[]{:S(2)}) %copy-start) | copy-done | bytes 32
  1.3 5.0 %shard_map.49 = (f32[136,1024]{1,0:T(8,128)S(1)}, f32[136,1024]{1,0:T(8,128)S(1)}, bf16[4096,1024]{1,0:T(8,128)(2,1)S(1)}, f32[256,1024]{1,0:T(8,128)S(1)}) custom-call(s32[1]{0:T(128)} %bitcast.me_ref, s32[1,2]{1,0:T(1,128)S(1)} %copy-done, bf16[4096,1024]{1,0:T(8,128)(2,1)} %x_hbm.1), custom_call_target="tpu_custom_call" | custom-call | flops 2147483648 | bytes 8388608 | tf_op jit(solution)/shard_map/pallas_call | solution.py:231
  6.3 0.5 %collective-permute-start = (f32[136,1024]{1,0:T(8,128)S(1)}, f32[136,1024]{1,0:T(8,128)S(1)}, u32[]{:S(2)}, u32[]{:S(2)}) collective-permute-start(f32[136,1024]{1,0:T(8,128)S(1)} %get-tuple-element.18), channel_id=1, source_target_pairs={{0,1},{1,0},{2,3},{3,2},{4,5},{5,4},{6,7},{7,6},{8,9},{9,8},{10,11... | collective-permute-start | bytes 1671176 | tf_op jit(solution)/shard_map/ppermute | solution.py:208
  6.8 1.9 %shard_map.51.second_ref = f32[256,768]{1,0:T(8,128)S(1)} custom-call(bf16[4096,1024]{1,0:T(8,128)(2,1)S(1)} %get-tuple-element.19.x_ref), custom_call_target="tpu_custom_call" | custom-call | flops 1610612736 | bytes 8388608 | tf_op jit(solution)/shard_map/pallas_call | solution.py:246
  8.7 0.0 collective-permute-done.refs_1_
  8.7 0.1 shard_map.50.after_ref
  8.8 2.3 %collective-permute-start.1 = (f32[136,1024]{1,0:T(8,128)S(1)}, f32[136,1024]{1,0:T(8,128)S(1)}, u32[]{:S(2)}, u32[]{:S(2)}) collective-permute-start(f32[136,1024]{1,0:T(8,128)S(1)} %shard_map.50.after_ref), channel_id=1, source_target_pairs={{0,16},{1,9},{2,18},{3,11},{4,20},{5,13},{6,22},{7,15},{8,24},{9,1... | collective-permute-start | bytes 1671176 | tf_op jit(solution)/shard_map/ppermute | solution.py:208
  11.1 2.2 %shard_map.52 = (f32[128,1024]{1,0:T(8,128)S(1)}, f32[64,1024]{1,0:T(8,128)S(1)}, f32[64,1024]{1,0:T(8,128)S(1)}, f32[128,1024]{1,0:T(8,128)S(1)}, f32[128,1024]...) custom-call(s32[1]{0:T(128)} %bitcast.me_ref, bf16[4096,1024]{1,0:T(8,128)(2,1)S(1)} %get-tuple-element.19.x_ref, ...), custom_call_target="tpu_custom_call" | custom-call | flops 1610612736 | bytes 8388608 | tf_op jit(solution)/shard_map/pallas_call | solution.py:279
  13.3 0.5 %collective-permute-start.7 = (f32[128,1024]{1,0:T(8,128)S(1)}, f32[128,1024]{1,0:T(8,128)S(1)}, u32[]{:S(2)}, u32[]{:S(2)}) collective-permute-start(f32[128,1024]{1,0:T(8,128)S(1)} %get-tuple-element.27), channel_id=1, source_target_pairs={{0,1},{1,0},{2,3},{3,2},{4,5},{5,4},{6,7},{7,6},{8,9},{9,8},{10,11... | collective-permute-start | bytes 1572872 | tf_op jit(solution)/shard_map/ppermute | solution.py:208
  13.8 0.1 collective-permute-start.3
  13.9 0.4 collective-permute-start.4
  14.4 0.1 collective-permute-start.2
  14.4 1.3 %collective-permute-done.3.refs_1_ = f32[64,1024]{1,0:T(8,128)S(1)} collective-permute-done((f32[64,1024]{1,0:T(8,128)S(1)}, f32[64,1024]{1,0:T(8,128)S(1)}, u32[]{:S(2)}, u32[]{:S(2)}) %collective-permute-start.3) | collective-permute-done | bytes 262176 | tf_op jit(solution)/shard_map/ppermute | solution.py:208
  15.8 0.4 collective-permute-done.4.refs_2_
  16.2 1.4 %collective-permute-start.5 = (f32[128,512]{1,0:T(8,128)S(1)}, f32[128,512]{1,0:T(8,128)S(1)}, u32[]{:S(2)}, u32[]{:S(2)}) collective-permute-start(f32[128,512]{1,0:T(8,128)S(1)} %shard_map.53.refs_5_), channel_id=1, source_target_pairs={{0,16},{1,9},{2,18},{3,11},{4,20},{5,13},{6,22},{7,15},{8,24},{9,1... | collective-permute-start | bytes 786440 | tf_op jit(solution)/shard_map/ppermute | solution.py:208
  17.6 0.0 collective-permute-done.7.refs_4_.refs_2_
  17.6 1.0 %collective-permute-done.1.refs_2_.refs_0_ = f32[136,1024]{1,0:T(8,128)S(1)} collective-permute-done((f32[136,1024]{1,0:T(8,128)S(1)}, f32[136,1024]{1,0:T(8,128)S(1)}, u32[]{:S(2)}, u32[]{:S(2)}) %collective-permute-start.1) | collective-permute-done | bytes 557088 | tf_op jit(solution)/shard_map/ppermute | solution.py:208
  18.7 2.4 %collective-permute-start.8 = (f32[136,512]{1,0:T(8,128)S(1)}, f32[136,512]{1,0:T(8,128)S(1)}, u32[]{:S(2)}, u32[]{:S(2)}) collective-permute-start(f32[136,512]{1,0:T(8,128)S(1)} %shard_map.55), channel_id=1, source_target_pairs={{0,8},{1,17},{2,10},{3,19},{4,12},{5,21},{6,14},{7,23},{8,0},{9,25... | collective-permute-start | bytes 835592 | tf_op jit(solution)/shard_map/ppermute | solution.py:208
  21.1 1.4 %collective-permute-start.6 = (f32[128,512]{1,0:T(8,128)S(1)}, f32[128,512]{1,0:T(8,128)S(1)}, u32[]{:S(2)}, u32[]{:S(2)}) collective-permute-start(f32[128,512]{1,0:T(8,128)S(1)} %shard_map.54.refs_6_), channel_id=1, source_target_pairs={{0,16},{1,9},{2,18},{3,11},{4,20},{5,13},{6,22},{7,15},{8,24},{9,1... | collective-permute-start | bytes 786440 | tf_op jit(solution)/shard_map/ppermute | solution.py:208
  22.4 1.3 %collective-permute-done.5.refs_3_.refs_5_ = f32[128,512]{1,0:T(8,128)S(1)} collective-permute-done((f32[128,512]{1,0:T(8,128)S(1)}, f32[128,512]{1,0:T(8,128)S(1)}, u32[]{:S(2)}, u32[]{:S(2)}) %collective-permute-start.5) | collective-permute-done | bytes 262176 | tf_op jit(solution)/shard_map/ppermute | solution.py:208
  23.7 1.4 %collective-permute-start.9 = (f32[128,512]{1,0:T(8,128)S(1)}, f32[128,512]{1,0:T(8,128)S(1)}, u32[]{:S(2)}, u32[]{:S(2)}) collective-permute-start(f32[128,512]{1,0:T(8,128)S(1)} %shard_map.56), channel_id=1, source_target_pairs={{0,8},{1,17},{2,10},{3,19},{4,12},{5,21},{6,14},{7,23},{8,0},{9,25... | collective-permute-start | bytes 786440 | tf_op jit(solution)/shard_map/ppermute | solution.py:208
  25.1 0.0 collective-permute-done.2.refs_4_.refs_1_
  25.1 3.3 %collective-permute-done.8.refs_6_.refs_7_ = f32[136,512]{1,0:T(8,128)S(1)} collective-permute-done((f32[136,512]{1,0:T(8,128)S(1)}, f32[136,512]{1,0:T(8,128)S(1)}, u32[]{:S(2)}, u32[]{:S(2)}) %collective-permute-start.8) | collective-permute-done | bytes 278560 | tf_op jit(solution)/shard_map/ppermute | solution.py:208
  28.4 1.9 %collective-permute-start.10 = (f32[72,512]{1,0:T(8,128)S(1)}, f32[72,512]{1,0:T(8,128)S(1)}, u32[]{:S(2)}, u32[]{:S(2)}) collective-permute-start(f32[72,512]{1,0:T(8,128)S(1)} %shard_map.57), channel_id=1, source_target_pairs={{0,2},{1,3},{2,0},{3,1},{4,6},{5,7},{6,4},{7,5},{8,10},{9,11},{10,... | collective-permute-start | bytes 442376 | tf_op jit(solution)/shard_map/ppermute | solution.py:208
  30.3 0.0 collective-permute-done.6.refs_2_.refs_6_
  30.3 0.9 %collective-permute-done.9.refs_3_.refs_8_ = f32[128,512]{1,0:T(8,128)S(1)} collective-permute-done((f32[128,512]{1,0:T(8,128)S(1)}, f32[128,512]{1,0:T(8,128)S(1)}, u32[]{:S(2)}, u32[]{:S(2)}) %collective-permute-start.9) | collective-permute-done | bytes 262176 | tf_op jit(solution)/shard_map/ppermute | solution.py:208
  31.2 1.9 %collective-permute-start.11 = (f32[64,512]{1,0:T(8,128)S(1)}, f32[64,512]{1,0:T(8,128)S(1)}, u32[]{:S(2)}, u32[]{:S(2)}) collective-permute-start(f32[64,512]{1,0:T(8,128)S(1)} %shard_map.58), channel_id=1, source_target_pairs={{0,2},{1,3},{2,0},{3,1},{4,6},{5,7},{6,4},{7,5},{8,10},{9,11},{10,... | collective-permute-start | bytes 393224 | tf_op jit(solution)/shard_map/ppermute | solution.py:208
  33.1 0.5 %collective-permute-done.10.refs_7_.refs_9_ = f32[72,512]{1,0:T(8,128)S(1)} collective-permute-done((f32[72,512]{1,0:T(8,128)S(1)}, f32[72,512]{1,0:T(8,128)S(1)}, u32[]{:S(2)}, u32[]{:S(2)}) %collective-permute-start.10) | collective-permute-done | bytes 147488 | tf_op jit(solution)/shard_map/ppermute | solution.py:208
  33.7 2.7 %collective-permute-start.12 = (f32[40,512]{1,0:T(8,128)S(1)}, f32[40,512]{1,0:T(8,128)S(1)}, u32[]{:S(2)}, u32[]{:S(2)}) collective-permute-start(f32[40,512]{1,0:T(8,128)S(1)} %shard_map.59), channel_id=1, source_target_pairs={{0,4},{1,5},{2,6},{3,7},{4,0},{5,1},{6,2},{7,3},{8,12},{9,13},{10,... | collective-permute-start | bytes 245768 | tf_op jit(solution)/shard_map/ppermute | solution.py:208
  36.4 1.3 %collective-permute-done.11.refs_4_.refs_10_ = f32[64,512]{1,0:T(8,128)S(1)} collective-permute-done((f32[64,512]{1,0:T(8,128)S(1)}, f32[64,512]{1,0:T(8,128)S(1)}, u32[]{:S(2)}, u32[]{:S(2)}) %collective-permute-start.11) | collective-permute-done | bytes 131104 | tf_op jit(solution)/shard_map/ppermute | solution.py:208
  37.7 2.7 %collective-permute-start.13 = (f32[32,512]{1,0:T(8,128)S(1)}, f32[32,512]{1,0:T(8,128)S(1)}, u32[]{:S(2)}, u32[]{:S(2)}) collective-permute-start(f32[32,512]{1,0:T(8,128)S(1)} %shard_map.60), channel_id=1, source_target_pairs={{0,4},{1,5},{2,6},{3,7},{4,0},{5,1},{6,2},{7,3},{8,12},{9,13},{10,... | collective-permute-start | bytes 196616 | tf_op jit(solution)/shard_map/ppermute | solution.py:208
  40.4 2.6 %collective-permute-done.13.refs_12_ = f32[32,512]{1,0:T(8,128)S(1)} collective-permute-done((f32[32,512]{1,0:T(8,128)S(1)}, f32[32,512]{1,0:T(8,128)S(1)}, u32[]{:S(2)}, u32[]{:S(2)}) %collective-permute-start.13) | collective-permute-done | bytes 65568 | tf_op jit(solution)/shard_map/ppermute | solution.py:208
  43.0 0.0 collective-permute-done.12.refs_11_
  43.0 0.8 %shard_map.61 = (f32[32,1024]{1,0:T(8,128)}, f32[1,1024]{1,0:T(1,128)}, f32[1,1]{1,0:T(1,128)}) custom-call(s32[1]{0:T(128)} %bitcast.me_ref, f32[136,1024]{1,0:T(8,128)S(1)} %get-tuple-element.17.refs_0_, f32[136,1024]{1,0:T(8,128)S(1)} %collective-permute-done.refs_1_, f32[136,1024]{1,0:T(8,128)S(1)} %collective-permute-done.1.refs_2_.refs_0_, ...), custom_call_target="tpu_custom_call" | custom-call | flops 1 | bytes 1 | tf_op jit(solution)/shard_map/pallas_call | solution.py:317
  (8 shorter events, 0.2 us)
Async XLA Ops:
  0.6 0.7 %copy-start = (s32[1,2]{1,0:T(1,128)S(1)}, s32[1,2]{1,0:T(1,128)}, u32[]{:S(2)}) copy-start(s32[1,2]{1,0:T(1,128)} %len_hbm.1) | copy-start | bytes 28
  6.3 2.4 %collective-permute-start = (f32[136,1024]{1,0:T(8,128)S(1)}, f32[136,1024]{1,0:T(8,128)S(1)}, u32[]{:S(2)}, u32[]{:S(2)}) collective-permute-start(f32[136,1024]{1,0:T(8,128)S(1)} %get-tuple-element.18), channel_id=1, source_target_pairs={{0,1},{1,0},{2,3},{3,2},{4,5},{5,4},{6,7},{7,6},{8,9},{9,8},{10,11... | collective-permute-start | bytes 1671176 | tf_op jit(solution)/shard_map/ppermute | solution.py:208
  8.8 9.8 %collective-permute-start.1 = (f32[136,1024]{1,0:T(8,128)S(1)}, f32[136,1024]{1,0:T(8,128)S(1)}, u32[]{:S(2)}, u32[]{:S(2)}) collective-permute-start(f32[136,1024]{1,0:T(8,128)S(1)} %shard_map.50.after_ref), channel_id=1, source_target_pairs={{0,16},{1,9},{2,18},{3,11},{4,20},{5,13},{6,22},{7,15},{8,24},{9,1... | collective-permute-start | bytes 1671176 | tf_op jit(solution)/shard_map/ppermute | solution.py:208
  13.3 4.3 %collective-permute-start.7 = (f32[128,1024]{1,0:T(8,128)S(1)}, f32[128,1024]{1,0:T(8,128)S(1)}, u32[]{:S(2)}, u32[]{:S(2)}) collective-permute-start(f32[128,1024]{1,0:T(8,128)S(1)} %get-tuple-element.27), channel_id=1, source_target_pairs={{0,1},{1,0},{2,3},{3,2},{4,5},{5,4},{6,7},{7,6},{8,9},{9,8},{10,11... | collective-permute-start | bytes 1572872 | tf_op jit(solution)/shard_map/ppermute | solution.py:208
  13.8 1.9 %collective-permute-start.3 = (f32[64,1024]{1,0:T(8,128)S(1)}, f32[64,1024]{1,0:T(8,128)S(1)}, u32[]{:S(2)}, u32[]{:S(2)}) collective-permute-start(f32[64,1024]{1,0:T(8,128)S(1)} %get-tuple-element.24), channel_id=1, source_target_pairs={{0,1},{1,0},{2,3},{3,2},{4,5},{5,4},{6,7},{7,6},{8,9},{9,8},{10,11... | collective-permute-start | bytes 786440 | tf_op jit(solution)/shard_map/ppermute | solution.py:208
  13.9 2.2 %collective-permute-start.4 = (f32[64,1024]{1,0:T(8,128)S(1)}, f32[64,1024]{1,0:T(8,128)S(1)}, u32[]{:S(2)}, u32[]{:S(2)}) collective-permute-start(f32[64,1024]{1,0:T(8,128)S(1)} %get-tuple-element.25), channel_id=1, source_target_pairs={{0,1},{1,0},{2,3},{3,2},{4,5},{5,4},{6,7},{7,6},{8,9},{9,8},{10,11... | collective-permute-start | bytes 786440 | tf_op jit(solution)/shard_map/ppermute | solution.py:208
  14.4 10.7 %collective-permute-start.2 = (f32[128,1024]{1,0:T(8,128)S(1)}, f32[128,1024]{1,0:T(8,128)S(1)}, u32[]{:S(2)}, u32[]{:S(2)}) collective-permute-start(f32[128,1024]{1,0:T(8,128)S(1)} %get-tuple-element.22), channel_id=1, source_target_pairs={{0,1},{1,0},{2,3},{3,2},{4,5},{5,4},{6,7},{7,6},{8,9},{9,8},{10,11... | collective-permute-start | bytes 1572872 | tf_op jit(solution)/shard_map/ppermute | solution.py:208
  16.2 7.5 %collective-permute-start.5 = (f32[128,512]{1,0:T(8,128)S(1)}, f32[128,512]{1,0:T(8,128)S(1)}, u32[]{:S(2)}, u32[]{:S(2)}) collective-permute-start(f32[128,512]{1,0:T(8,128)S(1)} %shard_map.53.refs_5_), channel_id=1, source_target_pairs={{0,16},{1,9},{2,18},{3,11},{4,20},{5,13},{6,22},{7,15},{8,24},{9,1... | collective-permute-start | bytes 786440 | tf_op jit(solution)/shard_map/ppermute | solution.py:208
  18.7 9.7 %collective-permute-start.8 = (f32[136,512]{1,0:T(8,128)S(1)}, f32[136,512]{1,0:T(8,128)S(1)}, u32[]{:S(2)}, u32[]{:S(2)}) collective-permute-start(f32[136,512]{1,0:T(8,128)S(1)} %shard_map.55), channel_id=1, source_target_pairs={{0,8},{1,17},{2,10},{3,19},{4,12},{5,21},{6,14},{7,23},{8,0},{9,25... | collective-permute-start | bytes 835592 | tf_op jit(solution)/shard_map/ppermute | solution.py:208
  21.1 9.3 %collective-permute-start.6 = (f32[128,512]{1,0:T(8,128)S(1)}, f32[128,512]{1,0:T(8,128)S(1)}, u32[]{:S(2)}, u32[]{:S(2)}) collective-permute-start(f32[128,512]{1,0:T(8,128)S(1)} %shard_map.54.refs_6_), channel_id=1, source_target_pairs={{0,16},{1,9},{2,18},{3,11},{4,20},{5,13},{6,22},{7,15},{8,24},{9,1... | collective-permute-start | bytes 786440 | tf_op jit(solution)/shard_map/ppermute | solution.py:208
  23.7 7.5 %collective-permute-start.9 = (f32[128,512]{1,0:T(8,128)S(1)}, f32[128,512]{1,0:T(8,128)S(1)}, u32[]{:S(2)}, u32[]{:S(2)}) collective-permute-start(f32[128,512]{1,0:T(8,128)S(1)} %shard_map.56), channel_id=1, source_target_pairs={{0,8},{1,17},{2,10},{3,19},{4,12},{5,21},{6,14},{7,23},{8,0},{9,25... | collective-permute-start | bytes 786440 | tf_op jit(solution)/shard_map/ppermute | solution.py:208
  28.4 5.2 %collective-permute-start.10 = (f32[72,512]{1,0:T(8,128)S(1)}, f32[72,512]{1,0:T(8,128)S(1)}, u32[]{:S(2)}, u32[]{:S(2)}) collective-permute-start(f32[72,512]{1,0:T(8,128)S(1)} %shard_map.57), channel_id=1, source_target_pairs={{0,2},{1,3},{2,0},{3,1},{4,6},{5,7},{6,4},{7,5},{8,10},{9,11},{10,... | collective-permute-start | bytes 442376 | tf_op jit(solution)/shard_map/ppermute | solution.py:208
  31.2 6.5 %collective-permute-start.11 = (f32[64,512]{1,0:T(8,128)S(1)}, f32[64,512]{1,0:T(8,128)S(1)}, u32[]{:S(2)}, u32[]{:S(2)}) collective-permute-start(f32[64,512]{1,0:T(8,128)S(1)} %shard_map.58), channel_id=1, source_target_pairs={{0,2},{1,3},{2,0},{3,1},{4,6},{5,7},{6,4},{7,5},{8,10},{9,11},{10,... | collective-permute-start | bytes 393224 | tf_op jit(solution)/shard_map/ppermute | solution.py:208
  33.7 9.3 %collective-permute-start.12 = (f32[40,512]{1,0:T(8,128)S(1)}, f32[40,512]{1,0:T(8,128)S(1)}, u32[]{:S(2)}, u32[]{:S(2)}) collective-permute-start(f32[40,512]{1,0:T(8,128)S(1)} %shard_map.59), channel_id=1, source_target_pairs={{0,4},{1,5},{2,6},{3,7},{4,0},{5,1},{6,2},{7,3},{8,12},{9,13},{10,... | collective-permute-start | bytes 245768 | tf_op jit(solution)/shard_map/ppermute | solution.py:208
  37.7 5.2 %collective-permute-start.13 = (f32[32,512]{1,0:T(8,128)S(1)}, f32[32,512]{1,0:T(8,128)S(1)}, u32[]{:S(2)}, u32[]{:S(2)}) collective-permute-start(f32[32,512]{1,0:T(8,128)S(1)} %shard_map.60), channel_id=1, source_target_pairs={{0,4},{1,5},{2,6},{3,7},{4,0},{5,1},{6,2},{7,3},{8,12},{9,13},{10,... | collective-permute-start | bytes 196616 | tf_op jit(solution)/shard_map/ppermute | solution.py:208
